TPU v7x, 128 devices: a whole 4x4x4 slice. The times are simulated.
128 devices in a mesh: dp: 8 (over z, core), mp: 16 (over y, x).
Axes of the slice: x: 4, y: 4, z: 4, core: 2. Of those that a mesh axis runs over, the one named last changes fastest.
Arguments:
- old_weight: float32 [1536, 43008], P('dp', 'mp'), may hold values from -6 to 6
- old_first: float32 [1536, 43008], P('dp', 'mp'), may hold values from -6 to 6
- old_second: float32 [1536, 43008], P('dp', 'mp'), may hold values from 0.1 to 2
- gradient: float32 [1536, 43008], P('dp', 'mp'), may hold values from -6 to 6
- old_rows: int32 [8, 192], replicated, may hold values from 0 to 1535, as said below
- new_rows: int32 [8, 192], replicated, may hold values from 0 to 1535, as said below
- new_units: int32 [16, 21], replicated, may hold values from 0 to 335, as said below
- step: int32 [1], replicated, may hold values from 1 to 49
Outputs:
- new_weight: float32 [1536, 43008], P('dp', 'mp')
- new_first: float32 [1536, 43008], P('dp', 'mp')
- new_second: float32 [1536, 43008], P('dp', 'mp')
- update: float32 [1536, 43008], P('dp', 'mp')
Inputs may be any that keep to these rules, and one draw needn't show every extreme that they name: old_rows names every slab row once. Of the rows in one old data shard, at most 36 are named by any one new data shard, and in every draw each old data shard has exactly 36 for some new data shard. new_rows names every slab row once; the bound on rows from one old data shard to one new data shard, stated for old_rows, holds. new_units names every column unit once. Of the units u * 21 to u * 21 + 20 of old tensor shard u, at most 2 are named by any one new tensor shard, and in every draw each old tensor shard has exactly 2 for some new tensor shard.
All inputs are finite; a program needn't handle non-finite values.
Results may differ from a plain program's by a relative error of at most 0.00018.
Values sent between devices are 32-bit elements; how exact they have to be, the bound alone decides.
No kernel may reach another device: no remote copies, remote signals or barrier semaphores. Data moves between devices by JAX's collectives and lax.ppermute only.
A program may use at most 128 MiB of HBM per device.

v0:
```python
import jax
import jax.numpy as jnp
from jax import lax
from jax.sharding import PartitionSpec as P

HEAD_DIM = 128


beta_one = 0.9
beta_two = 0.999
epsilon = 1e-08
learn_rate = 0.001
decay_rate = 0.1


def adam_step(weight, first, second, gradient, step):
    step_count = step[0].astype(jnp.float32)
    new_first = beta_one * first + (1.0 - beta_one) * gradient
    new_second = beta_two * second + (1.0 - beta_two) * gradient * gradient
    first_fix = 1.0 - jnp.power(jnp.float32(beta_one), step_count)
    second_fix = 1.0 - jnp.power(jnp.float32(beta_two), step_count)
    update = (
        new_first / first_fix / (jnp.sqrt(new_second / second_fix) + epsilon) + decay_rate * weight
    )
    new_weight = weight - learn_rate * update
    return (new_weight, new_first, new_second, update)


def moving_plan(old_flat, new_flat, shards, per_shard):
    total_rows = shards * per_shard
    new_place = jnp.argsort(new_flat, stable=True)
    old_place = jnp.argsort(old_flat, stable=True)
    target = new_place[old_flat] // per_shard
    onehot = (target[:, None] == jnp.arange(shards, dtype=jnp.int32)[None, :]).astype(jnp.int32)
    onehot = onehot.reshape(shards, per_shard, shards)
    before = jnp.cumsum(onehot, axis=1) - onehot
    slot_rank = jnp.sum(before * onehot, axis=2).reshape(total_rows)
    return (target, slot_rank, old_place)


def send_index(target, slot_rank, owner, shards, per_shard, capacity):
    mine_target = lax.dynamic_slice_in_dim(target, owner * per_shard, per_shard)
    mine_rank = lax.dynamic_slice_in_dim(slot_rank, owner * per_shard, per_shard)
    spots = mine_target * capacity + mine_rank
    slots = jnp.arange(shards * capacity, dtype=jnp.int32)
    match = (slots[:, None] == spots[None, :]).astype(jnp.int32)
    sources = jnp.arange(per_shard, dtype=jnp.int32)[None, :]
    found = jnp.sum(match, axis=1)
    return jnp.sum(match * sources, axis=1) + per_shard * (1 - found)


def receive_index(new_flat, slot_rank, old_place, owner, per_shard, capacity):
    wanted = lax.dynamic_slice_in_dim(new_flat, owner * per_shard, per_shard)
    anchor = old_place[wanted]
    return anchor // per_shard * capacity + slot_rank[anchor]


def room_for(count, shards):
    share = count // shards
    return share + share // 2 + min(count % shards, 1)


def body(old_weight, old_first, old_second, gradient, old_rows, new_rows, new_units, step):
    dp_shards = lax.axis_size("dp")
    mp_shards = lax.axis_size("mp")
    dp_index = lax.axis_index("dp")
    mp_index = lax.axis_index("mp")
    row_count = old_weight.shape[0]
    unit_count = new_units.shape[1]
    unit_width = HEAD_DIM
    row_room = room_for(row_count, dp_shards)
    unit_room = room_for(unit_count, mp_shards)
    old_flat = old_rows.reshape(-1)
    new_flat = new_rows.reshape(-1)
    row_target, row_rank, row_place = moving_plan(old_flat, new_flat, dp_shards, row_count)
    row_send = send_index(row_target, row_rank, dp_index, dp_shards, row_count, row_room)
    row_take = receive_index(new_flat, row_rank, row_place, dp_index, row_count, row_room)
    unit_old = jnp.arange(mp_shards * unit_count, dtype=jnp.int32)
    unit_flat = new_units.reshape(-1)
    unit_target, unit_rank, unit_place = moving_plan(unit_old, unit_flat, mp_shards, unit_count)
    unit_send = send_index(unit_target, unit_rank, mp_index, mp_shards, unit_count, unit_room)
    unit_take = receive_index(unit_flat, unit_rank, unit_place, mp_index, unit_count, unit_room)
    states = (old_weight, old_first, old_second)
    packed = tuple(
        (
            jnp.take(moment, row_send, axis=0, mode="fill", fill_value=0).reshape(
                dp_shards, row_room, unit_count * unit_width
            )
            for moment in states
        )
    )
    arrived = (
        lax.all_to_all(packed[0], "dp", split_axis=0, concat_axis=0, tiled=True),
        lax.all_to_all(packed[1], "dp", split_axis=0, concat_axis=0, tiled=True),
        lax.all_to_all(packed[2], "dp", split_axis=0, concat_axis=0, tiled=True),
    )
    rowed = tuple(
        (
            jnp.take(
                moment.reshape(dp_shards * row_room, unit_count * unit_width), row_take, axis=0
            )
            for moment in arrived
        )
    )
    packed = tuple(
        (
            jnp.take(
                moment.reshape(row_count, unit_count, unit_width),
                unit_send,
                axis=1,
                mode="fill",
                fill_value=0,
            ).reshape(row_count, mp_shards, unit_room, unit_width)
            for moment in rowed
        )
    )
    arrived = (
        lax.all_to_all(packed[0], "mp", split_axis=1, concat_axis=1, tiled=True),
        lax.all_to_all(packed[1], "mp", split_axis=1, concat_axis=1, tiled=True),
        lax.all_to_all(packed[2], "mp", split_axis=1, concat_axis=1, tiled=True),
    )
    placed = tuple(
        (
            jnp.take(
                moment.reshape(row_count, mp_shards * unit_room, unit_width), unit_take, axis=1
            ).reshape(row_count, unit_count * unit_width)
            for moment in arrived
        )
    )
    return adam_step(placed[0], placed[1], placed[2], gradient, step)


def solution(mesh):
    return jax.shard_map(
        body,
        mesh=mesh,
        in_specs=(P("dp", "mp"), P("dp", "mp"), P("dp", "mp"), P("dp", "mp"), P(), P(), P(), P()),
        out_specs=(P("dp", "mp"), P("dp", "mp"), P("dp", "mp"), P("dp", "mp")),
        check_vma=False,
    )
```

profile of v0, /device:TPU:12, one launch (start us, length us, event | category | flops | bytes accessed | tf_op | source)
XLA Modules:
  0.0 368.2 jit_solution(3002056445167120183)
XLA Ops:
  2.4 5.0 %sort.62 = (s32[1536]{0:T(1024)}, s32[1536]{0:T(1024)S(1)}) sort(s32[1536]{0:T(1024)S(1)} %reshape.235, s32[1536]{0:T(1024)S(1)} %iota.51), dimensions={0}, to_apply=%region_0.0 | sort | flops 16896 | bytes 24576 | tf_op jit(solution)/shard_map/jit(argsort)/sort | solution.py:31
  7.4 8.4 %gather_fusion = s32[1536]{0:T(1024)S(1)} fusion(s32[1536]{0:T(1024)S(1)} %get-tuple-element.12, s32[2048]{0:T(1024)S(1)} %pad_clamp_fusion), kind=kCustom, calls=%fused_computation.12 | custom fusion | bytes 18432 | tf_op jit(solution)/shard_map/gather | solution.py:33
  16.1 4.5 %reduce-window.6 = s32[8,8,2,128]{3,1,2,0:T(8,128)S(1)} reduce-window(s32[8,8,2,128]{3,1,2,0:T(8,128)S(1)} %convert_bitcast_fusion, s32[]{:T(128)} %constant.63.clone.1), window={size=1x1x1x128 pad=0_0x0_0x0_0x127_0}, to_apply=%region_1.2 | reduce-window | flops 2080768 | bytes 131076 | tf_op jit(solution)/shard_map/reduce-window
  21.4 3.7 gather_fusion.14
  25.1 7.5 %gather_fusion.10 = f32[288,2688]{1,0:T(8,128)} fusion(f32[192,2688]{1,0:T(8,128)} %param.17, s32[1024]{0:T(1024)S(1)} %pad_clamp_fusion.4), kind=kCustom, calls=%fused_computation.4.clone | custom fusion | bytes 6194304 | tf_op jit(solution)/shard_map/jit(_take)/gather | solution.py:86
  32.6 3.6 gather_fusion.6
  36.3 7.6 %broadcast_select_fusion.4 = (f32[288,2688]{1,0:T(8,128)}, f32[288,2688]{1,0:T(8,128)}, f32[288,2688]{1,0:T(8,128)}) fusion(f32[288,2688]{1,0:T(8,128)} %gather_fusion.10, pred[288]{0:T(512)(128)(4,1)S(1)} %get-tuple-element.32, f32[288,2688]{1,0:T(8,128)} %gather_fusion.14, f32[288,2688]{1,0:T(8,128)} %gather_fusion.6), kind=kLoop, calls=%fused_computation.39 | loop fusion | flops 2322432 | bytes 18579744 | tf_op jit(solution)/shard_map/jit(_take)/select_n | solution.py:86
  47.2 5.3 %all-to-all-start.2 = ((f32[8,36,2688]{2,1,0:T(8,128)}), f32[8,36,2688]{2,1,0:T(8,128)}, u32[]{:S(2)}, u32[]{:S(2)}) async-start(f32[8,36,2688]{2,1,0:T(8,128)} %reshape.249), calls=%async_computation.2 | async-start | bytes 6881280 | tf_op jit(solution)/shard_map/all_to_all | solution.py:94
  52.6 3.4 reshape.254
  55.9 38.4 %all-to-all-done.2 = f32[8,36,2688]{2,1,0:T(8,128)} async-done(((f32[8,36,2688]{2,1,0:T(8,128)}), f32[8,36,2688]{2,1,0:T(8,128)}, u32[]{:S(2)}, u32[]{:S(2)}) %all-to-all-start.2) | async-done | bytes 3096608 | tf_op jit(solution)/shard_map/all_to_all | solution.py:94
  94.3 4.5 %all-to-all-start.4 = ((f32[8,36,2688]{2,1,0:T(8,128)}), f32[8,36,2688]{2,1,0:T(8,128)}, u32[]{:S(2)}, u32[]{:S(2)}) async-start(f32[8,36,2688]{2,1,0:T(8,128)} %reshape.254), calls=%async_computation.4 | async-start | bytes 6881280 | tf_op jit(solution)/shard_map/all_to_all | solution.py:95
  102.1 38.3 %all-to-all-done.4 = f32[8,36,2688]{2,1,0:T(8,128)} async-done(((f32[8,36,2688]{2,1,0:T(8,128)}), f32[8,36,2688]{2,1,0:T(8,128)}, u32[]{:S(2)}, u32[]{:S(2)}) %all-to-all-start.4) | async-done | bytes 3096608 | tf_op jit(solution)/shard_map/all_to_all | solution.py:95
  140.4 4.7 %all-to-all-start = ((f32[8,36,2688]{2,1,0:T(8,128)}), f32[8,36,2688]{2,1,0:T(8,128)}, u32[]{:S(2)}, u32[]{:S(2)}) async-start(f32[8,36,2688]{2,1,0:T(8,128)} %reshape.240), calls=%async_computation | async-start | bytes 6881280 | tf_op jit(solution)/shard_map/all_to_all | solution.py:93
  145.2 3.8 %sort.64 = (s32[336]{0:T(512)}, s32[336]{0:T(512)S(1)}) sort(s32[336]{0:T(512)S(1)} %reshape.244, s32[336]{0:T(512)S(1)} %iota.53), dimensions={0}, to_apply=%region_7.10 | sort | flops 3024 | bytes 5376 | tf_op jit(solution)/shard_map/jit(argsort)/sort | solution.py:31
  152.9 5.0 %sort.63 = (s32[1536]{0:T(1024)}, s32[1536]{0:T(1024)S(1)}) sort(s32[1536]{0:T(1024)S(1)} %reshape.242, s32[1536]{0:T(1024)S(1)} %iota.52), dimensions={0}, to_apply=%region_6.8 | sort | flops 16896 | bytes 24576 | tf_op jit(solution)/shard_map/jit(argsort)/sort | solution.py:32
  164.4 5.4 %gather_fusion.11 = f32[192,2688]{1,0:T(8,128)} fusion(f32[288,2688]{1,0:T(8,128)} %reshape.250, s32[1024]{0:T(1024)S(1)} %pad_clamp_fusion.3), kind=kCustom, calls=%fused_computation.6.clone | custom fusion | bytes 4129536 | tf_op jit(solution)/shard_map/jit(_take)/gather | solution.py:99
  173.0 5.4 %gather_fusion.15 = f32[192,2688]{1,0:T(8,128)} fusion(f32[288,2688]{1,0:T(8,128)} %reshape.255, s32[1024]{0:T(1024)S(1)} %pad_clamp_fusion.3), kind=kCustom, calls=%fused_computation.7.clone | custom fusion | bytes 4129536 | tf_op jit(solution)/shard_map/jit(_take)/gather | solution.py:99
  178.4 8.1 %all-to-all-done = f32[8,36,2688]{2,1,0:T(8,128)} async-done(((f32[8,36,2688]{2,1,0:T(8,128)}), f32[8,36,2688]{2,1,0:T(8,128)}, u32[]{:S(2)}, u32[]{:S(2)}) %all-to-all-start) | async-done | bytes 3096608 | tf_op jit(solution)/shard_map/all_to_all | solution.py:93
  189.7 5.4 %gather_fusion.7 = f32[192,2688]{1,0:T(8,128)} fusion(f32[288,2688]{1,0:T(8,128)} %reshape.241, s32[1024]{0:T(1024)S(1)} %pad_clamp_fusion.3), kind=kCustom, calls=%fused_computation.1.clone | custom fusion | bytes 4129536 | tf_op jit(solution)/shard_map/jit(_take)/gather | solution.py:99
  195.1 4.6 %select_bitcast_fusion.1 = (f32[24,21,8,128]{3,2,1,0:T(8,128)S(1)}, f32[24,21,8,128]{3,2,1,0:T(8,128)S(1)}, f32[24,21,8,128]{3,2,1,0:T(8,128)}) fusion(f32[192,2688]{1,0:T(8,128)} %gather_fusion.11, pred[192]{0:T(512)(128)(4,1)S(1)} %get-tuple-element.30, f32[192,2688]{1,0:T(8,128)} %gather_fusion.15, f32[192,2688]{1,0:T(8,128)} %gather_fusion.7), kind=kLoop, calls=%fused_computation.32 | loop fusion | flops 1548288 | bytes 12386496
  202.8 4.0 %gather_fusion.12 = f32[32,192,128]{2,1,0:T(8,128)} fusion(f32[192,21,128]{2,0,1:T(8,128)} %bitcast.72, s32[1024]{0:T(1024)S(1)} %pad_clamp_fusion.2), kind=kCustom, calls=%fused_computation.8.clone | custom fusion | bytes 6291584 | tf_op jit(solution)/shard_map/jit(_take)/gather | solution.py:107
  206.7 4.0 %gather_fusion.16 = f32[32,192,128]{2,1,0:T(8,128)} fusion(f32[192,21,128]{2,0,1:T(8,128)} %bitcast.73, s32[1024]{0:T(1024)S(1)} %pad_clamp_fusion.2), kind=kCustom, calls=%fused_computation.9.clone | custom fusion | bytes 6291584 | tf_op jit(solution)/shard_map/jit(_take)/gather | solution.py:107
  213.8 4.0 %gather_fusion.8 = f32[32,192,128]{2,1,0:T(8,128)} fusion(f32[192,21,128]{2,0,1:T(8,128)} %bitcast.74, s32[1024]{0:T(1024)S(1)} %pad_clamp_fusion.2), kind=kCustom, calls=%fused_computation.2.clone | custom fusion | bytes 6291584 | tf_op jit(solution)/shard_map/jit(_take)/gather | solution.py:107
  217.8 6.7 %broadcast_select_fusion.1 = (f32[32,192,128]{2,1,0:T(8,128)S(1)}, f32[32,192,128]{2,1,0:T(8,128)S(1)}, f32[32,192,128]{2,1,0:T(8,128)}) fusion(f32[32,192,128]{2,1,0:T(8,128)} %gather_fusion.12, pred[32]{0:T(512)(128)(4,1)S(1)} %get-tuple-element.26, f32[32,192,128]{2,1,0:T(8,128)} %gather_fusion.16, f32[32,192,128]{2,1,0:T(8,128)} %gather_fusion.8), kind=kLoop, calls=%fused_computation.36 | loop fusion | flops 2359296 | bytes 18874400 | tf_op jit(solution)/shard_map/jit(_take)/select_n | solution.py:107
  224.5 43.2 %all_to_all.30 = f32[192,16,2,128]{3,0,2,1:T(8,128)} all-to-all(f32[192,16,2,128]{3,0,2,1:T(8,128)S(1)} %bitcast.77), channel_id=1, replica_groups=mesh['dp'=8,'mp'=16] {'mp'}, dimensions={1} | all-to-all | bytes 6291456 | tf_op jit(solution)/shard_map/all_to_all | solution.py:120
  267.8 42.4 %all_to_all.31 = f32[192,16,2,128]{3,0,2,1:T(8,128)} all-to-all(f32[192,16,2,128]{3,0,2,1:T(8,128)S(1)} %bitcast.76), channel_id=1, replica_groups=mesh['dp'=8,'mp'=16] {'mp'}, dimensions={1} | all-to-all | bytes 6291456 | tf_op jit(solution)/shard_map/all_to_all | solution.py:119
  310.2 8.3 %all-to-all-start.1 = ((f32[192,16,2,128]{3,0,2,1:T(8,128)}), f32[192,16,2,128]{3,0,2,1:T(8,128)}, u32[]{:S(2)}, u32[]{:S(2)}) async-start(f32[192,16,2,128]{3,0,2,1:T(8,128)} %bitcast.75), calls=%async_computation.1 | async-start | bytes 6291456 | tf_op jit(solution)/shard_map/all_to_all | solution.py:118
  319.2 3.7 sort.65
  326.9 3.9 %gather_fusion.13 = f32[21,192,128]{2,1,0:T(8,128)} fusion(f32[192,32,128]{2,0,1:T(8,128)} %bitcast.79, s32[1024]{0:T(1024)S(1)} %pad_clamp_fusion.1), kind=kCustom, calls=%fused_computation.10.clone | custom fusion | bytes 4128852 | tf_op jit(solution)/shard_map/jit(_take)/gather | solution.py:124
  330.8 26.5 %all-to-all-done.1 = f32[192,16,2,128]{3,0,2,1:T(8,128)} async-done(((f32[192,16,2,128]{3,0,2,1:T(8,128)}), f32[192,16,2,128]{3,0,2,1:T(8,128)}, u32[]{:S(2)}, u32[]{:S(2)}) %all-to-all-start.1) | async-done | bytes 3145760 | tf_op jit(solution)/shard_map/all_to_all | solution.py:118
  357.2 3.9 %gather_fusion.9 = f32[21,192,128]{2,1,0:T(8,128)} fusion(f32[192,32,128]{2,0,1:T(8,128)} %bitcast.10, s32[1024]{0:T(1024)S(1)} %pad_clamp_fusion.1), kind=kCustom, calls=%fused_computation.3.clone | custom fusion | bytes 4128852 | tf_op jit(solution)/shard_map/jit(_take)/gather | solution.py:124
  363.9 4.2 %bitcast_subtract_fusion = (f32[192,2688]{1,0:T(8,128)}, f32[192,2688]{1,0:T(8,128)}, f32[192,2688]{1,0:T(8,128)}, f32[192,2688]{1,0:T(8,128)}) fusion(f32[]{:T(128)} %bitcast.21, f32[]{:T(128)} %bitcast.16, f32[192,2688]{1,0:T(8,128)S(1)} %copy-done.4, f32[21,24,8,128]{3,2,1,0:T(8,128)S(1)} %get-tuple-element.36, ...), kind=kLoop, calls=%fused_computation.21 | loop fusion | flops 7225344 | bytes 16515101 | tf_op jit(solution)/shard_map/sub | solution.py:25
  (82 shorter events, 39.4 us)
Async XLA Ops:
  0.6 20.8 %copy-start = (f32[192,2688]{1,0:T(8,128)S(1)}, f32[192,2688]{1,0:T(8,128)}, u32[]{:S(2)}) copy-start(f32[192,2688]{1,0:T(8,128)} %param.18) | copy-start | bytes 6193156
  25.1 7.6 %copy-start.2 = (f32[192,2688]{1,0:T(8,128)S(1)}, f32[192,2688]{1,0:T(8,128)}, u32[]{:S(2)}) copy-start(f32[192,2688]{1,0:T(8,128)} %param.16) | copy-start | bytes 6193156
  47.2 47.0 %all-to-all-start.2 = ((f32[8,36,2688]{2,1,0:T(8,128)}), f32[8,36,2688]{2,1,0:T(8,128)}, u32[]{:S(2)}, u32[]{:S(2)}) async-start(f32[8,36,2688]{2,1,0:T(8,128)} %reshape.249), calls=%async_computation.2 | async-start | bytes 6881280 | tf_op jit(solution)/shard_map/all_to_all | solution.py:94
  94.3 46.1 %all-to-all-start.4 = ((f32[8,36,2688]{2,1,0:T(8,128)}), f32[8,36,2688]{2,1,0:T(8,128)}, u32[]{:S(2)}, u32[]{:S(2)}) async-start(f32[8,36,2688]{2,1,0:T(8,128)} %reshape.254), calls=%async_computation.4 | async-start | bytes 6881280 | tf_op jit(solution)/shard_map/all_to_all | solution.py:95
  102.1 42.9 %copy-start.5 = (s32[8,192]{1,0:T(8,128)S(1)}, s32[8,192]{1,0:T(8,128)}, u32[]{:S(2)}) copy-start(s32[8,192]{1,0:T(8,128)} %param.20) | copy-start | bytes 18436
  102.1 43.0 %copy-start.6 = (s32[16,21]{1,0:T(8,128)S(1)}, s32[16,21]{1,0:T(8,128)}, u32[]{:S(2)}) copy-start(s32[16,21]{1,0:T(8,128)} %param.22) | copy-start | bytes 4036
  140.4 46.1 %all-to-all-start = ((f32[8,36,2688]{2,1,0:T(8,128)}), f32[8,36,2688]{2,1,0:T(8,128)}, u32[]{:S(2)}, u32[]{:S(2)}) async-start(f32[8,36,2688]{2,1,0:T(8,128)} %reshape.240), calls=%async_computation | async-start | bytes 6881280 | tf_op jit(solution)/shard_map/all_to_all | solution.py:93
  310.2 47.1 %all-to-all-start.1 = ((f32[192,16,2,128]{3,0,2,1:T(8,128)}), f32[192,16,2,128]{3,0,2,1:T(8,128)}, u32[]{:S(2)}, u32[]{:S(2)}) async-start(f32[192,16,2,128]{3,0,2,1:T(8,128)} %bitcast.75), calls=%async_computation.1 | async-start | bytes 6291456 | tf_op jit(solution)/shard_map/all_to_all | solution.py:118
  361.1 2.4 copy-start.3
  361.1 2.8 copy-start.4
  363.9 4.2 %copy-start.1 = (f32[192,2688]{1,0:T(8,128)S(1)}, f32[192,2688]{1,0:T(8,128)}, u32[]{:S(2)}) copy-start(f32[192,2688]{1,0:T(8,128)} %param.18) | copy-start | bytes 6193156
where the time goes:
time: 372 us; the launch traced here: 368 us
  waiting for transfers between devices  111 us (30%)
  local copies, waits for them, and re-layouts  98 us (26%)
  blocking collectives  85.6 us (23%)
  other arithmetic  49 us (13%)
  starting transfers between devices  22.7 us (6%)
    all_to_all x1, blocking collectives, body(): lax.all_to_all(packed[2], 'mp', split_axis=1, concat_axis=1, tiled=True)  43.2 us
    all_to_all x1, blocking collectives, body(): lax.all_to_all(packed[1], 'mp', split_axis=1, concat_axis=1, tiled=True)  42.4 us
    all_to_all x1, waiting for transfers between devices, body(): lax.all_to_all(packed[1], 'dp', split_axis=0, concat_axis=0, tiled=True)  38.4 us
    all_to_all x1, waiting for transfers between devices, body(): lax.all_to_all(packed[2], 'dp', split_axis=0, concat_axis=0, tiled=True)  38.3 us
    all_to_all x1, waiting for transfers between devices, body(): lax.all_to_all(packed[0], 'mp', split_axis=1, concat_axis=1, tiled=True)  26.5 us
    gather x3, local copies, waits for them, and re-layouts, body(): jnp.take(moment.reshape(dp_shards * row_room, unit_count * unit_width), r...  16.1 us
    gather x3, local copies, waits for them, and re-layouts, body(): jnp.take(moment, row_send, axis=0, mode='fill', fill_value=0)  14.8 us
    gather x3, local copies, waits for them, and re-layouts, body(): jnp.take(moment.reshape(row_count, unit_count, unit_width), unit_send, ax...  12 us
  transfers between devices with their start and end apart: 4, of which 4 were waited for; matrix products, arithmetic and copies ran while one was open for 14% of the time, Pallas kernels for 0%

commit v1 on v0

v1 whole, which is shorter than its diff:
```python
import functools

import jax
import jax.numpy as jnp
from jax import lax
from jax.experimental import pallas as pl
from jax.experimental.pallas import tpu as pltpu
from jax.sharding import PartitionSpec as P

UNIT = 128
ROWS = 192
UNITS = 21
COLS = UNIT * UNITS
DP = 8
MP = 16
ROOM = 40
PAIR = 2
VMEM_LIMIT = 40 * 1024 * 1024

beta_one = 0.9
beta_two = 0.999
epsilon = 1e-08
learn_rate = 0.001
decay_rate = 0.1

MOVES = [(dz, dc) for dz in range(4) for dc in range(2)]
HBM = pl.BlockSpec(memory_space=pl.ANY)
VMEM = pl.BlockSpec(memory_space=pltpu.VMEM)
SMEM = pl.BlockSpec(memory_space=pltpu.SMEM)


def cost(nbytes, flops=0):
    return pl.CostEstimate(flops=flops, bytes_accessed=nbytes, transcendentals=0)


def params():
    return pltpu.CompilerParams(vmem_limit_bytes=VMEM_LIMIT)


def row_plan(old_rows, new_rows):
    d = lax.axis_index("dp")
    z, c = d // 2, d % 2
    shard = jnp.arange(DP, dtype=jnp.int32)
    old_mine = lax.dynamic_index_in_dim(old_rows, d, 0, keepdims=False)
    new_mine = lax.dynamic_index_in_dim(new_rows, d, 0, keepdims=False)
    slots = jnp.arange(DP * ROOM, dtype=jnp.int32)
    earlier = jnp.arange(ROWS)[None, :] < jnp.arange(ROWS)[:, None]

    hit = jnp.any(old_mine[:, None, None] == new_rows[None, :, :], axis=2)
    move_to = ((shard // 2 - z) % 4) * 2 + (shard % 2 + c) % 2
    target = jnp.sum(jnp.where(hit, move_to[None, :], 0), axis=1)
    rank = jnp.sum(((target[:, None] == target[None, :]) & earlier).astype(jnp.int32), axis=1)
    pack = (slots[:, None] == (target * ROOM + rank)[None, :]).astype(jnp.bfloat16)

    equal = new_mine[:, None, None] == old_rows[None, :, :]
    mine = jnp.any(equal, axis=0)
    before = jnp.sum((mine[:, None, :] & earlier[None, :, :]).astype(jnp.int32), axis=2)
    move_from = ((z - shard // 2) % 4) * 2 + (shard % 2 + c) % 2
    value = move_from[:, None] * ROOM + before
    source = jnp.sum(jnp.where(equal, value[None], 0), axis=(1, 2))
    unpack = (source[:, None] == slots[None, :]).astype(jnp.bfloat16)
    return pack, unpack


def unit_plan(new_units):
    m = lax.axis_index("mp")
    own = jnp.arange(UNITS, dtype=jnp.int32)
    slots = jnp.arange(MP * PAIR, dtype=jnp.int32)

    hit = jnp.any((m * UNITS + own)[:, None, None] == new_units[None, :, :], axis=2)
    target = jnp.sum(jnp.where(hit, jnp.arange(MP, dtype=jnp.int32)[None, :], 0), axis=1)
    earlier = own[None, :] < own[:, None]
    rank = jnp.sum(((target[:, None] == target[None, :]) & earlier).astype(jnp.int32), axis=1)
    here = (target * PAIR + rank)[None, :] == slots[:, None]
    send = jnp.sum(jnp.where(here, own[None, :], 0), axis=1)

    wanted = lax.dynamic_index_in_dim(new_units, m, 0, keepdims=False)
    origin = wanted // UNITS
    lower = (origin[:, None] == origin[None, :]) & (wanted[None, :] < wanted[:, None])
    take = origin * PAIR + jnp.sum(lower.astype(jnp.int32), axis=1)
    return send, take


def select_rows(onehot, values):
    high = values.astype(jnp.bfloat16)
    rest = values - high.astype(jnp.float32)
    middle = rest.astype(jnp.bfloat16)
    low = (rest - middle.astype(jnp.float32)).astype(jnp.bfloat16)
    dot = functools.partial(jnp.dot, preferred_element_type=jnp.float32)
    return (dot(onehot, high) + dot(onehot, middle)) + dot(onehot, low)


def unit_pack_kernel(send, x, out, sems):
    copies = []
    for s in range(MP * PAIR):
        columns = pl.ds(pl.multiple_of(send[s] * UNIT, UNIT), UNIT)
        copies.append(pltpu.make_async_copy(x.at[:, columns], out.at[s], sems.at[s]))
    for copy in copies:
        copy.start()
    for copy in copies:
        copy.wait()


def unit_pack(x, send):
    out = pl.pallas_call(
        unit_pack_kernel,
        out_shape=jax.ShapeDtypeStruct((MP * PAIR, ROWS, UNIT), jnp.float32),
        in_specs=[SMEM, HBM],
        out_specs=HBM,
        scratch_shapes=[pltpu.SemaphoreType.DMA((MP * PAIR,))],
        compiler_params=params(),
        cost_estimate=cost(6 * 2**20),
        name="unit_pack",
    )(send, x)
    return out.reshape(MP, PAIR, ROWS, UNIT)


WIDE = 3 * UNIT


def row_pack_kernel(onehot, x, *outs):
    picked = select_rows(onehot[...], x[...])
    for i, out in enumerate(outs):
        out[...] = picked[i * ROOM : (i + 1) * ROOM]


MESSAGES = [jax.ShapeDtypeStruct((ROOM, COLS), jnp.float32)] * DP


def row_pack(x, onehot):
    return pl.pallas_call(
        row_pack_kernel,
        out_shape=MESSAGES,
        grid=(COLS // WIDE,),
        in_specs=[
            pl.BlockSpec((DP * ROOM, ROWS), lambda i: (0, 0)),
            pl.BlockSpec((ROWS, WIDE), lambda i: (0, i)),
        ],
        out_specs=[pl.BlockSpec((ROOM, WIDE), lambda i: (0, i))] * DP,
        compiler_params=params(),
        cost_estimate=cost(6 * 2**20, 3 * 2 * 320 * 192 * COLS),
        name="row_pack",
    )(onehot, x)


def unit_row_pack_kernel(take, onehot, recv, *rest):
    outs, wide, sems = rest[:DP], rest[DP], rest[DP + 1]
    i = pl.program_id(0)
    width = WIDE // UNIT

    def copy_of(j):
        columns = pl.ds(j * UNIT, UNIT)
        return pltpu.make_async_copy(recv.at[take[j]], wide.at[:, columns], sems.at[j])

    @pl.when(i == 0)
    def _():
        for j in range(UNITS):
            copy_of(j).start()

    for step in range(COLS // WIDE):

        @pl.when(i == step)
        def _(step=step):
            for j in range(step * width, (step + 1) * width):
                copy_of(j).wait()
            picked = select_rows(onehot[...], wide[:, step * WIDE : (step + 1) * WIDE])
            for k, out in enumerate(outs):
                out[...] = picked[k * ROOM : (k + 1) * ROOM]


def unit_row_pack(recv, take, onehot):
    return pl.pallas_call(
        unit_row_pack_kernel,
        out_shape=MESSAGES,
        grid=(COLS // WIDE,),
        in_specs=[SMEM, pl.BlockSpec((DP * ROOM, ROWS), lambda i: (0, 0)), HBM],
        out_specs=[pl.BlockSpec((ROOM, WIDE), lambda i: (0, i))] * DP,
        scratch_shapes=[
            pltpu.VMEM((ROWS, COLS), jnp.float32),
            pltpu.SemaphoreType.DMA((UNITS,)),
        ],
        compiler_params=params(),
        cost_estimate=cost(6 * 2**20, 3 * 2 * 320 * 192 * COLS),
        name="unit_row_pack",
    )(take, onehot, recv.reshape(MP * PAIR, ROWS, UNIT))


def joined(parts):
    return jnp.concatenate([p[...] for p in parts], axis=0)


def row_unit_pack_kernel(send, onehot, *rest):
    parts, out, held, sems = rest[:DP], rest[DP], rest[DP + 1], rest[DP + 2]
    i = pl.program_id(0)
    picked = select_rows(onehot[...], joined(parts))
    width = WIDE // UNIT
    for k in range(width):
        held[i * width + k] = picked[:, k * UNIT : (k + 1) * UNIT]

    @pl.when(i == COLS // WIDE - 1)
    def _():
        copies = []
        for s in range(MP * PAIR):
            copies.append(pltpu.make_async_copy(held.at[send[s]], out.at[s], sems.at[s]))
        for copy in copies:
            copy.start()
        for copy in copies:
            copy.wait()


def row_unit_pack(parts, send, onehot):
    out = pl.pallas_call(
        row_unit_pack_kernel,
        out_shape=jax.ShapeDtypeStruct((MP * PAIR, ROWS, UNIT), jnp.float32),
        grid=(COLS // WIDE,),
        in_specs=[SMEM, pl.BlockSpec((ROWS, DP * ROOM), lambda i: (0, 0))]
        + [pl.BlockSpec((ROOM, WIDE), lambda i: (0, i))] * DP,
        out_specs=HBM,
        scratch_shapes=[
            pltpu.VMEM((UNITS, ROWS, UNIT), jnp.float32),
            pltpu.SemaphoreType.DMA((MP * PAIR,)),
        ],
        compiler_params=params(),
        cost_estimate=cost(7 * 2**20, 3 * 2 * 320 * 192 * COLS),
        name="row_unit_pack",
    )(send, onehot, *parts)
    return out.reshape(MP, PAIR, ROWS, UNIT)


def moment_kernel(is_first, onehot, gradient, *rest):
    parts, out = rest[:DP], rest[DP]
    picked = select_rows(onehot[...], joined(parts))
    g = gradient[...]
    if is_first:
        out[...] = beta_one * picked + (1.0 - beta_one) * g
    else:
        out[...] = beta_two * picked + (1.0 - beta_two) * g * g


def moment(parts, onehot, gradient, is_first):
    block = pl.BlockSpec((ROWS, WIDE), lambda i: (0, i))
    return pl.pallas_call(
        functools.partial(moment_kernel, is_first),
        out_shape=jax.ShapeDtypeStruct((ROWS, COLS), jnp.float32),
        grid=(COLS // WIDE,),
        in_specs=[pl.BlockSpec((ROWS, DP * ROOM), lambda i: (0, 0)), block]
        + [pl.BlockSpec((ROOM, WIDE), lambda i: (0, i))] * DP,
        out_specs=block,
        compiler_params=params(),
        cost_estimate=cost(7 * 2**20, 3 * 2 * 320 * 192 * COLS),
        name="new_first" if is_first else "new_second",
    )(onehot, gradient, *parts)


def update_kernel(take, fixes, recv, first, second, new_weight, update, wide, sems):
    i = pl.program_id(0)
    width = WIDE // UNIT

    def copy_of(j):
        columns = pl.ds(j * UNIT, UNIT)
        return pltpu.make_async_copy(recv.at[take[j]], wide.at[:, columns], sems.at[j])

    @pl.when(i == 0)
    def _():
        for j in range(UNITS):
            copy_of(j).start()

    for step in range(COLS // WIDE):

        @pl.when(i == step)
        def _(step=step):
            for j in range(step * width, (step + 1) * width):
                copy_of(j).wait()
            weight = wide[:, step * WIDE : (step + 1) * WIDE]
            root = jnp.sqrt(second[...] / fixes[1]) + epsilon
            change = first[...] / fixes[0] / root + decay_rate * weight
            update[...] = change
            new_weight[...] = weight - learn_rate * change


def weight_update(recv, take, fixes, first, second):
    block = pl.BlockSpec((ROWS, WIDE), lambda i: (0, i))
    return pl.pallas_call(
        update_kernel,
        out_shape=[jax.ShapeDtypeStruct((ROWS, COLS), jnp.float32)] * 2,
        grid=(COLS // WIDE,),
        in_specs=[SMEM, SMEM, HBM, block, block],
        out_specs=[block, block],
        scratch_shapes=[
            pltpu.VMEM((ROWS, COLS), jnp.float32),
            pltpu.SemaphoreType.DMA((UNITS,)),
        ],
        compiler_params=params(),
        cost_estimate=cost(10 * 2**20),
        name="weight_update",
    )(take, fixes, recv.reshape(MP * PAIR, ROWS, UNIT), first, second)


def swap_rows(messages):
    arrived = []
    for message, (dz, dc) in zip(messages, MOVES):
        if dz == 0 and dc == 0:
            arrived.append(message)
            continue
        pairs = [(z * 2 + c, (z + dz) % 4 * 2 + (c + dc) % 2) for z in range(4) for c in range(2)]
        arrived.append(lax.ppermute(message, "dp", pairs))
    return arrived


def swap_units(packed):
    return lax.all_to_all(packed, "mp", split_axis=0, concat_axis=0, tiled=True)


def body(old_weight, old_first, old_second, gradient, old_rows, new_rows, new_units, step):
    send, take = unit_plan(new_units)
    pack, unpack = row_plan(old_rows, new_rows)
    count = step[0].astype(jnp.float32)
    fixes = jnp.stack(
        [
            1.0 - jnp.power(jnp.float32(beta_one), count),
            1.0 - jnp.power(jnp.float32(beta_two), count),
        ]
    )

    first_units = swap_units(unit_pack(old_first, send))
    weight_rows = swap_rows(row_pack(old_weight, pack))
    second_units = swap_units(unit_pack(old_second, send))
    first_rows = swap_rows(unit_row_pack(first_units, take, pack))
    weight_units = swap_units(row_unit_pack(weight_rows, send, unpack))
    second_rows = swap_rows(unit_row_pack(second_units, take, pack))

    new_first = moment(first_rows, unpack, gradient, True)
    new_second = moment(second_rows, unpack, gradient, False)
    new_weight, update = weight_update(weight_units, take, fixes, new_first, new_second)
    return new_weight, new_first, new_second, update


def solution(mesh):
    return jax.shard_map(
        body,
        mesh=mesh,
        in_specs=(P("dp", "mp"), P("dp", "mp"), P("dp", "mp"), P("dp", "mp"), P(), P(), P(), P()),
        out_specs=(P("dp", "mp"), P("dp", "mp"), P("dp", "mp"), P("dp", "mp")),
        check_vma=False,
    )
```

time: 372 us -> 242 us (0.65)
  blocking collectives: 85.6 us -> 0 us
  local copies, waits for them, and re-layouts: 98 us -> 13.2 us
  Pallas kernels: 0 us -> 39.2 us
  other arithmetic: 49 us -> 12 us
  starting transfers between devices: 22.7 us -> 49.1 us
  waiting for transfers between devices: 111 us -> 124 us
    all_to_all x2 -> x0, blocking collectives: 85.6 us -> none  [the longest x1 43.2 us: body(): lax.all_to_all(packed[2], 'mp', split_axis=1, concat_axis=1, tiled=True)]
    ppermute x0 -> x21, waiting for transfers between devices: none -> 85.6 us  [swap_rows(): arrived.append(lax.ppermute(message, 'dp', pairs))]
    all_to_all x4 -> x3, waiting for transfers between devices: 111 us -> 38.7 us  [swap_units(): return lax.all_to_all(packed, 'mp', split_axis=0, concat_axis=0, tiled=True)]
    gather x18 -> x0, local copies, waits for them, and re-layouts: 68.7 us -> none  [the longest x3 16.1 us: body(): jnp.take(moment.reshape(dp_shards * row_room, unit_count * unit_width), r...]
    pallas_call x0 -> x9, Pallas kernels: none -> 39.2 us  [the longest x2 9.88 us: moment(): pl.pallas_call(functools.partial(moment_kernel, is_first), out_shape=jax....]
    reshape x15 -> x0, local copies, waits for them, and re-layouts: 28 us -> none  [the longest x3 10 us: body(): jnp.take(moment, row_send, axis=0, mode='fill', fill_value=0)]
    ppermute x0 -> x21, starting transfers between devices: none -> 25.3 us  [swap_rows(): arrived.append(lax.ppermute(message, 'dp', pairs))]
    sort x4 -> x0, other arithmetic: 17.5 us -> none  [the longest x2 8.81 us: moving_plan(): new_place = jnp.argsort(new_flat, stable=True)]
  transfers between devices with their start and end apart: 4 -> 24, of which waited for: 4 -> 15; matrix products, arithmetic and copies ran while one was open for 14% -> 4% of each run, Pallas kernels for 0% -> 13%
where the time goes in v1:
time: 242 us; the launch traced here: 240 us
  waiting for transfers between devices  124 us (51%)
  starting transfers between devices  49.1 us (20%)
  Pallas kernels  39.2 us (16%)
  local copies, waits for them, and re-layouts  13.2 us (5%)
  other arithmetic  12 us (5%)
    ppermute x21, waiting for transfers between devices, swap_rows(): arrived.append(lax.ppermute(message, 'dp', pairs))  85.6 us
    all_to_all x3, waiting for transfers between devices, swap_units(): return lax.all_to_all(packed, 'mp', split_axis=0, concat_axis=0, tiled=True)  38.7 us
    ppermute x21, starting transfers between devices, swap_rows(): arrived.append(lax.ppermute(message, 'dp', pairs))  25.3 us
    all_to_all x3, starting transfers between devices, swap_units(): return lax.all_to_all(packed, 'mp', split_axis=0, concat_axis=0, tiled=True)  23.8 us
    unnamed x24, local copies, waits for them, and re-layouts  13.2 us
    pallas_call x2, Pallas kernels, moment(): pl.pallas_call(functools.partial(moment_kernel, is_first), out_shape=jax....  9.88 us
    pallas_call x2, Pallas kernels, unit_row_pack(): pl.pallas_call(unit_row_pack_kernel, out_shape=MESSAGES, grid=(COLS // WI...  9.52 us
    pallas_call x1, Pallas kernels, row_unit_pack(): pl.pallas_call(row_unit_pack_kernel, out_shape=jax.ShapeDtypeStruct((MP *...  6.09 us
  transfers between devices with their start and end apart: 24, of which 15 were waited for; matrix products, arithmetic and copies ran while one was open for 4% of the time, Pallas kernels for 13%

profile of v1, /device:TPU:12, one launch (start us, length us, event | category | flops | bytes accessed | tf_op | source)
XLA Modules:
  0.0 239.7 jit_solution(12213779144284667212)
XLA Ops:
  3.9 2.5 %unit_pack.3 = f32[32,192,128]{2,1,0:T(8,128)} custom-call(s32[32]{0:T(128)S(1)} %select_reduce_fusion.1.send, f32[192,2688]{1,0:T(8,128)S(1)} %copy-done.7), custom_call_target="tpu_custom_call" | custom-call | bytes 6291456 | tf_op jit(solution)/shard_map/unit_pack/pallas_call | solution.py:105
  6.3 7.3 %all-to-all-start.2 = ((f32[16,2,192,128]{3,2,1,0:T(8,128)}), f32[16,2,192,128]{3,2,1,0:T(8,128)S(1)}, u32[]{:S(2)}, u32[]{:S(2)}) async-start(f32[16,2,192,128]{3,2,1,0:T(8,128)} %bitcast.8), calls=%async_computation.2 | async-start | bytes 6291456 | tf_op jit(solution)/shard_map/all_to_all | solution.py:311
  15.3 2.5 %unit_pack.2 = f32[32,192,128]{2,1,0:T(8,128)} custom-call(s32[32]{0:T(128)S(1)} %select_reduce_fusion.1.send, f32[192,2688]{1,0:T(8,128)S(1)} %copy-done.8), custom_call_target="tpu_custom_call" | custom-call | bytes 6291456 | tf_op jit(solution)/shard_map/unit_pack/pallas_call | solution.py:105
  17.8 38.7 %all-to-all-done.2 = f32[16,2,192,128]{3,2,1,0:T(8,128)S(1)} async-done(((f32[16,2,192,128]{3,2,1,0:T(8,128)}), f32[16,2,192,128]{3,2,1,0:T(8,128)S(1)}, u32[]{:S(2)}, u32[]{:S(2)}) %all-to-all-start.2) | async-done | bytes 3145760 | tf_op jit(solution)/shard_map/all_to_all | solution.py:311
  58.2 9.2 %all-to-all-start.1 = ((f32[16,2,192,128]{3,2,1,0:T(8,128)}), f32[16,2,192,128]{3,2,1,0:T(8,128)S(1)}, u32[]{:S(2)}, u32[]{:S(2)}) async-start(f32[16,2,192,128]{3,2,1,0:T(8,128)} %bitcast.6), calls=%async_computation.1 | async-start | bytes 6291456 | tf_op jit(solution)/shard_map/all_to_all | solution.py:311
  67.5 3.6 %compare_reduce_fusion.1 = pred[192,8]{1,0:T(8,128)(4,1)S(1)} fusion(s32[8,192]{1,0:T(8,128)S(1)} %copy-done.11, s32[192]{0:T(256)S(1)} %bitcast.18), kind=kLoop, calls=%fused_computation.4 | loop fusion | flops 588288 | bytes 8448 | tf_op jit(solution)/shard_map/reduce_or | solution.py:49
  73.0 3.6 %row_pack.1 = (f32[40,2688]{1,0:T(8,128)S(1)}, f32[40,2688]{1,0:T(8,128)S(1)}, f32[40,2688]{1,0:T(8,128)S(1)}, f32[40,2688]{1,0:T(8,128)S(1)}, f32[40,2688]{1,0:...) custom-call(bf16[320,192]{1,0:T(8,128)(2,1)S(1)} %fusion.1.onehot, ...), custom_call_target="tpu_custom_call" | custom-call | flops 990904320 | bytes 6291456 | tf_op jit(solution)/shard_map/row_pack/pallas_call | solution.py:131
  76.7 2.0 collective-permute-start.1
  85.6 5.9 %collective-permute-done.1.rest_2_ = f32[40,2688]{1,0:T(8,128)S(1)} collective-permute-done((f32[40,2688]{1,0:T(8,128)S(1)}, f32[40,2688]{1,0:T(8,128)S(1)}, u32[]{:S(2)}, u32[]{:S(2)}) %collective-permute-start.1) | collective-permute-done | bytes 430112 | tf_op jit(solution)/shard_map/ppermute | solution.py:306
  92.3 3.7 %fusion = s32[192]{0:T(256)S(1)} fusion(s32[8,192]{1,0:T(8,128)S(1)} %broadcast_add_fusion, s32[8,192]{1,0:T(8,128)S(1)} %copy-done.10, s32[192]{0:T(256)S(1)} %bitcast.17), kind=kLoop, calls=%fused_computation.2 | loop fusion | flops 884544 | bytes 13824 | tf_op jit(solution)/shard_map/reduce_sum | solution.py:60
  96.2 4.0 %collective-permute-done.2.rest_3_ = f32[40,2688]{1,0:T(8,128)S(1)} collective-permute-done((f32[40,2688]{1,0:T(8,128)S(1)}, f32[40,2688]{1,0:T(8,128)S(1)}, u32[]{:S(2)}, u32[]{:S(2)}) %collective-permute-start.2) | collective-permute-done | bytes 430112 | tf_op jit(solution)/shard_map/ppermute | solution.py:306
  100.2 11.1 %collective-permute-done.3.rest_4_ = f32[40,2688]{1,0:T(8,128)S(1)} collective-permute-done((f32[40,2688]{1,0:T(8,128)S(1)}, f32[40,2688]{1,0:T(8,128)S(1)}, u32[]{:S(2)}, u32[]{:S(2)}) %collective-permute-start.3) | collective-permute-done | bytes 430112 | tf_op jit(solution)/shard_map/ppermute | solution.py:306
  111.4 8.3 %collective-permute-done.4.rest_5_ = f32[40,2688]{1,0:T(8,128)S(1)} collective-permute-done((f32[40,2688]{1,0:T(8,128)S(1)}, f32[40,2688]{1,0:T(8,128)S(1)}, u32[]{:S(2)}, u32[]{:S(2)}) %collective-permute-start.4) | collective-permute-done | bytes 430112 | tf_op jit(solution)/shard_map/ppermute | solution.py:306
  119.8 6.1 %row_unit_pack.1 = f32[32,192,128]{2,1,0:T(8,128)} custom-call(s32[32]{0:T(128)S(1)} %select_reduce_fusion.1.send, bf16[192,320]{1,0:T(8,128)(2,1)S(1)} %fusion.2.onehot, f32[40,2688]{1,0:T(8,128)S(1)} %get-tuple-element.30.rest_0_, f32[40,2688]{1,0:T(8,128)S(1)} %collective-permute-done.rest_1_, f32[40,2688]{1,0:T(8,128)S(1)} %collective-permute-done.1.rest_2_, ...), custom_call_target="tpu_custom_call" | custom-call | flops 990904320 | bytes 7340032 | tf_op jit(solution)/shard_map/row_unit_pack/pallas_call | solution.py:212
  127.5 7.3 %all-to-all-start = ((f32[16,2,192,128]{3,2,1,0:T(8,128)}), f32[16,2,192,128]{3,2,1,0:T(8,128)S(1)}, u32[]{:S(2)}, u32[]{:S(2)}) async-start(f32[16,2,192,128]{3,2,1,0:T(8,128)} %bitcast.4), calls=%async_computation | async-start | bytes 6291456 | tf_op jit(solution)/shard_map/all_to_all | solution.py:311
  138.5 4.8 %unit_row_pack.3 = (f32[40,2688]{1,0:T(8,128)S(1)}, f32[40,2688]{1,0:T(8,128)S(1)}, f32[40,2688]{1,0:T(8,128)S(1)}, f32[40,2688]{1,0:T(8,128)S(1)}, f32[40,2688]...) custom-call(s32[21]{0:T(128)S(1)} %multiply_add_fusion.2.take, ...), custom_call_target="tpu_custom_call" | custom-call | flops 990904320 | bytes 6291456 | tf_op jit(solution)/shard_map/unit_row_pack/pallas_call | solution.py:172
  143.4 3.5 %collective-permute-start.15 = (f32[40,2688]{1,0:T(8,128)S(1)}, f32[40,2688]{1,0:T(8,128)S(1)}, u32[]{:S(2)}, u32[]{:S(2)}) collective-permute-start(f32[40,2688]{1,0:T(8,128)S(1)} %get-tuple-element.48), channel_id=1, source_target_pairs={{0,32},{16,48},{32,64},{48,80},{64,96},{80,112},{96,0},{112,16},{1... | collective-permute-start | bytes 1290248 | tf_op jit(solution)/shard_map/ppermute | solution.py:306
  150.0 4.8 %unit_row_pack.2 = (f32[40,2688]{1,0:T(8,128)S(1)}, f32[40,2688]{1,0:T(8,128)S(1)}, f32[40,2688]{1,0:T(8,128)S(1)}, f32[40,2688]{1,0:T(8,128)S(1)}, f32[40,2688]...) custom-call(s32[21]{0:T(128)S(1)} %multiply_add_fusion.2.take, ...), custom_call_target="tpu_custom_call" | custom-call | flops 990904320 | bytes 6291456 | tf_op jit(solution)/shard_map/unit_row_pack/pallas_call | solution.py:172
  154.8 3.2 %collective-permute-start.19 = (f32[40,2688]{1,0:T(8,128)S(1)}, f32[40,2688]{1,0:T(8,128)S(1)}, u32[]{:S(2)}, u32[]{:S(2)}) collective-permute-start(f32[40,2688]{1,0:T(8,128)S(1)} %get-tuple-element.52), channel_id=1, source_target_pairs={{0,96},{16,112},{32,0},{48,16},{64,32},{80,48},{96,64},{112,80},{1... | collective-permute-start | bytes 1290248 | tf_op jit(solution)/shard_map/ppermute | solution.py:306
  158.1 8.2 %collective-permute-done.16.rest_3_ = f32[40,2688]{1,0:T(8,128)S(1)} collective-permute-done((f32[40,2688]{1,0:T(8,128)S(1)}, f32[40,2688]{1,0:T(8,128)S(1)}, u32[]{:S(2)}, u32[]{:S(2)}) %collective-permute-start.16) | collective-permute-done | bytes 430112 | tf_op jit(solution)/shard_map/ppermute | solution.py:306
  166.4 10.8 %collective-permute-done.17.rest_4_ = f32[40,2688]{1,0:T(8,128)S(1)} collective-permute-done((f32[40,2688]{1,0:T(8,128)S(1)}, f32[40,2688]{1,0:T(8,128)S(1)}, u32[]{:S(2)}, u32[]{:S(2)}) %collective-permute-start.17) | collective-permute-done | bytes 430112 | tf_op jit(solution)/shard_map/ppermute | solution.py:306
  177.2 8.4 %collective-permute-done.18.rest_5_ = f32[40,2688]{1,0:T(8,128)S(1)} collective-permute-done((f32[40,2688]{1,0:T(8,128)S(1)}, f32[40,2688]{1,0:T(8,128)S(1)}, u32[]{:S(2)}, u32[]{:S(2)}) %collective-permute-start.18) | collective-permute-done | bytes 430112 | tf_op jit(solution)/shard_map/ppermute | solution.py:306
  185.6 2.4 collective-permute-start.10
  189.5 2.3 collective-permute-start.12
  191.8 3.5 %collective-permute-done.8.rest_2_ = f32[40,2688]{1,0:T(8,128)S(1)} collective-permute-done((f32[40,2688]{1,0:T(8,128)S(1)}, f32[40,2688]{1,0:T(8,128)S(1)}, u32[]{:S(2)}, u32[]{:S(2)}) %collective-permute-start.8) | collective-permute-done | bytes 430112 | tf_op jit(solution)/shard_map/ppermute | solution.py:306
  196.1 4.9 %new_second.1.second = f32[192,2688]{1,0:T(8,128)} custom-call(bf16[192,320]{1,0:T(8,128)(2,1)S(1)} %fusion.2.onehot, f32[192,2688]{1,0:T(8,128)S(1)} %copy-done, f32[40,2688]{1,0:T(8,128)S(1)} %get-tuple-element.46.rest_0_, f32[40,2688]{1,0:T(8,128)S(1)} %collective-permute-done.14.rest_1_, f32[40,2688]{1,0:T(8,128)S(1)} %collective-permute-done.15.rest_2_, ...), custom_call_target="tpu_custom_call" | custom-call | flops 990904320 | bytes 7340032 | tf_op jit(solution)/shard_map/new_second/pallas_call | solution.py:242
  201.0 3.6 %collective-permute-done.9.rest_3_ = f32[40,2688]{1,0:T(8,128)S(1)} collective-permute-done((f32[40,2688]{1,0:T(8,128)S(1)}, f32[40,2688]{1,0:T(8,128)S(1)}, u32[]{:S(2)}, u32[]{:S(2)}) %collective-permute-start.9) | collective-permute-done | bytes 430112 | tf_op jit(solution)/shard_map/ppermute | solution.py:306
  204.6 9.5 %collective-permute-done.10.rest_4_ = f32[40,2688]{1,0:T(8,128)S(1)} collective-permute-done((f32[40,2688]{1,0:T(8,128)S(1)}, f32[40,2688]{1,0:T(8,128)S(1)}, u32[]{:S(2)}, u32[]{:S(2)}) %collective-permute-start.10) | collective-permute-done | bytes 430112 | tf_op jit(solution)/shard_map/ppermute | solution.py:306
  214.1 8.3 %collective-permute-done.11.rest_5_ = f32[40,2688]{1,0:T(8,128)S(1)} collective-permute-done((f32[40,2688]{1,0:T(8,128)S(1)}, f32[40,2688]{1,0:T(8,128)S(1)}, u32[]{:S(2)}, u32[]{:S(2)}) %collective-permute-start.11) | collective-permute-done | bytes 430112 | tf_op jit(solution)/shard_map/ppermute | solution.py:306
  222.4 3.8 %collective-permute-done.13.rest_7_ = f32[40,2688]{1,0:T(8,128)S(1)} collective-permute-done((f32[40,2688]{1,0:T(8,128)S(1)}, f32[40,2688]{1,0:T(8,128)S(1)}, u32[]{:S(2)}, u32[]{:S(2)}) %collective-permute-start.13) | collective-permute-done | bytes 430112 | tf_op jit(solution)/shard_map/ppermute | solution.py:306
  226.2 4.9 %new_first.1.first = f32[192,2688]{1,0:T(8,128)} custom-call(bf16[192,320]{1,0:T(8,128)(2,1)S(1)} %fusion.2.onehot, f32[192,2688]{1,0:T(8,128)S(1)} %copy-done, f32[40,2688]{1,0:T(8,128)S(1)} %get-tuple-element.38.rest_0_, f32[40,2688]{1,0:T(8,128)S(1)} %collective-permute-done.7.rest_1_, f32[40,2688]{1,0:T(8,128)S(1)} %collective-permute-done.8.rest_2_, ...), custom_call_target="tpu_custom_call" | custom-call | flops 990904320 | bytes 7340032 | tf_op jit(solution)/shard_map/new_first/pallas_call | solution.py:242
  234.3 5.2 %weight_update.1 = (f32[192,2688]{1,0:T(8,128)}, f32[192,2688]{1,0:T(8,128)}) custom-call(s32[21]{0:T(128)S(1)} %multiply_add_fusion.2.take, f32[2]{0:T(128)S(1)} %pad_maximum_fusion.fixes, f32[32,192,128]{2,1,0:T(8,128)S(1)} %bitcast.13, f32[192,2688]{1,0:T(8,128)S(1)} %copy-done.2, f32[192,2688]{1,0:T(8,128)S(1)} %copy-done.1), custom_call_target="tpu_custom_call" | custom-call | bytes 10485760 | tf_op jit(solution)/shard_map/weight_update/pallas_call | solution.py:283
  (73 shorter events, 30.1 us)
Async XLA Ops:
  2.3 1.6 copy-start.7
  6.3 50.1 %all-to-all-start.2 = ((f32[16,2,192,128]{3,2,1,0:T(8,128)}), f32[16,2,192,128]{3,2,1,0:T(8,128)S(1)}, u32[]{:S(2)}, u32[]{:S(2)}) async-start(f32[16,2,192,128]{3,2,1,0:T(8,128)} %bitcast.8), calls=%async_computation.2 | async-start | bytes 6291456 | tf_op jit(solution)/shard_map/all_to_all | solution.py:311
  56.5 1.7 copy-start.5
  58.2 9.3 %copy-start.10 = (s32[8,192]{1,0:T(8,128)S(1)}, s32[8,192]{1,0:T(8,128)}, u32[]{:S(2)}) copy-start(s32[8,192]{1,0:T(8,128)} %param.12) | copy-start | bytes 18436
  58.2 9.3 %copy-start.11 = (s32[8,192]{1,0:T(8,128)S(1)}, s32[8,192]{1,0:T(8,128)}, u32[]{:S(2)}) copy-start(s32[8,192]{1,0:T(8,128)} %param.13) | copy-start | bytes 18436
  58.2 67.7 %all-to-all-start.1 = ((f32[16,2,192,128]{3,2,1,0:T(8,128)}), f32[16,2,192,128]{3,2,1,0:T(8,128)S(1)}, u32[]{:S(2)}, u32[]{:S(2)}) async-start(f32[16,2,192,128]{3,2,1,0:T(8,128)} %bitcast.6), calls=%async_computation.1 | async-start | bytes 6291456 | tf_op jit(solution)/shard_map/all_to_all | solution.py:311
  76.6 7.6 %collective-permute-start = (f32[40,2688]{1,0:T(8,128)S(1)}, f32[40,2688]{1,0:T(8,128)S(1)}, u32[]{:S(2)}, u32[]{:S(2)}) collective-permute-start(f32[40,2688]{1,0:T(8,128)S(1)} %get-tuple-element.31), channel_id=1, source_target_pairs={{0,16},{16,0},{32,48},{48,32},{64,80},{80,64},{96,112},{112,96},{1... | collective-permute-start | bytes 1290248 | tf_op jit(solution)/shard_map/ppermute | solution.py:306
  76.7 14.9 %collective-permute-start.1 = (f32[40,2688]{1,0:T(8,128)S(1)}, f32[40,2688]{1,0:T(8,128)S(1)}, u32[]{:S(2)}, u32[]{:S(2)}) collective-permute-start(f32[40,2688]{1,0:T(8,128)S(1)} %get-tuple-element.32), channel_id=1, source_target_pairs={{0,32},{16,48},{32,64},{48,80},{64,96},{80,112},{96,0},{112,16},{1... | collective-permute-start | bytes 1290248 | tf_op jit(solution)/shard_map/ppermute | solution.py:306
  78.6 21.6 %collective-permute-start.2 = (f32[40,2688]{1,0:T(8,128)S(1)}, f32[40,2688]{1,0:T(8,128)S(1)}, u32[]{:S(2)}, u32[]{:S(2)}) collective-permute-start(f32[40,2688]{1,0:T(8,128)S(1)} %get-tuple-element.33), channel_id=1, source_target_pairs={{0,48},{16,32},{32,80},{48,64},{64,112},{80,96},{96,16},{112,0},{1... | collective-permute-start | bytes 1290248 | tf_op jit(solution)/shard_map/ppermute | solution.py:306
  80.3 31.0 %collective-permute-start.3 = (f32[40,2688]{1,0:T(8,128)S(1)}, f32[40,2688]{1,0:T(8,128)S(1)}, u32[]{:S(2)}, u32[]{:S(2)}) collective-permute-start(f32[40,2688]{1,0:T(8,128)S(1)} %get-tuple-element.34), channel_id=1, source_target_pairs={{0,64},{16,80},{32,96},{48,112},{64,0},{80,16},{96,32},{112,48},{1... | collective-permute-start | bytes 1290248 | tf_op jit(solution)/shard_map/ppermute | solution.py:306
  82.3 37.3 %collective-permute-start.4 = (f32[40,2688]{1,0:T(8,128)S(1)}, f32[40,2688]{1,0:T(8,128)S(1)}, u32[]{:S(2)}, u32[]{:S(2)}) collective-permute-start(f32[40,2688]{1,0:T(8,128)S(1)} %get-tuple-element.35), channel_id=1, source_target_pairs={{0,80},{16,64},{32,112},{48,96},{64,16},{80,0},{96,48},{112,32},{1... | collective-permute-start | bytes 1290248 | tf_op jit(solution)/shard_map/ppermute | solution.py:306
  84.2 35.4 %collective-permute-start.5 = (f32[40,2688]{1,0:T(8,128)S(1)}, f32[40,2688]{1,0:T(8,128)S(1)}, u32[]{:S(2)}, u32[]{:S(2)}) collective-permute-start(f32[40,2688]{1,0:T(8,128)S(1)} %get-tuple-element.36), channel_id=1, source_target_pairs={{0,96},{16,112},{32,0},{48,16},{64,32},{80,48},{96,64},{112,80},{1... | collective-permute-start | bytes 1290248 | tf_op jit(solution)/shard_map/ppermute | solution.py:306
  91.5 28.2 %collective-permute-start.6 = (f32[40,2688]{1,0:T(8,128)S(1)}, f32[40,2688]{1,0:T(8,128)S(1)}, u32[]{:S(2)}, u32[]{:S(2)}) collective-permute-start(f32[40,2688]{1,0:T(8,128)S(1)} %get-tuple-element.37), channel_id=1, source_target_pairs={{0,112},{16,96},{32,16},{48,0},{64,48},{80,32},{96,80},{112,64},{1... | collective-permute-start | bytes 1290248 | tf_op jit(solution)/shard_map/ppermute | solution.py:306
  125.9 1.7 copy-start.3
  127.5 103.6 %all-to-all-start = ((f32[16,2,192,128]{3,2,1,0:T(8,128)}), f32[16,2,192,128]{3,2,1,0:T(8,128)S(1)}, u32[]{:S(2)}, u32[]{:S(2)}) async-start(f32[16,2,192,128]{3,2,1,0:T(8,128)} %bitcast.4), calls=%async_computation | async-start | bytes 6291456 | tf_op jit(solution)/shard_map/all_to_all | solution.py:311
  134.8 15.2 %copy-start.4 = (f32[16,2,192,128]{3,2,1,0:T(8,128)S(1)}, f32[16,2,192,128]{3,2,1,0:T(8,128)}, u32[]{:S(2)}) copy-start(f32[16,2,192,128]{3,2,1,0:T(8,128)} %copy-done.3) | copy-start | bytes 9437188
  136.7 1.9 copy-start.6
  143.3 52.8 %copy-start = (f32[192,2688]{1,0:T(8,128)S(1)}, f32[192,2688]{1,0:T(8,128)}, u32[]{:S(2)}) copy-start(f32[192,2688]{1,0:T(8,128)} %gradient.3) | copy-start | bytes 6193156
  143.3 11.5 %collective-permute-start.14 = (f32[40,2688]{1,0:T(8,128)S(1)}, f32[40,2688]{1,0:T(8,128)S(1)}, u32[]{:S(2)}, u32[]{:S(2)}) collective-permute-start(f32[40,2688]{1,0:T(8,128)S(1)} %get-tuple-element.47), channel_id=1, source_target_pairs={{0,16},{16,0},{32,48},{48,32},{64,80},{80,64},{96,112},{112,96},{1... | collective-permute-start | bytes 1290248 | tf_op jit(solution)/shard_map/ppermute | solution.py:306
  143.4 14.6 %collective-permute-start.15 = (f32[40,2688]{1,0:T(8,128)S(1)}, f32[40,2688]{1,0:T(8,128)S(1)}, u32[]{:S(2)}, u32[]{:S(2)}) collective-permute-start(f32[40,2688]{1,0:T(8,128)S(1)} %get-tuple-element.48), channel_id=1, source_target_pairs={{0,32},{16,48},{32,64},{48,80},{64,96},{80,112},{96,0},{112,16},{1... | collective-permute-start | bytes 1290248 | tf_op jit(solution)/shard_map/ppermute | solution.py:306
  146.9 19.4 %collective-permute-start.16 = (f32[40,2688]{1,0:T(8,128)S(1)}, f32[40,2688]{1,0:T(8,128)S(1)}, u32[]{:S(2)}, u32[]{:S(2)}) collective-permute-start(f32[40,2688]{1,0:T(8,128)S(1)} %get-tuple-element.49), channel_id=1, source_target_pairs={{0,48},{16,32},{32,80},{48,64},{64,112},{80,96},{96,16},{112,0},{1... | collective-permute-start | bytes 1290248 | tf_op jit(solution)/shard_map/ppermute | solution.py:306
  147.0 30.2 %collective-permute-start.17 = (f32[40,2688]{1,0:T(8,128)S(1)}, f32[40,2688]{1,0:T(8,128)S(1)}, u32[]{:S(2)}, u32[]{:S(2)}) collective-permute-start(f32[40,2688]{1,0:T(8,128)S(1)} %get-tuple-element.50), channel_id=1, source_target_pairs={{0,64},{16,80},{32,96},{48,112},{64,0},{80,16},{96,32},{112,48},{1... | collective-permute-start | bytes 1290248 | tf_op jit(solution)/shard_map/ppermute | solution.py:306
  148.1 37.4 %collective-permute-start.18 = (f32[40,2688]{1,0:T(8,128)S(1)}, f32[40,2688]{1,0:T(8,128)S(1)}, u32[]{:S(2)}, u32[]{:S(2)}) collective-permute-start(f32[40,2688]{1,0:T(8,128)S(1)} %get-tuple-element.51), channel_id=1, source_target_pairs={{0,80},{16,64},{32,112},{48,96},{64,16},{80,0},{96,48},{112,32},{1... | collective-permute-start | bytes 1290248 | tf_op jit(solution)/shard_map/ppermute | solution.py:306
  154.8 30.8 %collective-permute-start.19 = (f32[40,2688]{1,0:T(8,128)S(1)}, f32[40,2688]{1,0:T(8,128)S(1)}, u32[]{:S(2)}, u32[]{:S(2)}) collective-permute-start(f32[40,2688]{1,0:T(8,128)S(1)} %get-tuple-element.52), channel_id=1, source_target_pairs={{0,96},{16,112},{32,0},{48,16},{64,32},{80,48},{96,64},{112,80},{1... | collective-permute-start | bytes 1290248 | tf_op jit(solution)/shard_map/ppermute | solution.py:306
  158.0 30.1 %collective-permute-start.20 = (f32[40,2688]{1,0:T(8,128)S(1)}, f32[40,2688]{1,0:T(8,128)S(1)}, u32[]{:S(2)}, u32[]{:S(2)}) collective-permute-start(f32[40,2688]{1,0:T(8,128)S(1)} %get-tuple-element.53), channel_id=1, source_target_pairs={{0,112},{16,96},{32,16},{48,0},{64,48},{80,32},{96,80},{112,64},{1... | collective-permute-start | bytes 1290248 | tf_op jit(solution)/shard_map/ppermute | solution.py:306
  166.4 23.1 %collective-permute-start.7 = (f32[40,2688]{1,0:T(8,128)S(1)}, f32[40,2688]{1,0:T(8,128)S(1)}, u32[]{:S(2)}, u32[]{:S(2)}) collective-permute-start(f32[40,2688]{1,0:T(8,128)S(1)} %get-tuple-element.39), channel_id=1, source_target_pairs={{0,16},{16,0},{32,48},{48,32},{64,80},{80,64},{96,112},{112,96},{1... | collective-permute-start | bytes 1290248 | tf_op jit(solution)/shard_map/ppermute | solution.py:306
  177.2 18.1 %collective-permute-start.8 = (f32[40,2688]{1,0:T(8,128)S(1)}, f32[40,2688]{1,0:T(8,128)S(1)}, u32[]{:S(2)}, u32[]{:S(2)}) collective-permute-start(f32[40,2688]{1,0:T(8,128)S(1)} %get-tuple-element.40), channel_id=1, source_target_pairs={{0,32},{16,48},{32,64},{48,80},{64,96},{80,112},{96,0},{112,16},{1... | collective-permute-start | bytes 1290248 | tf_op jit(solution)/shard_map/ppermute | solution.py:306
  185.6 19.0 %collective-permute-start.9 = (f32[40,2688]{1,0:T(8,128)S(1)}, f32[40,2688]{1,0:T(8,128)S(1)}, u32[]{:S(2)}, u32[]{:S(2)}) collective-permute-start(f32[40,2688]{1,0:T(8,128)S(1)} %get-tuple-element.41), channel_id=1, source_target_pairs={{0,48},{16,32},{32,80},{48,64},{64,112},{80,96},{96,16},{112,0},{1... | collective-permute-start | bytes 1290248 | tf_op jit(solution)/shard_map/ppermute | solution.py:306
  185.6 28.5 %collective-permute-start.10 = (f32[40,2688]{1,0:T(8,128)S(1)}, f32[40,2688]{1,0:T(8,128)S(1)}, u32[]{:S(2)}, u32[]{:S(2)}) collective-permute-start(f32[40,2688]{1,0:T(8,128)S(1)} %get-tuple-element.42), channel_id=1, source_target_pairs={{0,64},{16,80},{32,96},{48,112},{64,0},{80,16},{96,32},{112,48},{1... | collective-permute-start | bytes 1290248 | tf_op jit(solution)/shard_map/ppermute | solution.py:306
  188.0 34.4 %collective-permute-start.11 = (f32[40,2688]{1,0:T(8,128)S(1)}, f32[40,2688]{1,0:T(8,128)S(1)}, u32[]{:S(2)}, u32[]{:S(2)}) collective-permute-start(f32[40,2688]{1,0:T(8,128)S(1)} %get-tuple-element.43), channel_id=1, source_target_pairs={{0,80},{16,64},{32,112},{48,96},{64,16},{80,0},{96,48},{112,32},{1... | collective-permute-start | bytes 1290248 | tf_op jit(solution)/shard_map/ppermute | solution.py:306
  189.5 32.9 %collective-permute-start.12 = (f32[40,2688]{1,0:T(8,128)S(1)}, f32[40,2688]{1,0:T(8,128)S(1)}, u32[]{:S(2)}, u32[]{:S(2)}) collective-permute-start(f32[40,2688]{1,0:T(8,128)S(1)} %get-tuple-element.44), channel_id=1, source_target_pairs={{0,96},{16,112},{32,0},{48,16},{64,32},{80,48},{96,64},{112,80},{1... | collective-permute-start | bytes 1290248 | tf_op jit(solution)/shard_map/ppermute | solution.py:306
  195.3 30.9 %collective-permute-start.13 = (f32[40,2688]{1,0:T(8,128)S(1)}, f32[40,2688]{1,0:T(8,128)S(1)}, u32[]{:S(2)}, u32[]{:S(2)}) collective-permute-start(f32[40,2688]{1,0:T(8,128)S(1)} %get-tuple-element.45), channel_id=1, source_target_pairs={{0,112},{16,96},{32,16},{48,0},{64,48},{80,32},{96,80},{112,64},{1... | collective-permute-start | bytes 1290248 | tf_op jit(solution)/shard_map/ppermute | solution.py:306
  (4 other events, 6.3 us)

commit v2 on v0

v2 whole, which is shorter than its diff:
```python
import functools

import jax
import jax.numpy as jnp
from jax import lax
from jax.experimental import pallas as pl
from jax.experimental.pallas import tpu as pltpu
from jax.sharding import PartitionSpec as P

UNIT = 128
HALF = UNIT // 2
ROWS = 192
FOLD = ROWS // 2
UNITS = 21
COLS = UNIT * UNITS
DP = 8
MP = 16
ROOM = 36
PAIR = 2
SLOTS = MP * PAIR
BLOCK = ROWS + FOLD
TILES = 32
WIDE = TILES // 2 * UNIT
MESSAGE = 2 * ROOM
STACK = DP * MESSAGE
PAIRS = TILES - UNITS
CHUNK = 4
VMEM_LIMIT = 24 * 1024 * 1024

beta_one = 0.9
beta_two = 0.999
epsilon = 1e-08
learn_rate = 0.001
decay_rate = 0.1

MOVES = [(0, 0), (0, 1), (1, 0), (3, 0), (1, 1), (3, 1), (2, 0), (2, 1)]
HBM = pl.BlockSpec(memory_space=pltpu.HBM)
ANY = pl.BlockSpec(memory_space=pl.ANY)
VMEM = pl.BlockSpec(memory_space=pltpu.VMEM)
SMEM = pl.BlockSpec(memory_space=pltpu.SMEM)


def f32(*shape):
    return jax.ShapeDtypeStruct(shape, jnp.float32)


def call(kernel, name, ins, outs, out_shape, scratch, mebibytes, *args):
    return pl.pallas_call(
        kernel,
        out_shape=out_shape,
        in_specs=ins,
        out_specs=outs,
        scratch_shapes=scratch,
        compiler_params=pltpu.CompilerParams(vmem_limit_bytes=VMEM_LIMIT),
        cost_estimate=pl.CostEstimate(
            flops=0, bytes_accessed=mebibytes * 2**20, transcendentals=0
        ),
        name=name,
    )(*args)


def row_plan_kernel(place, old, new, new_turned, pack, take):
    d = place[0]
    z, c = d // 2, d % 2
    old_mine = old[pl.ds(d, 1), :]
    lane = lax.broadcasted_iota(jnp.int32, (ROWS, DP), 1)
    new_mine = jnp.sum(jnp.where(lane == d, new_turned[...], 0), axis=1, keepdims=True)
    here = lax.broadcasted_iota(jnp.int32, (ROWS, ROWS), 0)
    there = lax.broadcasted_iota(jnp.int32, (ROWS, ROWS), 1)
    earlier = (here < there).astype(jnp.float32).astype(jnp.bfloat16)

    goes, comes = [], []
    for s in range(DP):
        hit = (new_turned[:, s : s + 1] == old_mine).astype(jnp.float32)
        goes.append(jnp.max(hit, axis=0, keepdims=True))
        hit = (new_mine == old[s : s + 1, :]).astype(jnp.float32)
        comes.append(jnp.max(hit, axis=0, keepdims=True))
    both = jnp.concatenate(goes + comes, axis=0)
    before = jnp.dot(both.astype(jnp.bfloat16), earlier, preferred_element_type=jnp.float32)
    both = both.astype(jnp.int32)
    before = before.astype(jnp.int32)

    def first_slot(dz, dc):
        at = 0
        for k, move in enumerate(MOVES):
            at = jnp.where((dz == move[0]) & (dc == move[1]), k * MESSAGE, at)
        return at

    slot = jnp.zeros((1, ROWS), jnp.int32)
    origin = jnp.zeros((ROWS, ROWS), jnp.int32)
    for s in range(DP):
        core = (s % 2 + c) % 2
        to = first_slot((s // 2 - z + 4) % 4, core)
        slot = slot + both[s : s + 1] * (to + before[s : s + 1])
        source = first_slot((z - s // 2 + 4) % 4, core)
        value = source + before[DP + s : DP + s + 1]
        origin = origin + jnp.where(new_mine == old[s : s + 1, :], value, 0)
    origin = jnp.sum(origin, axis=1, keepdims=True)

    def onehot(equal):
        return equal.astype(jnp.float32).astype(jnp.bfloat16)

    index = lax.broadcasted_iota(jnp.int32, (STACK, ROWS), 0)
    pack[0] = onehot(index == slot)
    pack[1] = onehot(index == slot + ROOM)
    index = lax.broadcasted_iota(jnp.int32, (ROWS, STACK), 1)
    take[:ROWS] = onehot(index == origin)
    take[ROWS:] = onehot(index == origin + ROOM)


def row_plan(old_rows, new_rows):
    place = lax.axis_index("dp").astype(jnp.int32).reshape(1)
    pack = jax.ShapeDtypeStruct((2, STACK, ROWS), jnp.bfloat16)
    take = jax.ShapeDtypeStruct((2 * ROWS, STACK), jnp.bfloat16)
    return call(
        row_plan_kernel,
        "row_plan",
        [SMEM, VMEM, VMEM, VMEM],
        [VMEM] * 2,
        [pack, take],
        [],
        1,
        place,
        old_rows,
        new_rows,
        new_rows.T,
    )


def unit_plan_kernel(place, units, turned, send, take):
    m = place[0]
    lane = lax.broadcasted_iota(jnp.int32, (1, UNIT), 1)
    line = lax.broadcasted_iota(jnp.int32, (UNITS, 1), 0)
    earlier = line < lane

    to_row = jnp.zeros((UNITS, UNIT), jnp.int32)
    to_column = jnp.zeros((UNITS, UNITS), jnp.int32)
    for t in range(1, MP):
        to_row = to_row + jnp.where(turned[:, t : t + 1] == m * UNITS + lane, t, 0)
        to_column = to_column + jnp.where(units[t : t + 1, :] == m * UNITS + line, t, 0)
    to_row = jnp.sum(to_row, axis=0, keepdims=True)
    to_column = jnp.sum(to_column, axis=1, keepdims=True)
    rank = jnp.sum(((to_row == to_column) & earlier).astype(jnp.int32), axis=0, keepdims=True)
    send[...] = to_row * PAIR + rank

    row = units[pl.ds(m, 1), :]
    column = lax.broadcasted_iota(jnp.int32, (UNITS, MP), 1) == m
    column = jnp.sum(jnp.where(column, turned[...], 0), axis=1, keepdims=True)
    from_row, from_column = jnp.zeros_like(row), jnp.zeros_like(column)
    for t in range(1, MP):
        from_row = from_row + (row >= t * UNITS).astype(jnp.int32)
        from_column = from_column + (column >= t * UNITS).astype(jnp.int32)
    lower = (from_row == from_column) & (column < row)
    take[...] = from_row * PAIR + jnp.sum(lower.astype(jnp.int32), axis=0, keepdims=True)


def unit_plan(new_units):
    place = lax.axis_index("mp").astype(jnp.int32).reshape(1)
    return call(
        unit_plan_kernel,
        "unit_plan",
        [SMEM, VMEM, VMEM],
        [VMEM] * 2,
        [jax.ShapeDtypeStruct((1, n), jnp.int32) for n in (UNIT, UNITS)],
        [],
        1,
        place,
        new_units,
        new_units.T,
    )


def terms(values):
    high = values.astype(jnp.bfloat16)
    rest = values - high.astype(jnp.float32)
    middle = rest.astype(jnp.bfloat16)
    low = (rest - middle.astype(jnp.float32)).astype(jnp.bfloat16)
    return high, middle, low


def select_rows(onehot, split):
    dot = functools.partial(jnp.dot, preferred_element_type=jnp.float32)
    return (dot(onehot, split[0]) + dot(onehot, split[1])) + dot(onehot, split[2])


def columns_of(u):
    return slice(u * UNIT, (u + 1) * UNIT)


def swapped(x):
    return pltpu.roll(x, HALF, 1)


def left_lanes(rows):
    return lax.broadcasted_iota(jnp.int32, (rows, UNIT), 1) < HALF


def folded(x, upper):
    first, last = x[:FOLD], x[FOLD:]
    if upper:
        return jnp.where(left_lanes(FOLD), swapped(first), last)
    return jnp.where(left_lanes(FOLD), first, swapped(last))


def unfolded(y, upper):
    if upper:
        return jnp.concatenate([swapped(y), y], axis=0)
    return jnp.concatenate([y, swapped(y)], axis=0)


def pack_rows(tile, pack, outs):
    for i in range(0, TILES // 2, CHUNK):
        left = jnp.concatenate([tile(n) for n in range(i, i + CHUNK)], axis=1)
        right = jnp.concatenate([tile(TILES // 2 + n) for n in range(i, i + CHUNK)], axis=1)
        packed = select_rows(pack[0], terms(left)) + select_rows(pack[1], terms(right))
        for k, out in enumerate(outs):
            out[:, i * UNIT : (i + CHUNK) * UNIT] = packed[k * MESSAGE : (k + 1) * MESSAGE]


def take_rows(parts, take, put):
    for i in range(0, TILES // 2, CHUNK):
        columns = slice(i * UNIT, (i + CHUNK) * UNIT)
        values = jnp.concatenate([p[:, columns] for p in parts], axis=0)
        picked = select_rows(take[...], terms(values))
        for k in range(CHUNK):
            put(i + k, picked[:ROWS, columns_of(k)])
            put(TILES // 2 + i + k, picked[ROWS:, columns_of(k)])


class Copies:
    def __init__(self, sems):
        self.sems, self.waiting = sems, []

    def start(self, source, target):
        copy = pltpu.make_async_copy(source, target, self.sems.at[len(self.waiting)])
        copy.start()
        self.waiting.append(copy)
        return copy

    def wait(self):
        for copy in self.waiting:
            copy.wait()


PARTS = 3


class Loads:
    def __init__(self, sems):
        self.sems, self.arrays = sems, []

    def start(self, source, target):
        parts = []
        for i in range(PARTS):
            columns = slice(i * COLS // PARTS, (i + 1) * COLS // PARTS)
            sem = self.sems.at[len(self.arrays) * PARTS + i]
            parts.append(
                pltpu.make_async_copy(source.at[:, columns], target.at[:, columns], sem)
            )
            parts[-1].start()
        self.arrays.append(parts)

    def wait(self, array, unit):
        parts = self.arrays[array]
        for i in range(unit * PARTS // UNITS + 1):
            if parts[i] is not None:
                parts[i].wait()
                parts[i] = None


MESSAGES = [f32(MESSAGE, WIDE)] * DP
SLOT_ARRAY = pltpu.HBM((SLOTS, BLOCK, UNIT), jnp.float32)
SLOT_SPEC = HBM
ARRAY = pltpu.VMEM((ROWS, COLS), jnp.float32)
FOLDS = pltpu.VMEM((UNITS, FOLD, UNIT), jnp.float32)
HELD = pltpu.VMEM((UNITS, ROWS, UNIT), jnp.float32)


def dma(n):
    return pltpu.SemaphoreType.DMA((n,))


def unit_pack_kernel(send, whole, half, out, whole_here, half_here, folds, loads, stores):
    loads, stores = Loads(loads), Copies(stores)
    loads.start(whole, whole_here)
    loads.start(half, half_here)
    for u in range(UNITS):
        loads.wait(0, u)
        stores.start(whole_here.at[:, columns_of(u)], out.at[send[0, u], pl.ds(0, ROWS)])
    for u in range(UNITS):
        loads.wait(1, u)
        folds[u] = folded(half_here[:, columns_of(u)], True)
        stores.start(folds.at[u], out.at[send[0, u], pl.ds(ROWS, FOLD)])
    stores.wait()


def unit_pack(whole, half, send):
    return call(
        unit_pack_kernel,
        "unit_pack",
        [SMEM, HBM, HBM],
        SLOT_SPEC,
        SLOT_ARRAY,
        [ARRAY, ARRAY, FOLDS, dma(2 * PARTS), dma(2 * UNITS)],
        9,
        send,
        whole,
        half,
    )


def row_pack_kernel(pack, whole, half, *rest):
    outs, (whole_here, half_here, loads) = rest[:DP], rest[DP:]
    loads = Loads(loads)
    loads.start(whole, whole_here)
    loads.start(half, half_here)

    def unit(k, u):
        u = min(u, UNITS - 1)
        loads.wait(k, u)
        return (whole_here, half_here)[k][:, columns_of(u)]

    def tile(n):
        if n < UNITS:
            return unit(0, n)
        u = 2 * (n - UNITS)
        return jnp.where(left_lanes(ROWS), unit(1, u), swapped(unit(1, u + 1)))

    pack_rows(tile, pack, outs)


def row_pack(whole, half, pack):
    return call(
        row_pack_kernel,
        "row_pack",
        [VMEM, HBM, HBM],
        [VMEM] * DP,
        MESSAGES,
        [ARRAY, ARRAY, dma(2 * PARTS)],
        9,
        pack,
        whole,
        half,
    )


def unit_row_pack_kernel(take, pack, recv, *rest):
    outs, (here, sems) = rest[:DP], rest[DP:]
    copies, arriving = Copies(sems), {}
    for i in range(0, TILES // 2, CHUNK):
        for n in [*range(i, i + CHUNK), *range(TILES // 2 + i, TILES // 2 + i + CHUNK)]:
            if n < UNITS:
                arriving[n] = copies.start(recv.at[take[0, n]], here.at[n])

    def unit(u):
        if u in arriving:
            arriving.pop(u).wait()
        return here.at[u]

    def tile(n):
        if n < UNITS:
            return unit(n)[:ROWS]
        u = 2 * (n - UNITS)
        a = unfolded(unit(u)[ROWS:], False)
        b = unfolded(unit(min(u + 1, UNITS - 1))[ROWS:], True)
        return jnp.where(left_lanes(ROWS), a, b)

    pack_rows(tile, pack, outs)


def unit_row_pack(recv, take, pack):
    return call(
        unit_row_pack_kernel,
        "unit_row_pack",
        [SMEM, VMEM, ANY],
        [VMEM] * DP,
        MESSAGES,
        [pltpu.VMEM((UNITS, BLOCK, UNIT), jnp.float32), dma(UNITS)],
        10,
        take,
        pack,
        recv,
    )


def row_unit_pack_kernel(send, take, *rest):
    parts, (out, held, folds, sems) = rest[:DP], rest[DP:]
    copies = Copies(sems)

    def put(n, tile):
        if n < UNITS:
            held[n] = tile
            copies.start(held.at[n], out.at[send[0, n], pl.ds(0, ROWS)])
            return
        for u, upper in ((2 * (n - UNITS), False), (2 * (n - UNITS) + 1, True)):
            if u < UNITS:
                folds[u] = folded(tile, upper)
                copies.start(folds.at[u], out.at[send[0, u], pl.ds(ROWS, FOLD)])

    take_rows(parts, take, put)
    copies.wait()


def row_unit_pack(parts, send, take):
    return call(
        row_unit_pack_kernel,
        "row_unit_pack",
        [SMEM] + [VMEM] * (1 + DP),
        SLOT_SPEC,
        SLOT_ARRAY,
        [HELD, FOLDS, dma(2 * UNITS)],
        10,
        send,
        take,
        *parts,
    )


def first_kernel(gradient, take, *rest):
    parts, (first, half, held, half_held, sems) = rest[:DP], rest[DP:]
    copies = Copies(sems)

    def put(n, tile):
        if n < UNITS:
            columns = columns_of(n)
            moment = beta_one * tile + (1.0 - beta_one) * gradient[:, columns]
            held[:, columns] = moment
            copies.start(held.at[:, columns], first.at[:, columns])
        else:
            half_held[n - UNITS] = tile
            copies.start(half_held.at[n - UNITS], half.at[n - UNITS])

    take_rows(parts, take, put)
    copies.wait()


def first_moment(parts, take, gradient):
    return call(
        first_kernel,
        "first_moment",
        [VMEM] * (2 + DP),
        [HBM, HBM],
        [pltpu.HBM((ROWS, COLS), jnp.float32), pltpu.HBM((PAIRS, ROWS, UNIT), jnp.float32)],
        [ARRAY, pltpu.VMEM((PAIRS, ROWS, UNIT), jnp.float32), dma(TILES)],
        11,
        gradient,
        take,
        *parts,
    )


def update_kernel(take, fixes, recv, first, half, gradient, *rest):
    outs, helds, rest = rest[:3], rest[3:6], rest[6:]
    here, first_here, half_here, gradient_here, whole_loads, unit_loads, stores = rest
    loads, whole, stores = Copies(unit_loads), Loads(whole_loads), Copies(stores)
    arrivals = [loads.start(recv.at[take[0, u]], here.at[u]) for u in range(UNITS // 3)]
    whole.start(gradient, gradient_here)
    whole.start(first, first_here)
    halves = loads.start(half, half_here)
    arrivals += [loads.start(recv.at[take[0, u]], here.at[u]) for u in range(UNITS // 3, UNITS)]
    for u in range(UNITS):
        arrivals[u].wait()
        columns = columns_of(u)
        weight = here[u, :ROWS]
        lower = unfolded(here[u, ROWS:], False)
        if u == 0:
            halves.wait()
        upper = half_here[u // 2]
        if u % 2 == 0:
            upper = swapped(upper)
        second = jnp.where(left_lanes(ROWS), lower, upper)
        whole.wait(0, u)
        g = gradient_here[:, columns]
        second = beta_two * second + (1.0 - beta_two) * g * g
        root = jnp.sqrt(second / fixes[1]) + epsilon
        whole.wait(1, u)
        update = first_here[:, columns] / fixes[0] / root + decay_rate * weight
        for held, out, value in zip(helds, outs, (weight - learn_rate * update, second, update)):
            held[:, columns] = value
            stores.start(held.at[:, columns], out.at[:, columns])
    stores.wait()


def weight_update(recv, take, fixes, first, half, gradient):
    return call(
        update_kernel,
        "weight_update",
        [SMEM, SMEM, ANY] + [HBM] * 3,
        [HBM] * 3,
        [f32(ROWS, COLS)] * 3,
        [ARRAY] * 3
        + [
            pltpu.VMEM((UNITS, BLOCK, UNIT), jnp.float32),
            ARRAY,
            pltpu.VMEM((PAIRS, ROWS, UNIT), jnp.float32),
            ARRAY,
            dma(2 * PARTS),
            dma(UNITS + 1),
            dma(3 * UNITS),
        ],
        16,
        take,
        fixes,
        recv,
        first,
        half,
        gradient,
    )


def swap_rows(parts):
    arrived = []
    for part, (dz, dc) in zip(parts, MOVES):
        pairs = [(z * 2 + c, (z + dz) % 4 * 2 + (c + dc) % 2) for z in range(4) for c in range(2)]
        arrived.append(lax.ppermute(part, "dp", pairs) if dz or dc else part)
    return arrived


def swap_units(packed):
    packed = packed.reshape(MP, PAIR, BLOCK, UNIT)
    arrived = lax.all_to_all(packed, "mp", split_axis=0, concat_axis=0, tiled=True)
    return arrived.reshape(SLOTS, BLOCK, UNIT)


def body(old_weight, old_first, old_second, gradient, old_rows, new_rows, new_units, step):
    send, take_units = unit_plan(new_units)
    pack, take = row_plan(old_rows, new_rows)
    in_hbm = functools.partial(pltpu.with_memory_space_constraint, memory_space=pltpu.HBM)
    count = step[0].astype(jnp.float32)
    fixes = jnp.stack(
        [
            1.0 - jnp.power(jnp.float32(beta_one), count),
            1.0 - jnp.power(jnp.float32(beta_two), count),
        ]
    )

    units = swap_units(unit_pack(in_hbm(old_first), in_hbm(old_second), send))
    rows = swap_rows(row_pack(in_hbm(old_weight), in_hbm(old_second), pack))
    packed = row_unit_pack(rows, send, take)
    units, packed = lax.optimization_barrier((units, packed))

    units_two = swap_units(packed)
    rows_two = swap_rows(unit_row_pack(units, take_units, pack))

    new_first, half = first_moment(rows_two, take, gradient)
    new_weight, new_second, update = weight_update(
        units_two, take_units, fixes, in_hbm(new_first), in_hbm(half), in_hbm(gradient)
    )
    return new_weight, new_first, new_second, update


def solution(mesh):
    return jax.shard_map(
        body,
        mesh=mesh,
        in_specs=(P("dp", "mp"), P("dp", "mp"), P("dp", "mp"), P("dp", "mp"), P(), P(), P(), P()),
        out_specs=(P("dp", "mp"), P("dp", "mp"), P("dp", "mp"), P("dp", "mp")),
        check_vma=False,
    )
```

time: 372 us -> 171 us (0.46)
  the two profiles are of different devices: /device:TPU:12 before, /device:TPU:1 now
where the time goes in v2:
time: 171 us
  waiting for transfers between devices  70.6 us (41%)
  starting transfers between devices  59.5 us (35%)
  Pallas kernels  37.7 us (22%)
    ppermute x14, waiting for transfers between devices, swap_rows(): arrived.append(lax.ppermute(part, 'dp', pairs) if dz or dc else part)  69.8 us
    ppermute x14, starting transfers between devices, swap_rows(): arrived.append(lax.ppermute(part, 'dp', pairs) if dz or dc else part)  44.7 us
    pallas_call x8, Pallas kernels, call(): pl.pallas_call(kernel, out_shape=out_shape, in_specs=ins, out_specs=outs,...  37.7 us
    all_to_all x2, starting transfers between devices, swap_units(): lax.all_to_all(packed, 'mp', split_axis=0, concat_axis=0, tiled=True)  14.7 us
  transfers between devices with their start and end apart: 16, of which 9 were waited for; matrix products, arithmetic and copies ran while one was open for 0% of the time, Pallas kernels for 15%

profile of v2, /device:TPU:1, one launch (start us, length us, event | category | flops | bytes accessed | tf_op | source)
XLA Modules:
  0.0 171.0 jit_solution(5497155815710254178)
XLA Ops:
  0.6 0.8 copy.12
  1.4 0.7 copy-done.2
  2.1 0.2 unit_plan.1
  2.3 4.3 %unit_pack.1 = f32[32,288,128]{2,1,0:T(8,128)} custom-call(s32[1,128]{1,0:T(1,128)S(1)} %get-tuple-element.32.send, f32[192,2688]{1,0:T(8,128)} %whole.2, f32[192,2688]{1,0:T(8,128)} %half.3), custom_call_target="tpu_custom_call" | custom-call | bytes 9437184 | tf_op jit(solution)/shard_map/unit_pack/pallas_call | solution.py:48
  6.6 7.7 %all-to-all-start = ((f32[16,2,288,128]{3,2,1,0:T(8,128)}), f32[16,2,288,128]{3,2,1,0:T(8,128)}, u32[]{:S(2)}, u32[]{:S(2)}) async-start(f32[16,2,288,128]{3,2,1,0:T(8,128)} %bitcast.11), calls=%async_computation | async-start | bytes 9437184 | tf_op jit(solution)/shard_map/all_to_all | solution.py:521
  14.4 1.2 row_plan.1
  15.6 6.1 %row_pack.1 = (f32[72,2048]{1,0:T(8,128)S(1)}, f32[72,2048]{1,0:T(8,128)S(1)}, f32[72,2048]{1,0:T(8,128)S(1)}, f32[72,2048]{1,0:T(8,128)S(1)}, f32[72,2048]{1,0:...) custom-call(bf16[2,576,192]{2,1,0:T(8,128)(2,1)S(1)} %get-tuple-element.34.pack, ...), custom_call_target="tpu_custom_call" | custom-call | bytes 9437184 | tf_op jit(solution)/shard_map/row_pack/pallas_call | solution.py:48
  21.7 1.0 collective-permute-start
  22.7 1.7 collective-permute-start.1
  24.4 2.1 %collective-permute-start.2 = (f32[72,2048]{1,0:T(8,128)S(1)}, f32[72,2048]{1,0:T(8,128)S(1)}, u32[]{:S(2)}, u32[]{:S(2)}) collective-permute-start(f32[72,2048]{1,0:T(8,128)S(1)} %get-tuple-element.38), channel_id=1, source_target_pairs={{0,96},{16,112},{32,0},{48,16},{64,32},{80,48},{96,64},{112,80},{1... | collective-permute-start | bytes 1769480 | tf_op jit(solution)/shard_map/ppermute | solution.py:515
  26.5 3.0 %collective-permute-start.4 = (f32[72,2048]{1,0:T(8,128)S(1)}, f32[72,2048]{1,0:T(8,128)S(1)}, u32[]{:S(2)}, u32[]{:S(2)}) collective-permute-start(f32[72,2048]{1,0:T(8,128)S(1)} %get-tuple-element.40), channel_id=1, source_target_pairs={{0,112},{16,96},{32,16},{48,0},{64,48},{80,32},{96,80},{112,64},{1... | collective-permute-start | bytes 1769480 | tf_op jit(solution)/shard_map/ppermute | solution.py:515
  29.5 0.2 collective-permute-start.5
  29.7 10.5 %collective-permute-done.1.rest_2_ = f32[72,2048]{1,0:T(8,128)S(1)} collective-permute-done((f32[72,2048]{1,0:T(8,128)S(1)}, f32[72,2048]{1,0:T(8,128)S(1)}, u32[]{:S(2)}, u32[]{:S(2)}) %collective-permute-start.1) | collective-permute-done | bytes 589856 | tf_op jit(solution)/shard_map/ppermute | solution.py:515
  40.2 2.2 %collective-permute-start.6 = (f32[72,2048]{1,0:T(8,128)S(1)}, f32[72,2048]{1,0:T(8,128)S(1)}, u32[]{:S(2)}, u32[]{:S(2)}) collective-permute-start(f32[72,2048]{1,0:T(8,128)S(1)} %get-tuple-element.42), channel_id=1, source_target_pairs={{0,80},{16,64},{32,112},{48,96},{64,16},{80,0},{96,48},{112,32},{1... | collective-permute-start | bytes 1769480 | tf_op jit(solution)/shard_map/ppermute | solution.py:515
  42.4 10.7 %collective-permute-done.3.rest_4_ = f32[72,2048]{1,0:T(8,128)S(1)} collective-permute-done((f32[72,2048]{1,0:T(8,128)S(1)}, f32[72,2048]{1,0:T(8,128)S(1)}, u32[]{:S(2)}, u32[]{:S(2)}) %collective-permute-start.3) | collective-permute-done | bytes 589856 | tf_op jit(solution)/shard_map/ppermute | solution.py:515
  53.1 0.1 collective-permute-done.4.rest_5_
  53.2 13.2 %collective-permute-done.5.rest_6_ = f32[72,2048]{1,0:T(8,128)S(1)} collective-permute-done((f32[72,2048]{1,0:T(8,128)S(1)}, f32[72,2048]{1,0:T(8,128)S(1)}, u32[]{:S(2)}, u32[]{:S(2)}) %collective-permute-start.5) | collective-permute-done | bytes 589856 | tf_op jit(solution)/shard_map/ppermute | solution.py:515
  66.4 12.8 %collective-permute-done.6.rest_7_ = f32[72,2048]{1,0:T(8,128)S(1)} collective-permute-done((f32[72,2048]{1,0:T(8,128)S(1)}, f32[72,2048]{1,0:T(8,128)S(1)}, u32[]{:S(2)}, u32[]{:S(2)}) %collective-permute-start.6) | collective-permute-done | bytes 589856 | tf_op jit(solution)/shard_map/ppermute | solution.py:515
  79.2 6.0 %row_unit_pack.1 = f32[32,288,128]{2,1,0:T(8,128)} custom-call(s32[1,128]{1,0:T(1,128)S(1)} %get-tuple-element.32.send, bf16[384,576]{1,0:T(8,128)(2,1)S(1)} %get-tuple-element.33.take, f32[72,2048]{1,0:T(8,128)S(1)} %get-tuple-element.35.rest_0_, f32[72,2048]{1,0:T(8,128)S(1)} %collective-permute-done.rest_1_, ...), custom_call_target="tpu_custom_call" | custom-call | bytes 10485760 | tf_op jit(solution)/shard_map/row_unit_pack/pallas_call | solution.py:48
  85.2 7.1 %all-to-all-start.1 = ((f32[16,2,288,128]{3,2,1,0:T(8,128)}), f32[16,2,288,128]{3,2,1,0:T(8,128)}, u32[]{:S(2)}, u32[]{:S(2)}) async-start(f32[16,2,288,128]{3,2,1,0:T(8,128)} %bitcast.10), calls=%async_computation.1 | async-start | bytes 9437184 | tf_op jit(solution)/shard_map/all_to_all | solution.py:521
  92.3 6.9 %unit_row_pack.1 = (f32[72,2048]{1,0:T(8,128)S(1)}, f32[72,2048]{1,0:T(8,128)S(1)}, f32[72,2048]{1,0:T(8,128)S(1)}, f32[72,2048]{1,0:T(8,128)S(1)}, f32[72,2048]...) custom-call(s32[1,21]{1,0:T(1,128)S(1)} %get-tuple-element.31.take, ...), custom_call_target="tpu_custom_call" | custom-call | bytes 10485760 | tf_op jit(solution)/shard_map/unit_row_pack/pallas_call | solution.py:48
  99.2 0.9 collective-permute-start.10
  100.0 2.2 %collective-permute-start.11 = (f32[72,2048]{1,0:T(8,128)S(1)}, f32[72,2048]{1,0:T(8,128)S(1)}, u32[]{:S(2)}, u32[]{:S(2)}) collective-permute-start(f32[72,2048]{1,0:T(8,128)S(1)} %get-tuple-element.50), channel_id=1, source_target_pairs={{0,112},{16,96},{32,16},{48,0},{64,48},{80,32},{96,80},{112,64},{1... | collective-permute-start | bytes 1769480 | tf_op jit(solution)/shard_map/ppermute | solution.py:515
  102.2 0.7 collective-permute-start.12
  102.9 2.8 %collective-permute-start.13 = (f32[72,2048]{1,0:T(8,128)S(1)}, f32[72,2048]{1,0:T(8,128)S(1)}, u32[]{:S(2)}, u32[]{:S(2)}) collective-permute-start(f32[72,2048]{1,0:T(8,128)S(1)} %get-tuple-element.52), channel_id=1, source_target_pairs={{0,80},{16,64},{32,112},{48,96},{64,16},{80,0},{96,48},{112,32},{1... | collective-permute-start | bytes 1769480 | tf_op jit(solution)/shard_map/ppermute | solution.py:515
  105.7 10.5 %collective-permute-done.10.rest_4_ = f32[72,2048]{1,0:T(8,128)S(1)} collective-permute-done((f32[72,2048]{1,0:T(8,128)S(1)}, f32[72,2048]{1,0:T(8,128)S(1)}, u32[]{:S(2)}, u32[]{:S(2)}) %collective-permute-start.10) | collective-permute-done | bytes 589856 | tf_op jit(solution)/shard_map/ppermute | solution.py:515
  116.2 28.0 %collective-permute-start.9 = (f32[72,2048]{1,0:T(8,128)S(1)}, f32[72,2048]{1,0:T(8,128)S(1)}, u32[]{:S(2)}, u32[]{:S(2)}) collective-permute-start(f32[72,2048]{1,0:T(8,128)S(1)} %get-tuple-element.48), channel_id=1, source_target_pairs={{0,96},{16,112},{32,0},{48,16},{64,32},{80,48},{96,64},{112,80},{1... | collective-permute-start | bytes 1769480 | tf_op jit(solution)/shard_map/ppermute | solution.py:515
  145.0 9.4 %collective-permute-done.8.rest_2_ = f32[72,2048]{1,0:T(8,128)S(1)} collective-permute-done((f32[72,2048]{1,0:T(8,128)S(1)}, f32[72,2048]{1,0:T(8,128)S(1)}, u32[]{:S(2)}, u32[]{:S(2)}) %collective-permute-start.8) | collective-permute-done | bytes 589856 | tf_op jit(solution)/shard_map/ppermute | solution.py:515
  154.4 2.7 %collective-permute-done.9.rest_3_ = f32[72,2048]{1,0:T(8,128)S(1)} collective-permute-done((f32[72,2048]{1,0:T(8,128)S(1)}, f32[72,2048]{1,0:T(8,128)S(1)}, u32[]{:S(2)}, u32[]{:S(2)}) %collective-permute-start.9) | collective-permute-done | bytes 589856 | tf_op jit(solution)/shard_map/ppermute | solution.py:515
  157.1 5.4 %first_moment.1 = (f32[192,2688]{1,0:T(8,128)}, f32[11,192,128]{2,1,0:T(8,128)}) custom-call(f32[192,2688]{1,0:T(8,128)S(1)} %copy-done, bf16[384,576]{1,0:T(8,128)(2,1)S(1)} %get-tuple-element.33.take, f32[72,2048]{1,0:T(8,128)S(1)} %get-tuple-element.45.rest_0_, f32[72,2048]{1,0:T(8,128)S(1)} %collective-permute-done.7.rest_1_, ...), custom_call_target="tpu_custom_call" | custom-call | bytes 11534336 | tf_op jit(solution)/shard_map/first_moment/pallas_call | solution.py:48
  162.4 0.7 all-to-all-done.1
  163.1 7.7 %weight_update.1 = (f32[192,2688]{1,0:T(8,128)}, f32[192,2688]{1,0:T(8,128)}, f32[192,2688]{1,0:T(8,128)}) custom-call(s32[1,21]{1,0:T(1,128)S(1)} %get-tuple-element.31.take, f32[2]{0:T(128)S(1)} %pad_maximum_fusion.fixes, f32[32,288,128]{2,1,0:T(8,128)} %bitcast.7.recv, f32[192,2688]{1,0:T(8,128)} %get-tuple-element.28.first, ...), custom_call_target="tpu_custom_call" | custom-call | bytes 16777216 | tf_op jit(solution)/shard_map/weight_update/pallas_call | solution.py:48
  (19 shorter events, 0.2 us)
Async XLA Ops:
  1.4 0.7 copy-start.2
  6.6 7.7 %copy-start.1 = (s32[8,192]{1,0:T(8,128)S(1)}, s32[8,192]{1,0:T(8,128)}, u32[]{:S(2)}) copy-start(s32[8,192]{1,0:T(8,128)} %new.1) | copy-start | bytes 18436
  6.6 7.8 %copy-start.3 = (s32[8,192]{1,0:T(8,128)S(1)}, s32[8,192]{1,0:T(8,128)}, u32[]{:S(2)}) copy-start(s32[8,192]{1,0:T(8,128)} %old.1) | copy-start | bytes 18436
  6.6 78.6 %all-to-all-start = ((f32[16,2,288,128]{3,2,1,0:T(8,128)}), f32[16,2,288,128]{3,2,1,0:T(8,128)}, u32[]{:S(2)}, u32[]{:S(2)}) async-start(f32[16,2,288,128]{3,2,1,0:T(8,128)} %bitcast.11), calls=%async_computation | async-start | bytes 9437184 | tf_op jit(solution)/shard_map/all_to_all | solution.py:521
  21.7 7.8 %collective-permute-start = (f32[72,2048]{1,0:T(8,128)S(1)}, f32[72,2048]{1,0:T(8,128)S(1)}, u32[]{:S(2)}, u32[]{:S(2)}) collective-permute-start(f32[72,2048]{1,0:T(8,128)S(1)} %get-tuple-element.36), channel_id=1, source_target_pairs={{0,16},{16,0},{32,48},{48,32},{64,80},{80,64},{96,112},{112,96},{1... | collective-permute-start | bytes 1769480 | tf_op jit(solution)/shard_map/ppermute | solution.py:515
  22.7 17.5 %collective-permute-start.1 = (f32[72,2048]{1,0:T(8,128)S(1)}, f32[72,2048]{1,0:T(8,128)S(1)}, u32[]{:S(2)}, u32[]{:S(2)}) collective-permute-start(f32[72,2048]{1,0:T(8,128)S(1)} %get-tuple-element.37), channel_id=1, source_target_pairs={{0,32},{16,48},{32,64},{48,80},{64,96},{80,112},{96,0},{112,16},{1... | collective-permute-start | bytes 1769480 | tf_op jit(solution)/shard_map/ppermute | solution.py:515
  24.4 18.0 %collective-permute-start.2 = (f32[72,2048]{1,0:T(8,128)S(1)}, f32[72,2048]{1,0:T(8,128)S(1)}, u32[]{:S(2)}, u32[]{:S(2)}) collective-permute-start(f32[72,2048]{1,0:T(8,128)S(1)} %get-tuple-element.38), channel_id=1, source_target_pairs={{0,96},{16,112},{32,0},{48,16},{64,32},{80,48},{96,64},{112,80},{1... | collective-permute-start | bytes 1769480 | tf_op jit(solution)/shard_map/ppermute | solution.py:515
  26.5 26.6 %collective-permute-start.3 = (f32[72,2048]{1,0:T(8,128)S(1)}, f32[72,2048]{1,0:T(8,128)S(1)}, u32[]{:S(2)}, u32[]{:S(2)}) collective-permute-start(f32[72,2048]{1,0:T(8,128)S(1)} %get-tuple-element.39), channel_id=1, source_target_pairs={{0,48},{16,32},{32,80},{48,64},{64,112},{80,96},{96,16},{112,0},{1... | collective-permute-start | bytes 1769480 | tf_op jit(solution)/shard_map/ppermute | solution.py:515
  26.5 26.7 %collective-permute-start.4 = (f32[72,2048]{1,0:T(8,128)S(1)}, f32[72,2048]{1,0:T(8,128)S(1)}, u32[]{:S(2)}, u32[]{:S(2)}) collective-permute-start(f32[72,2048]{1,0:T(8,128)S(1)} %get-tuple-element.40), channel_id=1, source_target_pairs={{0,112},{16,96},{32,16},{48,0},{64,48},{80,32},{96,80},{112,64},{1... | collective-permute-start | bytes 1769480 | tf_op jit(solution)/shard_map/ppermute | solution.py:515
  29.5 36.9 %collective-permute-start.5 = (f32[72,2048]{1,0:T(8,128)S(1)}, f32[72,2048]{1,0:T(8,128)S(1)}, u32[]{:S(2)}, u32[]{:S(2)}) collective-permute-start(f32[72,2048]{1,0:T(8,128)S(1)} %get-tuple-element.41), channel_id=1, source_target_pairs={{0,64},{16,80},{32,96},{48,112},{64,0},{80,16},{96,32},{112,48},{1... | collective-permute-start | bytes 1769480 | tf_op jit(solution)/shard_map/ppermute | solution.py:515
  40.2 39.0 %collective-permute-start.6 = (f32[72,2048]{1,0:T(8,128)S(1)}, f32[72,2048]{1,0:T(8,128)S(1)}, u32[]{:S(2)}, u32[]{:S(2)}) collective-permute-start(f32[72,2048]{1,0:T(8,128)S(1)} %get-tuple-element.42), channel_id=1, source_target_pairs={{0,80},{16,64},{32,112},{48,96},{64,16},{80,0},{96,48},{112,32},{1... | collective-permute-start | bytes 1769480 | tf_op jit(solution)/shard_map/ppermute | solution.py:515
  85.2 78.0 %all-to-all-start.1 = ((f32[16,2,288,128]{3,2,1,0:T(8,128)}), f32[16,2,288,128]{3,2,1,0:T(8,128)}, u32[]{:S(2)}, u32[]{:S(2)}) async-start(f32[16,2,288,128]{3,2,1,0:T(8,128)} %bitcast.10), calls=%async_computation.1 | async-start | bytes 9437184 | tf_op jit(solution)/shard_map/all_to_all | solution.py:521
  92.3 64.8 %copy-start = (f32[192,2688]{1,0:T(8,128)S(1)}, f32[192,2688]{1,0:T(8,128)}, u32[]{:S(2)}) copy-start(f32[192,2688]{1,0:T(8,128)} %gradient.3) | copy-start | bytes 6193156
  99.2 17.0 %collective-permute-start.10 = (f32[72,2048]{1,0:T(8,128)S(1)}, f32[72,2048]{1,0:T(8,128)S(1)}, u32[]{:S(2)}, u32[]{:S(2)}) collective-permute-start(f32[72,2048]{1,0:T(8,128)S(1)} %get-tuple-element.49), channel_id=1, source_target_pairs={{0,48},{16,32},{32,80},{48,64},{64,112},{80,96},{96,16},{112,0},{1... | collective-permute-start | bytes 1769480 | tf_op jit(solution)/shard_map/ppermute | solution.py:515
  100.0 16.1 %collective-permute-start.11 = (f32[72,2048]{1,0:T(8,128)S(1)}, f32[72,2048]{1,0:T(8,128)S(1)}, u32[]{:S(2)}, u32[]{:S(2)}) collective-permute-start(f32[72,2048]{1,0:T(8,128)S(1)} %get-tuple-element.50), channel_id=1, source_target_pairs={{0,112},{16,96},{32,16},{48,0},{64,48},{80,32},{96,80},{112,64},{1... | collective-permute-start | bytes 1769480 | tf_op jit(solution)/shard_map/ppermute | solution.py:515
  102.2 42.8 %collective-permute-start.12 = (f32[72,2048]{1,0:T(8,128)S(1)}, f32[72,2048]{1,0:T(8,128)S(1)}, u32[]{:S(2)}, u32[]{:S(2)}) collective-permute-start(f32[72,2048]{1,0:T(8,128)S(1)} %get-tuple-element.51), channel_id=1, source_target_pairs={{0,64},{16,80},{32,96},{48,112},{64,0},{80,16},{96,32},{112,48},{1... | collective-permute-start | bytes 1769480 | tf_op jit(solution)/shard_map/ppermute | solution.py:515
  102.9 42.1 %collective-permute-start.13 = (f32[72,2048]{1,0:T(8,128)S(1)}, f32[72,2048]{1,0:T(8,128)S(1)}, u32[]{:S(2)}, u32[]{:S(2)}) collective-permute-start(f32[72,2048]{1,0:T(8,128)S(1)} %get-tuple-element.52), channel_id=1, source_target_pairs={{0,80},{16,64},{32,112},{48,96},{64,16},{80,0},{96,48},{112,32},{1... | collective-permute-start | bytes 1769480 | tf_op jit(solution)/shard_map/ppermute | solution.py:515
  105.7 39.3 %collective-permute-start.7 = (f32[72,2048]{1,0:T(8,128)S(1)}, f32[72,2048]{1,0:T(8,128)S(1)}, u32[]{:S(2)}, u32[]{:S(2)}) collective-permute-start(f32[72,2048]{1,0:T(8,128)S(1)} %get-tuple-element.46), channel_id=1, source_target_pairs={{0,16},{16,0},{32,48},{48,32},{64,80},{80,64},{96,112},{112,96},{1... | collective-permute-start | bytes 1769480 | tf_op jit(solution)/shard_map/ppermute | solution.py:515
  116.2 38.2 %collective-permute-start.8 = (f32[72,2048]{1,0:T(8,128)S(1)}, f32[72,2048]{1,0:T(8,128)S(1)}, u32[]{:S(2)}, u32[]{:S(2)}) collective-permute-start(f32[72,2048]{1,0:T(8,128)S(1)} %get-tuple-element.47), channel_id=1, source_target_pairs={{0,32},{16,48},{32,64},{48,80},{64,96},{80,112},{96,0},{112,16},{1... | collective-permute-start | bytes 1769480 | tf_op jit(solution)/shard_map/ppermute | solution.py:515
  116.2 40.9 %collective-permute-start.9 = (f32[72,2048]{1,0:T(8,128)S(1)}, f32[72,2048]{1,0:T(8,128)S(1)}, u32[]{:S(2)}, u32[]{:S(2)}) collective-permute-start(f32[72,2048]{1,0:T(8,128)S(1)} %get-tuple-element.48), channel_id=1, source_target_pairs={{0,96},{16,112},{32,0},{48,16},{64,32},{80,48},{96,64},{112,80},{1... | collective-permute-start | bytes 1769480 | tf_op jit(solution)/shard_map/ppermute | solution.py:515

commit v3 on v2

--- a/solution.py
+++ b/solution.py
@@ -21,8 +21,9 @@
 BLOCK = ROWS + FOLD
 TILES = 32
 WIDE = TILES // 2 * UNIT
+MAIN = 32
+REST = ROOM - MAIN
 MESSAGE = 2 * ROOM
-STACK = DP * MESSAGE
 PAIRS = TILES - UNITS
 CHUNK = 4
 VMEM_LIMIT = 24 * 1024 * 1024
@@ -33,7 +34,7 @@
 learn_rate = 0.001
 decay_rate = 0.1
 
-MOVES = [(0, 0), (0, 1), (1, 0), (3, 0), (1, 1), (3, 1), (2, 0), (2, 1)]
+MOVES = [(0, 0), (0, 1), (2, 0), (2, 1), (1, 0), (3, 0), (1, 1), (3, 1)]
 HBM = pl.BlockSpec(memory_space=pltpu.HBM)
 ANY = pl.BlockSpec(memory_space=pl.ANY)
 VMEM = pl.BlockSpec(memory_space=pltpu.VMEM)
@@ -59,19 +60,25 @@
     )(*args)
 
 
-def row_plan_kernel(place, old, new, new_turned, pack, take):
+def turned(row):
+    n = row.shape[1]
+    here = lax.broadcasted_iota(jnp.int32, (n, n), 0)
+    there = lax.broadcasted_iota(jnp.int32, (n, n), 1)
+    return jnp.sum(jnp.where(here == there, row, 0), axis=1, keepdims=True)
+
+
+def row_plan_kernel(place, old, new, pack, pack_rest, take, take_rest):
     d = place[0]
     z, c = d // 2, d % 2
     old_mine = old[pl.ds(d, 1), :]
-    lane = lax.broadcasted_iota(jnp.int32, (ROWS, DP), 1)
-    new_mine = jnp.sum(jnp.where(lane == d, new_turned[...], 0), axis=1, keepdims=True)
+    new_mine = turned(new[pl.ds(d, 1), :])
     here = lax.broadcasted_iota(jnp.int32, (ROWS, ROWS), 0)
     there = lax.broadcasted_iota(jnp.int32, (ROWS, ROWS), 1)
     earlier = (here < there).astype(jnp.float32).astype(jnp.bfloat16)
 
     goes, comes = [], []
     for s in range(DP):
-        hit = (new_turned[:, s : s + 1] == old_mine).astype(jnp.float32)
+        hit = (turned(new[s : s + 1, :]) == old_mine).astype(jnp.float32)
         goes.append(jnp.max(hit, axis=0, keepdims=True))
         hit = (new_mine == old[s : s + 1, :]).astype(jnp.float32)
         comes.append(jnp.max(hit, axis=0, keepdims=True))
@@ -80,54 +87,68 @@
     both = both.astype(jnp.int32)
     before = before.astype(jnp.int32)
 
-    def first_slot(dz, dc):
+    def message(dz, dc):
         at = 0
         for k, move in enumerate(MOVES):
-            at = jnp.where((dz == move[0]) & (dc == move[1]), k * MESSAGE, at)
+            at = jnp.where((dz == move[0]) & (dc == move[1]), k, at)
         return at
 
-    slot = jnp.zeros((1, ROWS), jnp.int32)
-    origin = jnp.zeros((ROWS, ROWS), jnp.int32)
+    goes = jnp.zeros((1, ROWS), jnp.int32)
+    comes = jnp.zeros((ROWS, ROWS), jnp.int32)
     for s in range(DP):
         core = (s % 2 + c) % 2
-        to = first_slot((s // 2 - z + 4) % 4, core)
-        slot = slot + both[s : s + 1] * (to + before[s : s + 1])
-        source = first_slot((z - s // 2 + 4) % 4, core)
+        to = message((s // 2 - z + 4) % 4, core) * 64
+        goes = goes + both[s : s + 1] * (to + before[s : s + 1])
+        source = message((z - s // 2 + 4) % 4, core) * 64
         value = source + before[DP + s : DP + s + 1]
-        origin = origin + jnp.where(new_mine == old[s : s + 1, :], value, 0)
-    origin = jnp.sum(origin, axis=1, keepdims=True)
+        comes = comes + jnp.where(new_mine == old[s : s + 1, :], value, 0)
+    comes = jnp.sum(comes, axis=1, keepdims=True)
+
+    def places(code):
+        k, rank = code >> 6, code & 63
+        main = jnp.where(rank < MAIN, k * MAIN + rank, -1)
+        return main, jnp.where(rank < MAIN, -1, k * 2 * REST + rank - MAIN)
 
     def onehot(equal):
         return equal.astype(jnp.float32).astype(jnp.bfloat16)
 
-    index = lax.broadcasted_iota(jnp.int32, (STACK, ROWS), 0)
-    pack[0] = onehot(index == slot)
-    pack[1] = onehot(index == slot + ROOM)
-    index = lax.broadcasted_iota(jnp.int32, (ROWS, STACK), 1)
-    take[:ROWS] = onehot(index == origin)
-    take[ROWS:] = onehot(index == origin + ROOM)
+    def index(shape, axis):
+        return lax.broadcasted_iota(jnp.int32, shape, axis)
+
+    main, rest = places(goes)
+    pack[...] = onehot(index((DP * MAIN, ROWS), 0) == main)
+    rest = jnp.concatenate([rest, jnp.where(rest < 0, rest, rest + REST)], axis=1)
+    pack_rest[...] = onehot(index((DP * 2 * REST, 2 * ROWS), 0) == rest)
+    main, rest = places(comes)
+    take[...] = onehot(index((ROWS, DP * MAIN), 1) == main)
+    rest = jnp.concatenate([rest, jnp.where(rest < 0, rest, rest + REST)], axis=0)
+    take_rest[...] = onehot(index((2 * ROWS, DP * 2 * REST), 1) == rest)
 
 
 def row_plan(old_rows, new_rows):
     place = lax.axis_index("dp").astype(jnp.int32).reshape(1)
-    pack = jax.ShapeDtypeStruct((2, STACK, ROWS), jnp.bfloat16)
-    take = jax.ShapeDtypeStruct((2 * ROWS, STACK), jnp.bfloat16)
-    return call(
+    shapes = [
+        (DP * MAIN, ROWS),
+        (DP * 2 * REST, 2 * ROWS),
+        (ROWS, DP * MAIN),
+        (2 * ROWS, DP * 2 * REST),
+    ]
+    plan = call(
         row_plan_kernel,
         "row_plan",
-        [SMEM, VMEM, VMEM, VMEM],
-        [VMEM] * 2,
-        [pack, take],
+        [SMEM, VMEM, VMEM],
+        [VMEM] * 4,
+        [jax.ShapeDtypeStruct(shape, jnp.bfloat16) for shape in shapes],
         [],
         1,
         place,
         old_rows,
         new_rows,
-        new_rows.T,
-    )
-
-
-def unit_plan_kernel(place, units, turned, send, take):
+    )
+    return plan[:2], plan[2:]
+
+
+def unit_plan_kernel(place, units, send, take):
     m = place[0]
     lane = lax.broadcasted_iota(jnp.int32, (1, UNIT), 1)
     line = lax.broadcasted_iota(jnp.int32, (UNITS, 1), 0)
@@ -136,7 +157,7 @@
     to_row = jnp.zeros((UNITS, UNIT), jnp.int32)
     to_column = jnp.zeros((UNITS, UNITS), jnp.int32)
     for t in range(1, MP):
-        to_row = to_row + jnp.where(turned[:, t : t + 1] == m * UNITS + lane, t, 0)
+        to_row = to_row + jnp.where(turned(units[t : t + 1, :]) == m * UNITS + lane, t, 0)
         to_column = to_column + jnp.where(units[t : t + 1, :] == m * UNITS + line, t, 0)
     to_row = jnp.sum(to_row, axis=0, keepdims=True)
     to_column = jnp.sum(to_column, axis=1, keepdims=True)
@@ -144,8 +165,7 @@
     send[...] = to_row * PAIR + rank
 
     row = units[pl.ds(m, 1), :]
-    column = lax.broadcasted_iota(jnp.int32, (UNITS, MP), 1) == m
-    column = jnp.sum(jnp.where(column, turned[...], 0), axis=1, keepdims=True)
+    column = turned(row)
     from_row, from_column = jnp.zeros_like(row), jnp.zeros_like(column)
     for t in range(1, MP):
         from_row = from_row + (row >= t * UNITS).astype(jnp.int32)
@@ -159,28 +179,30 @@
     return call(
         unit_plan_kernel,
         "unit_plan",
-        [SMEM, VMEM, VMEM],
+        [SMEM, VMEM],
         [VMEM] * 2,
         [jax.ShapeDtypeStruct((1, n), jnp.int32) for n in (UNIT, UNITS)],
         [],
         1,
         place,
         new_units,
-        new_units.T,
-    )
+    )
+
+
+TERMS = 3
 
 
 def terms(values):
-    high = values.astype(jnp.bfloat16)
-    rest = values - high.astype(jnp.float32)
-    middle = rest.astype(jnp.bfloat16)
-    low = (rest - middle.astype(jnp.float32)).astype(jnp.bfloat16)
-    return high, middle, low
+    split = []
+    for _ in range(TERMS):
+        split.append(values.astype(jnp.bfloat16))
+        values = values - split[-1].astype(jnp.float32)
+    return split
 
 
 def select_rows(onehot, split):
     dot = functools.partial(jnp.dot, preferred_element_type=jnp.float32)
-    return (dot(onehot, split[0]) + dot(onehot, split[1])) + dot(onehot, split[2])
+    return functools.reduce(lambda a, b: a + b, [dot(onehot, term) for term in split])
 
 
 def columns_of(u):
@@ -208,23 +230,38 @@
     return jnp.concatenate([y, swapped(y)], axis=0)
 
 
-def pack_rows(tile, pack, outs):
+def joined(values, axis):
+    return jnp.concatenate(values, axis=axis)
+
+
+def pack_rows(tile, pack, pack_rest, outs):
+    width = CHUNK * UNIT
     for i in range(0, TILES // 2, CHUNK):
-        left = jnp.concatenate([tile(n) for n in range(i, i + CHUNK)], axis=1)
-        right = jnp.concatenate([tile(TILES // 2 + n) for n in range(i, i + CHUNK)], axis=1)
-        packed = select_rows(pack[0], terms(left)) + select_rows(pack[1], terms(right))
+        left = terms(joined([tile(n) for n in range(i, i + CHUNK)], 1))
+        right = terms(joined([tile(TILES // 2 + n) for n in range(i, i + CHUNK)], 1))
+        main = select_rows(pack[...], [joined(both, 1) for both in zip(left, right)])
+        rest = select_rows(pack_rest[...], [joined(both, 0) for both in zip(left, right)])
+        columns = slice(i * UNIT, (i + CHUNK) * UNIT)
         for k, out in enumerate(outs):
-            out[:, i * UNIT : (i + CHUNK) * UNIT] = packed[k * MESSAGE : (k + 1) * MESSAGE]
-
-
-def take_rows(parts, take, put):
+            rows = slice(k * MAIN, (k + 1) * MAIN)
+            out[:MAIN, columns] = main[rows, :width]
+            out[MAIN : 2 * MAIN, columns] = main[rows, width:]
+            out[2 * MAIN :, columns] = rest[k * 2 * REST : (k + 1) * 2 * REST]
+
+
+def take_rows(parts, take, take_rest, put):
+    width = CHUNK * UNIT
     for i in range(0, TILES // 2, CHUNK):
         columns = slice(i * UNIT, (i + CHUNK) * UNIT)
-        values = jnp.concatenate([p[:, columns] for p in parts], axis=0)
-        picked = select_rows(take[...], terms(values))
+        left = joined([p[:MAIN, columns] for p in parts], 0)
+        right = joined([p[MAIN : 2 * MAIN, columns] for p in parts], 0)
+        rest = joined([p[2 * MAIN :, columns] for p in parts], 0)
+        main = select_rows(take[...], terms(joined([left, right], 1)))
+        rest = select_rows(take_rest[...], terms(rest))
+        left, right = main[:, :width] + rest[:ROWS], main[:, width:] + rest[ROWS:]
         for k in range(CHUNK):
-            put(i + k, picked[:ROWS, columns_of(k)])
-            put(TILES // 2 + i + k, picked[ROWS:, columns_of(k)])
+            put(i + k, left[:, columns_of(k)])
+            put(TILES // 2 + i + k, right[:, columns_of(k)])
 
 
 class Copies:
@@ -243,26 +280,32 @@
 
 
 PARTS = 3
+SPAN = UNITS // PARTS
+
+
+def span_of(i):
+    return slice(i * SPAN * UNIT, (i + 1) * SPAN * UNIT)
 
 
 class Loads:
     def __init__(self, sems):
         self.sems, self.arrays = sems, []
 
-    def start(self, source, target):
-        parts = []
+    def start(self, *pairs):
+        parts = [[] for _ in pairs]
         for i in range(PARTS):
-            columns = slice(i * COLS // PARTS, (i + 1) * COLS // PARTS)
-            sem = self.sems.at[len(self.arrays) * PARTS + i]
-            parts.append(
-                pltpu.make_async_copy(source.at[:, columns], target.at[:, columns], sem)
-            )
-            parts[-1].start()
-        self.arrays.append(parts)
+            for k, (source, target) in enumerate(pairs):
+                sem = self.sems.at[(len(self.arrays) + k) * PARTS + i]
+                copy = pltpu.make_async_copy(
+                    source.at[:, span_of(i)], target.at[:, span_of(i)], sem
+                )
+                copy.start()
+                parts[k].append(copy)
+        self.arrays += parts
 
     def wait(self, array, unit):
         parts = self.arrays[array]
-        for i in range(unit * PARTS // UNITS + 1):
+        for i in range(unit // SPAN + 1):
             if parts[i] is not None:
                 parts[i].wait()
                 parts[i] = None
@@ -282,12 +325,10 @@
 
 def unit_pack_kernel(send, whole, half, out, whole_here, half_here, folds, loads, stores):
     loads, stores = Loads(loads), Copies(stores)
-    loads.start(whole, whole_here)
-    loads.start(half, half_here)
+    loads.start((whole, whole_here), (half, half_here))
     for u in range(UNITS):
         loads.wait(0, u)
         stores.start(whole_here.at[:, columns_of(u)], out.at[send[0, u], pl.ds(0, ROWS)])
-    for u in range(UNITS):
         loads.wait(1, u)
         folds[u] = folded(half_here[:, columns_of(u)], True)
         stores.start(folds.at[u], out.at[send[0, u], pl.ds(ROWS, FOLD)])
@@ -309,11 +350,10 @@
     )
 
 
-def row_pack_kernel(pack, whole, half, *rest):
+def row_pack_kernel(pack, pack_rest, whole, half, *rest):
     outs, (whole_here, half_here, loads) = rest[:DP], rest[DP:]
     loads = Loads(loads)
-    loads.start(whole, whole_here)
-    loads.start(half, half_here)
+    loads.start((whole, whole_here), (half, half_here))
 
     def unit(k, u):
         u = min(u, UNITS - 1)
@@ -326,25 +366,25 @@
         u = 2 * (n - UNITS)
         return jnp.where(left_lanes(ROWS), unit(1, u), swapped(unit(1, u + 1)))
 
-    pack_rows(tile, pack, outs)
+    pack_rows(tile, pack, pack_rest, outs)
 
 
 def row_pack(whole, half, pack):
     return call(
         row_pack_kernel,
         "row_pack",
-        [VMEM, HBM, HBM],
+        [VMEM, VMEM, HBM, HBM],
         [VMEM] * DP,
         MESSAGES,
         [ARRAY, ARRAY, dma(2 * PARTS)],
         9,
-        pack,
+        *pack,
         whole,
         half,
     )
 
 
-def unit_row_pack_kernel(take, pack, recv, *rest):
+def unit_row_pack_kernel(take, pack, pack_rest, recv, *rest):
     outs, (here, sems) = rest[:DP], rest[DP:]
     copies, arriving = Copies(sems), {}
     for i in range(0, TILES // 2, CHUNK):
@@ -365,25 +405,25 @@
         b = unfolded(unit(min(u + 1, UNITS - 1))[ROWS:], True)
         return jnp.where(left_lanes(ROWS), a, b)
 
-    pack_rows(tile, pack, outs)
+    pack_rows(tile, pack, pack_rest, outs)
 
 
 def unit_row_pack(recv, take, pack):
     return call(
         unit_row_pack_kernel,
         "unit_row_pack",
-        [SMEM, VMEM, ANY],
+        [SMEM, VMEM, VMEM, ANY],
         [VMEM] * DP,
         MESSAGES,
         [pltpu.VMEM((UNITS, BLOCK, UNIT), jnp.float32), dma(UNITS)],
         10,
         take,
-        pack,
+        *pack,
         recv,
     )
 
 
-def row_unit_pack_kernel(send, take, *rest):
+def row_unit_pack_kernel(send, take, take_rest, *rest):
     parts, (out, held, folds, sems) = rest[:DP], rest[DP:]
     copies = Copies(sems)
 
@@ -397,7 +437,7 @@
                 folds[u] = folded(tile, upper)
                 copies.start(folds.at[u], out.at[send[0, u], pl.ds(ROWS, FOLD)])
 
-    take_rows(parts, take, put)
+    take_rows(parts, take, take_rest, put)
     copies.wait()
 
 
@@ -405,32 +445,35 @@
     return call(
         row_unit_pack_kernel,
         "row_unit_pack",
-        [SMEM] + [VMEM] * (1 + DP),
+        [SMEM] + [VMEM] * (2 + DP),
         SLOT_SPEC,
         SLOT_ARRAY,
         [HELD, FOLDS, dma(2 * UNITS)],
         10,
         send,
-        take,
+        *take,
         *parts,
     )
 
 
-def first_kernel(gradient, take, *rest):
+def first_kernel(gradient, take, take_rest, *rest):
     parts, (first, half, held, half_held, sems) = rest[:DP], rest[DP:]
-    copies = Copies(sems)
+    copies, done = Copies(sems), set()
 
     def put(n, tile):
         if n < UNITS:
             columns = columns_of(n)
             moment = beta_one * tile + (1.0 - beta_one) * gradient[:, columns]
             held[:, columns] = moment
-            copies.start(held.at[:, columns], first.at[:, columns])
+            done.add(n)
+            span = n // SPAN
+            if all(u in done for u in range(span * SPAN, (span + 1) * SPAN)):
+                copies.start(held.at[:, span_of(span)], first.at[:, span_of(span)])
         else:
             half_held[n - UNITS] = tile
             copies.start(half_held.at[n - UNITS], half.at[n - UNITS])
 
-    take_rows(parts, take, put)
+    take_rows(parts, take, take_rest, put)
     copies.wait()
 
 
@@ -438,13 +481,13 @@
     return call(
         first_kernel,
         "first_moment",
-        [VMEM] * (2 + DP),
+        [VMEM] * (3 + DP),
         [HBM, HBM],
         [pltpu.HBM((ROWS, COLS), jnp.float32), pltpu.HBM((PAIRS, ROWS, UNIT), jnp.float32)],
         [ARRAY, pltpu.VMEM((PAIRS, ROWS, UNIT), jnp.float32), dma(TILES)],
         11,
         gradient,
-        take,
+        *take,
         *parts,
     )
 
@@ -454,8 +497,7 @@
     here, first_here, half_here, gradient_here, whole_loads, unit_loads, stores = rest
     loads, whole, stores = Copies(unit_loads), Loads(whole_loads), Copies(stores)
     arrivals = [loads.start(recv.at[take[0, u]], here.at[u]) for u in range(UNITS // 3)]
-    whole.start(gradient, gradient_here)
-    whole.start(first, first_here)
+    whole.start((gradient, gradient_here), (first, first_here))
     halves = loads.start(half, half_here)
     arrivals += [loads.start(recv.at[take[0, u]], here.at[u]) for u in range(UNITS // 3, UNITS)]
     for u in range(UNITS):
@@ -477,7 +519,9 @@
         update = first_here[:, columns] / fixes[0] / root + decay_rate * weight
         for held, out, value in zip(helds, outs, (weight - learn_rate * update, second, update)):
             held[:, columns] = value
-            stores.start(held.at[:, columns], out.at[:, columns])
+            if u % SPAN == SPAN - 1:
+                span = span_of(u // SPAN)
+                stores.start(held.at[:, span], out.at[:, span])
     stores.wait()
 
 
@@ -496,7 +540,7 @@
             ARRAY,
             dma(2 * PARTS),
             dma(UNITS + 1),
-            dma(3 * UNITS),
+            dma(3 * PARTS),
         ],
         16,
         take,

time: 171 us -> 167 us (0.977)
  the two profiles are of different devices: /device:TPU:1 before, /device:TPU:0 now
where the time goes in v3:
time: 167 us; the launch traced here: 166 us
  waiting for transfers between devices  99.1 us (59%)
  Pallas kernels  33.3 us (20%)
  starting transfers between devices  31.3 us (19%)
  between operations  1.68 us (1%)
    ppermute x14, waiting for transfers between devices, swap_rows(): arrived.append(lax.ppermute(part, 'dp', pairs) if dz or dc else part)  89.7 us
    pallas_call x8, Pallas kernels, call(): pl.pallas_call(kernel, out_shape=out_shape, in_specs=ins, out_specs=outs,...  33.3 us
    ppermute x14, starting transfers between devices, swap_rows(): arrived.append(lax.ppermute(part, 'dp', pairs) if dz or dc else part)  19 us
    all_to_all x2, starting transfers between devices, swap_units(): lax.all_to_all(packed, 'mp', split_axis=0, concat_axis=0, tiled=True)  12.3 us
    all_to_all x2, waiting for transfers between devices, swap_units(): lax.all_to_all(packed, 'mp', split_axis=0, concat_axis=0, tiled=True)  9.39 us
  transfers between devices with their start and end apart: 16, of which 11 were waited for; matrix products, arithmetic and copies ran while one was open for 0% of the time, Pallas kernels for 13%

profile of v3, /device:TPU:0, one launch (start us, length us, event | category | flops | bytes accessed | tf_op | source)
XLA Modules:
  0.0 166.1 jit_solution(1359731193337469857)
XLA Ops:
  0.6 0.7 copy-done.1
  1.3 0.2 unit_plan.1
  1.5 4.2 %unit_pack.1 = f32[32,288,128]{2,1,0:T(8,128)} custom-call(s32[1,128]{1,0:T(1,128)S(1)} %get-tuple-element.34.send, f32[192,2688]{1,0:T(8,128)} %whole.2, f32[192,2688]{1,0:T(8,128)} %half.3), custom_call_target="tpu_custom_call" | custom-call | bytes 9437184 | tf_op jit(solution)/shard_map/unit_pack/pallas_call | solution.py:49
  5.8 7.2 %all-to-all-start = ((f32[16,2,288,128]{3,2,1,0:T(8,128)}), f32[16,2,288,128]{3,2,1,0:T(8,128)}, u32[]{:S(2)}, u32[]{:S(2)}) async-start(f32[16,2,288,128]{3,2,1,0:T(8,128)} %bitcast.7), calls=%async_computation | async-start | bytes 9437184 | tf_op jit(solution)/shard_map/all_to_all | solution.py:565
  13.0 1.3 row_plan.1
  14.2 5.4 %row_pack.1 = (f32[72,2048]{1,0:T(8,128)S(1)}, f32[72,2048]{1,0:T(8,128)S(1)}, f32[72,2048]{1,0:T(8,128)S(1)}, f32[72,2048]{1,0:T(8,128)S(1)}, f32[72,2048]{1,0:...) custom-call(bf16[256,192]{1,0:T(8,128)(2,1)S(1)} %get-tuple-element.37.pack, ...), custom_call_target="tpu_custom_call" | custom-call | bytes 9437184 | tf_op jit(solution)/shard_map/row_pack/pallas_call | solution.py:49
  19.7 0.1 collective-permute-start
  19.8 4.0 %collective-permute-start.1 = (f32[72,2048]{1,0:T(8,128)S(1)}, f32[72,2048]{1,0:T(8,128)S(1)}, u32[]{:S(2)}, u32[]{:S(2)}) collective-permute-start(f32[72,2048]{1,0:T(8,128)S(1)} %get-tuple-element.41), channel_id=1, source_target_pairs={{0,64},{16,80},{32,96},{48,112},{64,0},{80,16},{96,32},{112,48},{1... | collective-permute-start | bytes 1769480 | tf_op jit(solution)/shard_map/ppermute | solution.py:559
  23.8 1.3 collective-permute-start.3
  25.1 2.1 %collective-permute-start.4 = (f32[72,2048]{1,0:T(8,128)S(1)}, f32[72,2048]{1,0:T(8,128)S(1)}, u32[]{:S(2)}, u32[]{:S(2)}) collective-permute-start(f32[72,2048]{1,0:T(8,128)S(1)} %get-tuple-element.44), channel_id=1, source_target_pairs={{0,96},{16,112},{32,0},{48,16},{64,32},{80,48},{96,64},{112,80},{1... | collective-permute-start | bytes 1769480 | tf_op jit(solution)/shard_map/ppermute | solution.py:559
  27.2 10.8 %collective-permute-done.1.rest_2_ = f32[72,2048]{1,0:T(8,128)S(1)} collective-permute-done((f32[72,2048]{1,0:T(8,128)S(1)}, f32[72,2048]{1,0:T(8,128)S(1)}, u32[]{:S(2)}, u32[]{:S(2)}) %collective-permute-start.1) | collective-permute-done | bytes 589856 | tf_op jit(solution)/shard_map/ppermute | solution.py:559
  38.0 2.4 %collective-permute-start.6 = (f32[72,2048]{1,0:T(8,128)S(1)}, f32[72,2048]{1,0:T(8,128)S(1)}, u32[]{:S(2)}, u32[]{:S(2)}) collective-permute-start(f32[72,2048]{1,0:T(8,128)S(1)} %get-tuple-element.46), channel_id=1, source_target_pairs={{0,112},{16,96},{32,16},{48,0},{64,48},{80,32},{96,80},{112,64},{1... | collective-permute-start | bytes 1769480 | tf_op jit(solution)/shard_map/ppermute | solution.py:559
  40.5 9.6 %collective-permute-done.2.rest_3_ = f32[72,2048]{1,0:T(8,128)S(1)} collective-permute-done((f32[72,2048]{1,0:T(8,128)S(1)}, f32[72,2048]{1,0:T(8,128)S(1)}, u32[]{:S(2)}, u32[]{:S(2)}) %collective-permute-start.2) | collective-permute-done | bytes 589856 | tf_op jit(solution)/shard_map/ppermute | solution.py:559
  50.1 12.8 %collective-permute-done.3.rest_4_ = f32[72,2048]{1,0:T(8,128)S(1)} collective-permute-done((f32[72,2048]{1,0:T(8,128)S(1)}, f32[72,2048]{1,0:T(8,128)S(1)}, u32[]{:S(2)}, u32[]{:S(2)}) %collective-permute-start.3) | collective-permute-done | bytes 589856 | tf_op jit(solution)/shard_map/ppermute | solution.py:559
  63.0 1.2 collective-permute-done.4.rest_5_
  64.2 11.4 %collective-permute-done.5.rest_6_ = f32[72,2048]{1,0:T(8,128)S(1)} collective-permute-done((f32[72,2048]{1,0:T(8,128)S(1)}, f32[72,2048]{1,0:T(8,128)S(1)}, u32[]{:S(2)}, u32[]{:S(2)}) %collective-permute-start.5) | collective-permute-done | bytes 589856 | tf_op jit(solution)/shard_map/ppermute | solution.py:559
  75.5 0.3 collective-permute-done.6.rest_7_
  75.9 4.8 %row_unit_pack.1 = f32[32,288,128]{2,1,0:T(8,128)} custom-call(s32[1,128]{1,0:T(1,128)S(1)} %get-tuple-element.34.send, bf16[192,256]{1,0:T(8,128)(2,1)S(1)} %get-tuple-element.35.take, bf16[384,64]{1,0:T(8,128)(2,1)S(1)} %get-tuple-element.36.take_rest, f32[72,2048]{1,0:T(8,128)S(1)} %get-tuple-element.39.rest_0_, ...), custom_call_target="tpu_custom_call" | custom-call | bytes 10485760 | tf_op jit(solution)/shard_map/row_unit_pack/pallas_call | solution.py:49
  80.7 3.0 %all-to-all-done = f32[16,2,288,128]{3,2,1,0:T(8,128)} async-done(((f32[16,2,288,128]{3,2,1,0:T(8,128)}), f32[16,2,288,128]{3,2,1,0:T(8,128)}, u32[]{:S(2)}, u32[]{:S(2)}) %all-to-all-start) | async-done | bytes 4718624 | tf_op jit(solution)/shard_map/all_to_all | solution.py:565
  83.7 5.1 %all-to-all-start.1 = ((f32[16,2,288,128]{3,2,1,0:T(8,128)}), f32[16,2,288,128]{3,2,1,0:T(8,128)}, u32[]{:S(2)}, u32[]{:S(2)}) async-start(f32[16,2,288,128]{3,2,1,0:T(8,128)} %bitcast.6), calls=%async_computation.1 | async-start | bytes 9437184 | tf_op jit(solution)/shard_map/all_to_all | solution.py:565
  88.8 5.6 %unit_row_pack.1 = (f32[72,2048]{1,0:T(8,128)S(1)}, f32[72,2048]{1,0:T(8,128)S(1)}, f32[72,2048]{1,0:T(8,128)S(1)}, f32[72,2048]{1,0:T(8,128)S(1)}, f32[72,2048]...) custom-call(s32[1,21]{1,0:T(1,128)S(1)} %get-tuple-element.33.take, ...), custom_call_target="tpu_custom_call" | custom-call | bytes 10485760 | tf_op jit(solution)/shard_map/unit_row_pack/pallas_call | solution.py:49
  94.4 2.0 %collective-permute-start.10 = (f32[72,2048]{1,0:T(8,128)S(1)}, f32[72,2048]{1,0:T(8,128)S(1)}, u32[]{:S(2)}, u32[]{:S(2)}) collective-permute-start(f32[72,2048]{1,0:T(8,128)S(1)} %get-tuple-element.53), channel_id=1, source_target_pairs={{0,32},{16,48},{32,64},{48,80},{64,96},{80,112},{96,0},{112,16},{1... | collective-permute-start | bytes 1769480 | tf_op jit(solution)/shard_map/ppermute | solution.py:559
  96.4 2.2 %collective-permute-start.11 = (f32[72,2048]{1,0:T(8,128)S(1)}, f32[72,2048]{1,0:T(8,128)S(1)}, u32[]{:S(2)}, u32[]{:S(2)}) collective-permute-start(f32[72,2048]{1,0:T(8,128)S(1)} %get-tuple-element.54), channel_id=1, source_target_pairs={{0,96},{16,112},{32,0},{48,16},{64,32},{80,48},{96,64},{112,80},{1... | collective-permute-start | bytes 1769480 | tf_op jit(solution)/shard_map/ppermute | solution.py:559
  98.6 3.0 %collective-permute-start.13 = (f32[72,2048]{1,0:T(8,128)S(1)}, f32[72,2048]{1,0:T(8,128)S(1)}, u32[]{:S(2)}, u32[]{:S(2)}) collective-permute-start(f32[72,2048]{1,0:T(8,128)S(1)} %get-tuple-element.56), channel_id=1, source_target_pairs={{0,112},{16,96},{32,16},{48,0},{64,48},{80,32},{96,80},{112,64},{1... | collective-permute-start | bytes 1769480 | tf_op jit(solution)/shard_map/ppermute | solution.py:559
  101.6 11.2 %collective-permute-done.10.rest_4_ = f32[72,2048]{1,0:T(8,128)S(1)} collective-permute-done((f32[72,2048]{1,0:T(8,128)S(1)}, f32[72,2048]{1,0:T(8,128)S(1)}, u32[]{:S(2)}, u32[]{:S(2)}) %collective-permute-start.10) | collective-permute-done | bytes 589856 | tf_op jit(solution)/shard_map/ppermute | solution.py:559
  112.8 1.9 %collective-permute-start.8 = (f32[72,2048]{1,0:T(8,128)S(1)}, f32[72,2048]{1,0:T(8,128)S(1)}, u32[]{:S(2)}, u32[]{:S(2)}) collective-permute-start(f32[72,2048]{1,0:T(8,128)S(1)} %get-tuple-element.51), channel_id=1, source_target_pairs={{0,64},{16,80},{32,96},{48,112},{64,0},{80,16},{96,32},{112,48},{1... | collective-permute-start | bytes 1769480 | tf_op jit(solution)/shard_map/ppermute | solution.py:559
  115.4 0.1 pad_maximum_fusion.fixes
  115.5 7.4 %collective-permute-done.12.rest_6_ = f32[72,2048]{1,0:T(8,128)S(1)} collective-permute-done((f32[72,2048]{1,0:T(8,128)S(1)}, f32[72,2048]{1,0:T(8,128)S(1)}, u32[]{:S(2)}, u32[]{:S(2)}) %collective-permute-start.12) | collective-permute-done | bytes 589856 | tf_op jit(solution)/shard_map/ppermute | solution.py:559
  122.8 24.9 %collective-permute-done.13.rest_7_ = f32[72,2048]{1,0:T(8,128)S(1)} collective-permute-done((f32[72,2048]{1,0:T(8,128)S(1)}, f32[72,2048]{1,0:T(8,128)S(1)}, u32[]{:S(2)}, u32[]{:S(2)}) %collective-permute-start.13) | collective-permute-done | bytes 589856 | tf_op jit(solution)/shard_map/ppermute | solution.py:559
  147.8 4.5 %first_moment.1 = (f32[192,2688]{1,0:T(8,128)}, f32[11,192,128]{2,1,0:T(8,128)}) custom-call(f32[192,2688]{1,0:T(8,128)S(1)} %copy-done, bf16[192,256]{1,0:T(8,128)(2,1)S(1)} %get-tuple-element.35.take, bf16[384,64]{1,0:T(8,128)(2,1)S(1)} %get-tuple-element.36.take_rest, f32[72,2048]{1,0:T(8,128)S(1)} %get-tuple-element.49.rest_0_, ...), custom_call_target="tpu_custom_call" | custom-call | bytes 11534336 | tf_op jit(solution)/shard_map/first_moment/pallas_call | solution.py:49
  152.3 6.4 %all-to-all-done.1 = f32[16,2,288,128]{3,2,1,0:T(8,128)} async-done(((f32[16,2,288,128]{3,2,1,0:T(8,128)}), f32[16,2,288,128]{3,2,1,0:T(8,128)}, u32[]{:S(2)}, u32[]{:S(2)}) %all-to-all-start.1) | async-done | bytes 4718624 | tf_op jit(solution)/shard_map/all_to_all | solution.py:565
  158.7 7.3 %weight_update.1 = (f32[192,2688]{1,0:T(8,128)}, f32[192,2688]{1,0:T(8,128)}, f32[192,2688]{1,0:T(8,128)}) custom-call(s32[1,21]{1,0:T(1,128)S(1)} %get-tuple-element.33.take, f32[2]{0:T(128)S(1)} %pad_maximum_fusion.fixes, f32[32,288,128]{2,1,0:T(8,128)} %bitcast.5.recv, f32[192,2688]{1,0:T(8,128)} %get-tuple-element.30.first, ...), custom_call_target="tpu_custom_call" | custom-call | bytes 16777216 | tf_op jit(solution)/shard_map/weight_update/pallas_call | solution.py:49
  (17 shorter events, 0.1 us)
Async XLA Ops:
  0.6 0.7 copy-start.1
  5.7 7.2 %copy-start.2 = (s32[8,192]{1,0:T(8,128)S(1)}, s32[8,192]{1,0:T(8,128)}, u32[]{:S(2)}) copy-start(s32[8,192]{1,0:T(8,128)} %old.1) | copy-start | bytes 18436
  5.7 7.2 %copy-start.3 = (s32[8,192]{1,0:T(8,128)S(1)}, s32[8,192]{1,0:T(8,128)}, u32[]{:S(2)}) copy-start(s32[8,192]{1,0:T(8,128)} %new.1) | copy-start | bytes 18436
  5.8 77.9 %all-to-all-start = ((f32[16,2,288,128]{3,2,1,0:T(8,128)}), f32[16,2,288,128]{3,2,1,0:T(8,128)}, u32[]{:S(2)}, u32[]{:S(2)}) async-start(f32[16,2,288,128]{3,2,1,0:T(8,128)} %bitcast.7), calls=%async_computation | async-start | bytes 9437184 | tf_op jit(solution)/shard_map/all_to_all | solution.py:565
  19.7 7.5 %collective-permute-start = (f32[72,2048]{1,0:T(8,128)S(1)}, f32[72,2048]{1,0:T(8,128)S(1)}, u32[]{:S(2)}, u32[]{:S(2)}) collective-permute-start(f32[72,2048]{1,0:T(8,128)S(1)} %get-tuple-element.40), channel_id=1, source_target_pairs={{0,16},{16,0},{32,48},{48,32},{64,80},{80,64},{96,112},{112,96},{1... | collective-permute-start | bytes 1769480 | tf_op jit(solution)/shard_map/ppermute | solution.py:559
  19.8 18.2 %collective-permute-start.1 = (f32[72,2048]{1,0:T(8,128)S(1)}, f32[72,2048]{1,0:T(8,128)S(1)}, u32[]{:S(2)}, u32[]{:S(2)}) collective-permute-start(f32[72,2048]{1,0:T(8,128)S(1)} %get-tuple-element.41), channel_id=1, source_target_pairs={{0,64},{16,80},{32,96},{48,112},{64,0},{80,16},{96,32},{112,48},{1... | collective-permute-start | bytes 1769480 | tf_op jit(solution)/shard_map/ppermute | solution.py:559
  23.7 26.4 %collective-permute-start.2 = (f32[72,2048]{1,0:T(8,128)S(1)}, f32[72,2048]{1,0:T(8,128)S(1)}, u32[]{:S(2)}, u32[]{:S(2)}) collective-permute-start(f32[72,2048]{1,0:T(8,128)S(1)} %get-tuple-element.42), channel_id=1, source_target_pairs={{0,80},{16,64},{32,112},{48,96},{64,16},{80,0},{96,48},{112,32},{1... | collective-permute-start | bytes 1769480 | tf_op jit(solution)/shard_map/ppermute | solution.py:559
  23.8 39.2 %collective-permute-start.3 = (f32[72,2048]{1,0:T(8,128)S(1)}, f32[72,2048]{1,0:T(8,128)S(1)}, u32[]{:S(2)}, u32[]{:S(2)}) collective-permute-start(f32[72,2048]{1,0:T(8,128)S(1)} %get-tuple-element.43), channel_id=1, source_target_pairs={{0,32},{16,48},{32,64},{48,80},{64,96},{80,112},{96,0},{112,16},{1... | collective-permute-start | bytes 1769480 | tf_op jit(solution)/shard_map/ppermute | solution.py:559
  25.1 39.1 %collective-permute-start.4 = (f32[72,2048]{1,0:T(8,128)S(1)}, f32[72,2048]{1,0:T(8,128)S(1)}, u32[]{:S(2)}, u32[]{:S(2)}) collective-permute-start(f32[72,2048]{1,0:T(8,128)S(1)} %get-tuple-element.44), channel_id=1, source_target_pairs={{0,96},{16,112},{32,0},{48,16},{64,32},{80,48},{96,64},{112,80},{1... | collective-permute-start | bytes 1769480 | tf_op jit(solution)/shard_map/ppermute | solution.py:559
  27.2 48.3 %collective-permute-start.5 = (f32[72,2048]{1,0:T(8,128)S(1)}, f32[72,2048]{1,0:T(8,128)S(1)}, u32[]{:S(2)}, u32[]{:S(2)}) collective-permute-start(f32[72,2048]{1,0:T(8,128)S(1)} %get-tuple-element.45), channel_id=1, source_target_pairs={{0,48},{16,32},{32,80},{48,64},{64,112},{80,96},{96,16},{112,0},{1... | collective-permute-start | bytes 1769480 | tf_op jit(solution)/shard_map/ppermute | solution.py:559
  38.0 37.9 %collective-permute-start.6 = (f32[72,2048]{1,0:T(8,128)S(1)}, f32[72,2048]{1,0:T(8,128)S(1)}, u32[]{:S(2)}, u32[]{:S(2)}) collective-permute-start(f32[72,2048]{1,0:T(8,128)S(1)} %get-tuple-element.46), channel_id=1, source_target_pairs={{0,112},{16,96},{32,16},{48,0},{64,48},{80,32},{96,80},{112,64},{1... | collective-permute-start | bytes 1769480 | tf_op jit(solution)/shard_map/ppermute | solution.py:559
  83.7 75.0 %all-to-all-start.1 = ((f32[16,2,288,128]{3,2,1,0:T(8,128)}), f32[16,2,288,128]{3,2,1,0:T(8,128)}, u32[]{:S(2)}, u32[]{:S(2)}) async-start(f32[16,2,288,128]{3,2,1,0:T(8,128)} %bitcast.6), calls=%async_computation.1 | async-start | bytes 9437184 | tf_op jit(solution)/shard_map/all_to_all | solution.py:565
  88.8 59.0 %copy-start = (f32[192,2688]{1,0:T(8,128)S(1)}, f32[192,2688]{1,0:T(8,128)}, u32[]{:S(2)}) copy-start(f32[192,2688]{1,0:T(8,128)} %gradient.3) | copy-start | bytes 6193156
  94.4 18.4 %collective-permute-start.10 = (f32[72,2048]{1,0:T(8,128)S(1)}, f32[72,2048]{1,0:T(8,128)S(1)}, u32[]{:S(2)}, u32[]{:S(2)}) collective-permute-start(f32[72,2048]{1,0:T(8,128)S(1)} %get-tuple-element.53), channel_id=1, source_target_pairs={{0,32},{16,48},{32,64},{48,80},{64,96},{80,112},{96,0},{112,16},{1... | collective-permute-start | bytes 1769480 | tf_op jit(solution)/shard_map/ppermute | solution.py:559
  96.4 18.2 %collective-permute-start.11 = (f32[72,2048]{1,0:T(8,128)S(1)}, f32[72,2048]{1,0:T(8,128)S(1)}, u32[]{:S(2)}, u32[]{:S(2)}) collective-permute-start(f32[72,2048]{1,0:T(8,128)S(1)} %get-tuple-element.54), channel_id=1, source_target_pairs={{0,96},{16,112},{32,0},{48,16},{64,32},{80,48},{96,64},{112,80},{1... | collective-permute-start | bytes 1769480 | tf_op jit(solution)/shard_map/ppermute | solution.py:559
  98.6 24.2 %collective-permute-start.12 = (f32[72,2048]{1,0:T(8,128)S(1)}, f32[72,2048]{1,0:T(8,128)S(1)}, u32[]{:S(2)}, u32[]{:S(2)}) collective-permute-start(f32[72,2048]{1,0:T(8,128)S(1)} %get-tuple-element.55), channel_id=1, source_target_pairs={{0,48},{16,32},{32,80},{48,64},{64,112},{80,96},{96,16},{112,0},{1... | collective-permute-start | bytes 1769480 | tf_op jit(solution)/shard_map/ppermute | solution.py:559
  98.6 49.1 %collective-permute-start.13 = (f32[72,2048]{1,0:T(8,128)S(1)}, f32[72,2048]{1,0:T(8,128)S(1)}, u32[]{:S(2)}, u32[]{:S(2)}) collective-permute-start(f32[72,2048]{1,0:T(8,128)S(1)} %get-tuple-element.56), channel_id=1, source_target_pairs={{0,112},{16,96},{32,16},{48,0},{64,48},{80,32},{96,80},{112,64},{1... | collective-permute-start | bytes 1769480 | tf_op jit(solution)/shard_map/ppermute | solution.py:559
  101.6 46.2 %collective-permute-start.7 = (f32[72,2048]{1,0:T(8,128)S(1)}, f32[72,2048]{1,0:T(8,128)S(1)}, u32[]{:S(2)}, u32[]{:S(2)}) collective-permute-start(f32[72,2048]{1,0:T(8,128)S(1)} %get-tuple-element.50), channel_id=1, source_target_pairs={{0,16},{16,0},{32,48},{48,32},{64,80},{80,64},{96,112},{112,96},{1... | collective-permute-start | bytes 1769480 | tf_op jit(solution)/shard_map/ppermute | solution.py:559
  112.8 35.0 %collective-permute-start.8 = (f32[72,2048]{1,0:T(8,128)S(1)}, f32[72,2048]{1,0:T(8,128)S(1)}, u32[]{:S(2)}, u32[]{:S(2)}) collective-permute-start(f32[72,2048]{1,0:T(8,128)S(1)} %get-tuple-element.51), channel_id=1, source_target_pairs={{0,64},{16,80},{32,96},{48,112},{64,0},{80,16},{96,32},{112,48},{1... | collective-permute-start | bytes 1769480 | tf_op jit(solution)/shard_map/ppermute | solution.py:559
  114.7 33.1 %collective-permute-start.9 = (f32[72,2048]{1,0:T(8,128)S(1)}, f32[72,2048]{1,0:T(8,128)S(1)}, u32[]{:S(2)}, u32[]{:S(2)}) collective-permute-start(f32[72,2048]{1,0:T(8,128)S(1)} %get-tuple-element.52), channel_id=1, source_target_pairs={{0,80},{16,64},{32,112},{48,96},{64,16},{80,0},{96,48},{112,32},{1... | collective-permute-start | bytes 1769480 | tf_op jit(solution)/shard_map/ppermute | solution.py:559

commit v4 on v3

--- a/solution.py
+++ b/solution.py
@@ -34,7 +34,8 @@
 learn_rate = 0.001
 decay_rate = 0.1
 
-MOVES = [(0, 0), (0, 1), (2, 0), (2, 1), (1, 0), (3, 0), (1, 1), (3, 1)]
+MOVES = [(0, 0), (0, 1), (1, 0), (3, 0), (1, 1), (3, 1), (2, 0), (2, 1)]
+SINGLE = 6
 HBM = pl.BlockSpec(memory_space=pltpu.HBM)
 ANY = pl.BlockSpec(memory_space=pl.ANY)
 VMEM = pl.BlockSpec(memory_space=pltpu.VMEM)
@@ -58,6 +59,9 @@
         ),
         name=name,
     )(*args)
+
+
+GRID_ORDER = [(a - x) % 4 * 4 + x for a in range(4) for x in range(4)]
 
 
 def turned(row):
@@ -148,6 +152,10 @@
     return plan[:2], plan[2:]
 
 
+def chunk_of(shard):
+    return ((shard >> 2) + shard & 3) * 4 + (shard & 3)
+
+
 def unit_plan_kernel(place, units, send, take):
     m = place[0]
     lane = lax.broadcasted_iota(jnp.int32, (1, UNIT), 1)
@@ -162,7 +170,7 @@
     to_row = jnp.sum(to_row, axis=0, keepdims=True)
     to_column = jnp.sum(to_column, axis=1, keepdims=True)
     rank = jnp.sum(((to_row == to_column) & earlier).astype(jnp.int32), axis=0, keepdims=True)
-    send[...] = to_row * PAIR + rank
+    send[...] = chunk_of(to_row) * PAIR + rank
 
     row = units[pl.ds(m, 1), :]
     column = turned(row)
@@ -171,7 +179,7 @@
         from_row = from_row + (row >= t * UNITS).astype(jnp.int32)
         from_column = from_column + (column >= t * UNITS).astype(jnp.int32)
     lower = (from_row == from_column) & (column < row)
-    take[...] = from_row * PAIR + jnp.sum(lower.astype(jnp.int32), axis=0, keepdims=True)
+    take[...] = chunk_of(from_row) * PAIR + jnp.sum(lower.astype(jnp.int32), axis=0, keepdims=True)
 
 
 def unit_plan(new_units):
@@ -189,7 +197,7 @@
     )
 
 
-TERMS = 3
+TERMS = 2
 
 
 def terms(values):
@@ -235,6 +243,8 @@
 
 
 def pack_rows(tile, pack, pack_rest, outs):
+    double = outs[SINGLE]
+    outs = [*outs[:SINGLE], double.at[pl.ds(0, MESSAGE)], double.at[pl.ds(MESSAGE, MESSAGE)]]
     width = CHUNK * UNIT
     for i in range(0, TILES // 2, CHUNK):
         left = terms(joined([tile(n) for n in range(i, i + CHUNK)], 1))
@@ -250,6 +260,7 @@
 
 
 def take_rows(parts, take, take_rest, put):
+    parts = [*parts[:SINGLE], parts[SINGLE].at[pl.ds(0, MESSAGE)], parts[SINGLE + 1]]
     width = CHUNK * UNIT
     for i in range(0, TILES // 2, CHUNK):
         columns = slice(i * UNIT, (i + CHUNK) * UNIT)
@@ -279,7 +290,7 @@
             copy.wait()
 
 
-PARTS = 3
+PARTS = 7
 SPAN = UNITS // PARTS
 
 
@@ -311,7 +322,8 @@
                 parts[i] = None
 
 
-MESSAGES = [f32(MESSAGE, WIDE)] * DP
+MESSAGES = [f32(MESSAGE, WIDE)] * SINGLE + [f32(2 * MESSAGE, WIDE)]
+N_OUT = len(MESSAGES)
 SLOT_ARRAY = pltpu.HBM((SLOTS, BLOCK, UNIT), jnp.float32)
 SLOT_SPEC = HBM
 ARRAY = pltpu.VMEM((ROWS, COLS), jnp.float32)
@@ -351,7 +363,7 @@
 
 
 def row_pack_kernel(pack, pack_rest, whole, half, *rest):
-    outs, (whole_here, half_here, loads) = rest[:DP], rest[DP:]
+    outs, (whole_here, half_here, loads) = rest[:N_OUT], rest[N_OUT:]
     loads = Loads(loads)
     loads.start((whole, whole_here), (half, half_here))
 
@@ -374,7 +386,7 @@
         row_pack_kernel,
         "row_pack",
         [VMEM, VMEM, HBM, HBM],
-        [VMEM] * DP,
+        [VMEM] * N_OUT,
         MESSAGES,
         [ARRAY, ARRAY, dma(2 * PARTS)],
         9,
@@ -385,7 +397,7 @@
 
 
 def unit_row_pack_kernel(take, pack, pack_rest, recv, *rest):
-    outs, (here, sems) = rest[:DP], rest[DP:]
+    outs, (here, sems) = rest[:N_OUT], rest[N_OUT:]
     copies, arriving = Copies(sems), {}
     for i in range(0, TILES // 2, CHUNK):
         for n in [*range(i, i + CHUNK), *range(TILES // 2 + i, TILES // 2 + i + CHUNK)]:
@@ -413,7 +425,7 @@
         unit_row_pack_kernel,
         "unit_row_pack",
         [SMEM, VMEM, VMEM, ANY],
-        [VMEM] * DP,
+        [VMEM] * N_OUT,
         MESSAGES,
         [pltpu.VMEM((UNITS, BLOCK, UNIT), jnp.float32), dma(UNITS)],
         10,
@@ -456,67 +468,73 @@
     )
 
 
-def first_kernel(gradient, take, take_rest, *rest):
-    parts, (first, half, held, half_held, sems) = rest[:DP], rest[DP:]
-    copies, done = Copies(sems), set()
+def first_kernel(fixes, gradient, take, take_rest, *rest):
+    parts, (first, known, other, held, half, known_held, other_held, sems) = rest[:DP], rest[DP:]
+    copies = Copies(sems)
 
     def put(n, tile):
         if n < UNITS:
             columns = columns_of(n)
-            moment = beta_one * tile + (1.0 - beta_one) * gradient[:, columns]
-            held[:, columns] = moment
-            done.add(n)
-            span = n // SPAN
-            if all(u in done for u in range(span * SPAN, (span + 1) * SPAN)):
-                copies.start(held.at[:, span_of(span)], first.at[:, span_of(span)])
+            held[:, columns] = beta_one * tile + (1.0 - beta_one) * gradient[:, columns]
         else:
-            half_held[n - UNITS] = tile
-            copies.start(half_held.at[n - UNITS], half.at[n - UNITS])
+            half[n - UNITS] = tile
 
     take_rows(parts, take, take_rest, put)
+    for u in range(UNITS):
+        columns = columns_of(u)
+        upper = half[u // 2]
+        if u % 2 == 0:
+            upper = swapped(upper)
+        g = gradient[:, columns]
+        added = (1.0 - beta_two) * g * g
+        second = beta_two * upper + added
+        root = jnp.sqrt(second * fixes[1]) + epsilon
+        scaled = held[:, columns] * fixes[0]
+        known_held[:, columns] = jnp.where(left_lanes(ROWS), scaled, scaled / root)
+        other_held[:, columns] = jnp.where(left_lanes(ROWS), added, second)
+        if u % SPAN == SPAN - 1:
+            span = span_of(u // SPAN)
+            for here, out in ((held, first), (known_held, known), (other_held, other)):
+                copies.start(here.at[:, span], out.at[:, span])
     copies.wait()
 
 
-def first_moment(parts, take, gradient):
+def first_moment(parts, take, gradient, fixes):
+    whole = pltpu.HBM((ROWS, COLS), jnp.float32)
     return call(
         first_kernel,
         "first_moment",
-        [VMEM] * (3 + DP),
-        [HBM, HBM],
-        [pltpu.HBM((ROWS, COLS), jnp.float32), pltpu.HBM((PAIRS, ROWS, UNIT), jnp.float32)],
-        [ARRAY, pltpu.VMEM((PAIRS, ROWS, UNIT), jnp.float32), dma(TILES)],
-        11,
+        [SMEM] + [VMEM] * (3 + DP),
+        [HBM] * 3,
+        [whole] * 3,
+        [ARRAY, pltpu.VMEM((PAIRS, ROWS, UNIT), jnp.float32), ARRAY, ARRAY, dma(3 * PARTS)],
+        12,
+        fixes,
         gradient,
         *take,
         *parts,
     )
 
 
-def update_kernel(take, fixes, recv, first, half, gradient, *rest):
+def update_kernel(take, fixes, recv, known, other, *rest):
     outs, helds, rest = rest[:3], rest[3:6], rest[6:]
-    here, first_here, half_here, gradient_here, whole_loads, unit_loads, stores = rest
+    here, known_here, other_here, whole_loads, unit_loads, stores = rest
     loads, whole, stores = Copies(unit_loads), Loads(whole_loads), Copies(stores)
-    arrivals = [loads.start(recv.at[take[0, u]], here.at[u]) for u in range(UNITS // 3)]
-    whole.start((gradient, gradient_here), (first, first_here))
-    halves = loads.start(half, half_here)
-    arrivals += [loads.start(recv.at[take[0, u]], here.at[u]) for u in range(UNITS // 3, UNITS)]
+    arrivals = [loads.start(recv.at[take[0, u]], here.at[u]) for u in range(SPAN)]
+    whole.start((other, other_here), (known, known_here))
+    arrivals += [loads.start(recv.at[take[0, u]], here.at[u]) for u in range(SPAN, UNITS)]
     for u in range(UNITS):
         arrivals[u].wait()
+        whole.wait(0, u)
+        whole.wait(1, u)
         columns = columns_of(u)
         weight = here[u, :ROWS]
         lower = unfolded(here[u, ROWS:], False)
-        if u == 0:
-            halves.wait()
-        upper = half_here[u // 2]
-        if u % 2 == 0:
-            upper = swapped(upper)
-        second = jnp.where(left_lanes(ROWS), lower, upper)
-        whole.wait(0, u)
-        g = gradient_here[:, columns]
-        second = beta_two * second + (1.0 - beta_two) * g * g
-        root = jnp.sqrt(second / fixes[1]) + epsilon
-        whole.wait(1, u)
-        update = first_here[:, columns] / fixes[0] / root + decay_rate * weight
+        added = other_here[:, columns]
+        second = jnp.where(left_lanes(ROWS), beta_two * lower + added, added)
+        root = jnp.sqrt(second * fixes[1]) + epsilon
+        scaled = known_here[:, columns]
+        update = jnp.where(left_lanes(ROWS), scaled / root, scaled) + decay_rate * weight
         for held, out, value in zip(helds, outs, (weight - learn_rate * update, second, update)):
             held[:, columns] = value
             if u % SPAN == SPAN - 1:
@@ -525,44 +543,46 @@
     stores.wait()
 
 
-def weight_update(recv, take, fixes, first, half, gradient):
+def weight_update(recv, take, fixes, known, other):
     return call(
         update_kernel,
         "weight_update",
-        [SMEM, SMEM, ANY] + [HBM] * 3,
+        [SMEM, SMEM, ANY] + [HBM] * 2,
         [HBM] * 3,
         [f32(ROWS, COLS)] * 3,
         [ARRAY] * 3
         + [
             pltpu.VMEM((UNITS, BLOCK, UNIT), jnp.float32),
             ARRAY,
-            pltpu.VMEM((PAIRS, ROWS, UNIT), jnp.float32),
             ARRAY,
             dma(2 * PARTS),
-            dma(UNITS + 1),
+            dma(UNITS),
             dma(3 * PARTS),
         ],
-        16,
+        14,
         take,
         fixes,
         recv,
-        first,
-        half,
-        gradient,
-    )
+        known,
+        other,
+    )
+
+
+def move(part, dz, dc):
+    pairs = [(z * 2 + c, (z + dz) % 4 * 2 + (c + dc) % 2) for z in range(4) for c in range(2)]
+    return lax.ppermute(part, "dp", pairs)
 
 
 def swap_rows(parts):
-    arrived = []
-    for part, (dz, dc) in zip(parts, MOVES):
-        pairs = [(z * 2 + c, (z + dz) % 4 * 2 + (c + dc) % 2) for z in range(4) for c in range(2)]
-        arrived.append(lax.ppermute(part, "dp", pairs) if dz or dc else part)
-    return arrived
+    arrived = [move(part, *step) if any(step) else part for part, step in zip(parts, MOVES)]
+    return arrived + [move(arrived[SINGLE][MESSAGE:], 0, 1)]
 
 
 def swap_units(packed):
     packed = packed.reshape(MP, PAIR, BLOCK, UNIT)
-    arrived = lax.all_to_all(packed, "mp", split_axis=0, concat_axis=0, tiled=True)
+    arrived = lax.all_to_all(
+        packed, "mp", split_axis=0, concat_axis=0, tiled=True, axis_index_groups=[GRID_ORDER]
+    )
     return arrived.reshape(SLOTS, BLOCK, UNIT)
 
 
@@ -573,8 +593,8 @@
     count = step[0].astype(jnp.float32)
     fixes = jnp.stack(
         [
-            1.0 - jnp.power(jnp.float32(beta_one), count),
-            1.0 - jnp.power(jnp.float32(beta_two), count),
+            1.0 / (1.0 - jnp.power(jnp.float32(beta_one), count)),
+            1.0 / (1.0 - jnp.power(jnp.float32(beta_two), count)),
         ]
     )
 
@@ -586,9 +606,9 @@
     units_two = swap_units(packed)
     rows_two = swap_rows(unit_row_pack(units, take_units, pack))
 
-    new_first, half = first_moment(rows_two, take, gradient)
+    new_first, known, other = first_moment(rows_two, take, gradient, fixes)
     new_weight, new_second, update = weight_update(
-        units_two, take_units, fixes, in_hbm(new_first), in_hbm(half), in_hbm(gradient)
+        units_two, take_units, fixes, in_hbm(known), in_hbm(other)
     )
     return new_weight, new_first, new_second, update
 

time: 167 us -> 161 us (0.964)
  the two profiles are of different devices: /device:TPU:0 before, /device:TPU:5 now
where the time goes in v4:
time: 161 us
  waiting for transfers between devices  88.2 us (55%)
  starting transfers between devices  38.6 us (24%)
  Pallas kernels  31.6 us (20%)
  between operations  1.76 us (1%)
    ppermute x14, waiting for transfers between devices, move(): return lax.ppermute(part, 'dp', pairs)  85.1 us
    pallas_call x8, Pallas kernels, call(): pl.pallas_call(kernel, out_shape=out_shape, in_specs=ins, out_specs=outs,...  31.6 us
    ppermute x14, starting transfers between devices, move(): return lax.ppermute(part, 'dp', pairs)  25 us
    all_to_all x2, starting transfers between devices, swap_units(): lax.all_to_all(packed, 'mp', split_axis=0, concat_axis=0, tiled=True, axi...  13.6 us
  transfers between devices with their start and end apart: 16, of which 8 were waited for; matrix products, arithmetic and copies ran while one was open for 0% of the time, Pallas kernels for 13%

profile of v4, /device:TPU:5, one launch (start us, length us, event | category | flops | bytes accessed | tf_op | source)
XLA Modules:
  0.0 161.1 jit_solution(1025548132521475916)
XLA Ops:
  0.6 0.7 copy-done.1
  1.3 0.2 unit_plan.1
  1.5 4.4 %unit_pack.1 = f32[32,288,128]{2,1,0:T(8,128)} custom-call(s32[1,128]{1,0:T(1,128)S(1)} %get-tuple-element.33.send, f32[192,2688]{1,0:T(8,128)} %whole.2, f32[192,2688]{1,0:T(8,128)} %half.3), custom_call_target="tpu_custom_call" | custom-call | bytes 9437184 | tf_op jit(solution)/shard_map/unit_pack/pallas_call | solution.py:50
  6.0 6.9 %all-to-all-start = ((f32[16,2,288,128]{3,2,1,0:T(8,128)}), f32[16,2,288,128]{3,2,1,0:T(8,128)}, u32[]{:S(2)}, u32[]{:S(2)}) async-start(f32[16,2,288,128]{3,2,1,0:T(8,128)} %bitcast.7), calls=%async_computation | async-start | bytes 9437184 | tf_op jit(solution)/shard_map/all_to_all | solution.py:583
  12.9 1.3 row_plan.1
  14.2 5.0 %row_pack.1 = (f32[72,2048]{1,0:T(8,128)S(1)}, f32[72,2048]{1,0:T(8,128)S(1)}, f32[72,2048]{1,0:T(8,128)S(1)}, f32[72,2048]{1,0:T(8,128)S(1)}, f32[72,2048]{1,0:...) custom-call(bf16[256,192]{1,0:T(8,128)(2,1)S(1)} %get-tuple-element.36.pack, ...), custom_call_target="tpu_custom_call" | custom-call | bytes 9437184 | tf_op jit(solution)/shard_map/row_pack/pallas_call | solution.py:50
  19.2 3.7 %collective-permute-start.5 = (f32[144,2048]{1,0:T(8,128)S(1)}, f32[144,2048]{1,0:T(8,128)S(1)}, u32[]{:S(2)}, u32[]{:S(2)}) collective-permute-start(f32[144,2048]{1,0:T(8,128)S(1)} %get-tuple-element.44), channel_id=1, source_target_pairs={{0,64},{16,80},{32,96},{48,112},{64,0},{80,16},{96,32},{112,48},{1... | collective-permute-start | bytes 3538952 | tf_op jit(solution)/shard_map/ppermute | solution.py:573
  22.8 1.5 collective-permute-start
  24.3 0.7 collective-permute-start.1
  25.1 1.9 %collective-permute-start.2 = (f32[72,2048]{1,0:T(8,128)S(1)}, f32[72,2048]{1,0:T(8,128)S(1)}, u32[]{:S(2)}, u32[]{:S(2)}) collective-permute-start(f32[72,2048]{1,0:T(8,128)S(1)} %get-tuple-element.41), channel_id=1, source_target_pairs={{0,96},{16,112},{32,0},{48,16},{64,32},{80,48},{96,64},{112,80},{1... | collective-permute-start | bytes 1769480 | tf_op jit(solution)/shard_map/ppermute | solution.py:573
  27.0 20.9 %collective-permute-done.5.rest_6_ = f32[144,2048]{1,0:T(8,128)S(1)} collective-permute-done((f32[144,2048]{1,0:T(8,128)S(1)}, f32[144,2048]{1,0:T(8,128)S(1)}, u32[]{:S(2)}, u32[]{:S(2)}) %collective-permute-start.5) | collective-permute-done | bytes 1179680 | tf_op jit(solution)/shard_map/ppermute | solution.py:573
  47.9 6.6 %collective-permute-start.4 = (f32[72,2048]{1,0:T(8,128)S(1)}, f32[72,2048]{1,0:T(8,128)S(1)}, u32[]{:S(2)}, u32[]{:S(2)}) collective-permute-start(f32[72,2048]{1,0:T(8,128)S(1)} %get-tuple-element.43), channel_id=1, source_target_pairs={{0,112},{16,96},{32,16},{48,0},{64,48},{80,32},{96,80},{112,64},{1... | collective-permute-start | bytes 1769480 | tf_op jit(solution)/shard_map/ppermute | solution.py:573
  54.6 0.1 collective-permute-start.6
  54.7 7.3 %collective-permute-done.1.rest_2_ = f32[72,2048]{1,0:T(8,128)S(1)} collective-permute-done((f32[72,2048]{1,0:T(8,128)S(1)}, f32[72,2048]{1,0:T(8,128)S(1)}, u32[]{:S(2)}, u32[]{:S(2)}) %collective-permute-start.1) | collective-permute-done | bytes 589856 | tf_op jit(solution)/shard_map/ppermute | solution.py:573
  62.1 12.7 %collective-permute-done.3.rest_4_ = f32[72,2048]{1,0:T(8,128)S(1)} collective-permute-done((f32[72,2048]{1,0:T(8,128)S(1)}, f32[72,2048]{1,0:T(8,128)S(1)}, u32[]{:S(2)}, u32[]{:S(2)}) %collective-permute-start.3) | collective-permute-done | bytes 589856 | tf_op jit(solution)/shard_map/ppermute | solution.py:573
  74.7 0.8 collective-permute-done.4.rest_5_
  75.5 3.8 %row_unit_pack.1 = f32[32,288,128]{2,1,0:T(8,128)} custom-call(s32[1,128]{1,0:T(1,128)S(1)} %get-tuple-element.33.send, bf16[192,256]{1,0:T(8,128)(2,1)S(1)} %get-tuple-element.34.take, bf16[384,64]{1,0:T(8,128)(2,1)S(1)} %get-tuple-element.35.take_rest, f32[72,2048]{1,0:T(8,128)S(1)} %get-tuple-element.38.rest_0_, ...), custom_call_target="tpu_custom_call" | custom-call | bytes 10485760 | tf_op jit(solution)/shard_map/row_unit_pack/pallas_call | solution.py:50
  79.3 6.7 %all-to-all-start.1 = ((f32[16,2,288,128]{3,2,1,0:T(8,128)}), f32[16,2,288,128]{3,2,1,0:T(8,128)}, u32[]{:S(2)}, u32[]{:S(2)}) async-start(f32[16,2,288,128]{3,2,1,0:T(8,128)} %bitcast.6), calls=%async_computation.1 | async-start | bytes 9437184 | tf_op jit(solution)/shard_map/all_to_all | solution.py:583
  86.1 4.8 %unit_row_pack.1 = (f32[72,2048]{1,0:T(8,128)S(1)}, f32[72,2048]{1,0:T(8,128)S(1)}, f32[72,2048]{1,0:T(8,128)S(1)}, f32[72,2048]{1,0:T(8,128)S(1)}, f32[72,2048]...) custom-call(s32[1,21]{1,0:T(1,128)S(1)} %get-tuple-element.32.take, ...), custom_call_target="tpu_custom_call" | custom-call | bytes 10485760 | tf_op jit(solution)/shard_map/unit_row_pack/pallas_call | solution.py:50
  90.8 2.3 %collective-permute-start.12 = (f32[144,2048]{1,0:T(8,128)S(1)}, f32[144,2048]{1,0:T(8,128)S(1)}, u32[]{:S(2)}, u32[]{:S(2)}) collective-permute-start(f32[144,2048]{1,0:T(8,128)S(1)} %get-tuple-element.53), channel_id=1, source_target_pairs={{0,64},{16,80},{32,96},{48,112},{64,0},{80,16},{96,32},{112,48},{1... | collective-permute-start | bytes 3538952 | tf_op jit(solution)/shard_map/ppermute | solution.py:573
  93.1 1.1 collective-permute-start.7
  94.2 0.7 collective-permute-start.8
  94.9 2.0 %collective-permute-start.9 = (f32[72,2048]{1,0:T(8,128)S(1)}, f32[72,2048]{1,0:T(8,128)S(1)}, u32[]{:S(2)}, u32[]{:S(2)}) collective-permute-start(f32[72,2048]{1,0:T(8,128)S(1)} %get-tuple-element.50), channel_id=1, source_target_pairs={{0,96},{16,112},{32,0},{48,16},{64,32},{80,48},{96,64},{112,80},{1... | collective-permute-start | bytes 1769480 | tf_op jit(solution)/shard_map/ppermute | solution.py:573
  96.9 23.1 %collective-permute-done.12.rest_6_ = f32[144,2048]{1,0:T(8,128)S(1)} collective-permute-done((f32[144,2048]{1,0:T(8,128)S(1)}, f32[144,2048]{1,0:T(8,128)S(1)}, u32[]{:S(2)}, u32[]{:S(2)}) %collective-permute-start.12) | collective-permute-done | bytes 1179680 | tf_op jit(solution)/shard_map/ppermute | solution.py:573
  120.1 4.3 %collective-permute-start.11 = (f32[72,2048]{1,0:T(8,128)S(1)}, f32[72,2048]{1,0:T(8,128)S(1)}, u32[]{:S(2)}, u32[]{:S(2)}) collective-permute-start(f32[72,2048]{1,0:T(8,128)S(1)} %get-tuple-element.52), channel_id=1, source_target_pairs={{0,112},{16,96},{32,16},{48,0},{64,48},{80,32},{96,80},{112,64},{1... | collective-permute-start | bytes 1769480 | tf_op jit(solution)/shard_map/ppermute | solution.py:573
  124.4 0.1 collective-permute-start.13
  125.3 0.1 pad_maximum_fusion.fixes
  125.4 7.7 %collective-permute-done.8.rest_2_ = f32[72,2048]{1,0:T(8,128)S(1)} collective-permute-done((f32[72,2048]{1,0:T(8,128)S(1)}, f32[72,2048]{1,0:T(8,128)S(1)}, u32[]{:S(2)}, u32[]{:S(2)}) %collective-permute-start.8) | collective-permute-done | bytes 589856 | tf_op jit(solution)/shard_map/ppermute | solution.py:573
  133.1 12.5 %collective-permute-done.10.rest_4_ = f32[72,2048]{1,0:T(8,128)S(1)} collective-permute-done((f32[72,2048]{1,0:T(8,128)S(1)}, f32[72,2048]{1,0:T(8,128)S(1)}, u32[]{:S(2)}, u32[]{:S(2)}) %collective-permute-start.10) | collective-permute-done | bytes 589856 | tf_op jit(solution)/shard_map/ppermute | solution.py:573
  145.7 5.8 %first_moment.1 = (f32[192,2688]{1,0:T(8,128)}, f32[192,2688]{1,0:T(8,128)}, f32[192,2688]{1,0:T(8,128)}) custom-call(f32[2]{0:T(128)S(1)} %pad_maximum_fusion.fixes, f32[192,2688]{1,0:T(8,128)S(1)} %copy-done, bf16[192,256]{1,0:T(8,128)(2,1)S(1)} %get-tuple-element.34.take, bf16[384,64]{1,0:T(8,128)(2,1)S(1)} %get-tuple-element.35.take_rest, ...), custom_call_target="tpu_custom_call" | custom-call | bytes 12582912 | tf_op jit(solution)/shard_map/first_moment/pallas_call | solution.py:50
  151.5 3.1 %all-to-all-done.1 = f32[16,2,288,128]{3,2,1,0:T(8,128)} async-done(((f32[16,2,288,128]{3,2,1,0:T(8,128)}), f32[16,2,288,128]{3,2,1,0:T(8,128)}, u32[]{:S(2)}, u32[]{:S(2)}) %all-to-all-start.1) | async-done | bytes 4718624 | tf_op jit(solution)/shard_map/all_to_all | solution.py:583
  154.6 6.4 %weight_update.1 = (f32[192,2688]{1,0:T(8,128)}, f32[192,2688]{1,0:T(8,128)}, f32[192,2688]{1,0:T(8,128)}) custom-call(s32[1,21]{1,0:T(1,128)S(1)} %get-tuple-element.32.take, f32[2]{0:T(128)S(1)} %pad_maximum_fusion.fixes, f32[32,288,128]{2,1,0:T(8,128)} %bitcast.5.recv, f32[192,2688]{1,0:T(8,128)} %get-tuple-element.54.known, ...), custom_call_target="tpu_custom_call" | custom-call | bytes 14680064 | tf_op jit(solution)/shard_map/weight_update/pallas_call | solution.py:50
  (19 shorter events, 0.1 us)
Async XLA Ops:
  0.6 0.7 copy-start.1
  6.0 6.9 %copy-start.2 = (s32[8,192]{1,0:T(8,128)S(1)}, s32[8,192]{1,0:T(8,128)}, u32[]{:S(2)}) copy-start(s32[8,192]{1,0:T(8,128)} %old.1) | copy-start | bytes 18436
  6.0 6.9 %copy-start.3 = (s32[8,192]{1,0:T(8,128)S(1)}, s32[8,192]{1,0:T(8,128)}, u32[]{:S(2)}) copy-start(s32[8,192]{1,0:T(8,128)} %new.1) | copy-start | bytes 18436
  6.0 73.4 %all-to-all-start = ((f32[16,2,288,128]{3,2,1,0:T(8,128)}), f32[16,2,288,128]{3,2,1,0:T(8,128)}, u32[]{:S(2)}, u32[]{:S(2)}) async-start(f32[16,2,288,128]{3,2,1,0:T(8,128)} %bitcast.7), calls=%async_computation | async-start | bytes 9437184 | tf_op jit(solution)/shard_map/all_to_all | solution.py:583
  19.2 28.8 %collective-permute-start.5 = (f32[144,2048]{1,0:T(8,128)S(1)}, f32[144,2048]{1,0:T(8,128)S(1)}, u32[]{:S(2)}, u32[]{:S(2)}) collective-permute-start(f32[144,2048]{1,0:T(8,128)S(1)} %get-tuple-element.44), channel_id=1, source_target_pairs={{0,64},{16,80},{32,96},{48,112},{64,0},{80,16},{96,32},{112,48},{1... | collective-permute-start | bytes 3538952 | tf_op jit(solution)/shard_map/ppermute | solution.py:573
  22.8 31.8 %collective-permute-start = (f32[72,2048]{1,0:T(8,128)S(1)}, f32[72,2048]{1,0:T(8,128)S(1)}, u32[]{:S(2)}, u32[]{:S(2)}) collective-permute-start(f32[72,2048]{1,0:T(8,128)S(1)} %get-tuple-element.39), channel_id=1, source_target_pairs={{0,16},{16,0},{32,48},{48,32},{64,80},{80,64},{96,112},{112,96},{1... | collective-permute-start | bytes 1769480 | tf_op jit(solution)/shard_map/ppermute | solution.py:573
  24.3 37.7 %collective-permute-start.1 = (f32[72,2048]{1,0:T(8,128)S(1)}, f32[72,2048]{1,0:T(8,128)S(1)}, u32[]{:S(2)}, u32[]{:S(2)}) collective-permute-start(f32[72,2048]{1,0:T(8,128)S(1)} %get-tuple-element.40), channel_id=1, source_target_pairs={{0,32},{16,48},{32,64},{48,80},{64,96},{80,112},{96,0},{112,16},{1... | collective-permute-start | bytes 1769480 | tf_op jit(solution)/shard_map/ppermute | solution.py:573
  25.1 37.0 %collective-permute-start.2 = (f32[72,2048]{1,0:T(8,128)S(1)}, f32[72,2048]{1,0:T(8,128)S(1)}, u32[]{:S(2)}, u32[]{:S(2)}) collective-permute-start(f32[72,2048]{1,0:T(8,128)S(1)} %get-tuple-element.41), channel_id=1, source_target_pairs={{0,96},{16,112},{32,0},{48,16},{64,32},{80,48},{96,64},{112,80},{1... | collective-permute-start | bytes 1769480 | tf_op jit(solution)/shard_map/ppermute | solution.py:573
  27.0 47.7 %collective-permute-start.3 = (f32[72,2048]{1,0:T(8,128)S(1)}, f32[72,2048]{1,0:T(8,128)S(1)}, u32[]{:S(2)}, u32[]{:S(2)}) collective-permute-start(f32[72,2048]{1,0:T(8,128)S(1)} %get-tuple-element.42), channel_id=1, source_target_pairs={{0,48},{16,32},{32,80},{48,64},{64,112},{80,96},{96,16},{112,0},{1... | collective-permute-start | bytes 1769480 | tf_op jit(solution)/shard_map/ppermute | solution.py:573
  47.9 27.6 %collective-permute-start.4 = (f32[72,2048]{1,0:T(8,128)S(1)}, f32[72,2048]{1,0:T(8,128)S(1)}, u32[]{:S(2)}, u32[]{:S(2)}) collective-permute-start(f32[72,2048]{1,0:T(8,128)S(1)} %get-tuple-element.43), channel_id=1, source_target_pairs={{0,112},{16,96},{32,16},{48,0},{64,48},{80,32},{96,80},{112,64},{1... | collective-permute-start | bytes 1769480 | tf_op jit(solution)/shard_map/ppermute | solution.py:573
  54.6 20.9 %collective-permute-start.6 = (f32[72,2048]{1,0:T(8,128)S(1)}, f32[72,2048]{1,0:T(8,128)S(1)}, u32[]{:S(2)}, u32[]{:S(2)}) collective-permute-start(f32[72,2048]{1,0:T(8,128)S(1)} %slice.8), channel_id=1, source_target_pairs={{0,16},{16,0},{32,48},{48,32},{64,80},{80,64},{96,112},{112,96},{1... | collective-permute-start | bytes 1769480 | tf_op jit(solution)/shard_map/ppermute | solution.py:573
  79.3 75.2 %all-to-all-start.1 = ((f32[16,2,288,128]{3,2,1,0:T(8,128)}), f32[16,2,288,128]{3,2,1,0:T(8,128)}, u32[]{:S(2)}, u32[]{:S(2)}) async-start(f32[16,2,288,128]{3,2,1,0:T(8,128)} %bitcast.6), calls=%async_computation.1 | async-start | bytes 9437184 | tf_op jit(solution)/shard_map/all_to_all | solution.py:583
  86.1 59.6 %copy-start = (f32[192,2688]{1,0:T(8,128)S(1)}, f32[192,2688]{1,0:T(8,128)}, u32[]{:S(2)}) copy-start(f32[192,2688]{1,0:T(8,128)} %gradient.1) | copy-start | bytes 6193156
  90.8 29.2 %collective-permute-start.12 = (f32[144,2048]{1,0:T(8,128)S(1)}, f32[144,2048]{1,0:T(8,128)S(1)}, u32[]{:S(2)}, u32[]{:S(2)}) collective-permute-start(f32[144,2048]{1,0:T(8,128)S(1)} %get-tuple-element.53), channel_id=1, source_target_pairs={{0,64},{16,80},{32,96},{48,112},{64,0},{80,16},{96,32},{112,48},{1... | collective-permute-start | bytes 3538952 | tf_op jit(solution)/shard_map/ppermute | solution.py:573
  93.1 31.3 %collective-permute-start.7 = (f32[72,2048]{1,0:T(8,128)S(1)}, f32[72,2048]{1,0:T(8,128)S(1)}, u32[]{:S(2)}, u32[]{:S(2)}) collective-permute-start(f32[72,2048]{1,0:T(8,128)S(1)} %get-tuple-element.48), channel_id=1, source_target_pairs={{0,16},{16,0},{32,48},{48,32},{64,80},{80,64},{96,112},{112,96},{1... | collective-permute-start | bytes 1769480 | tf_op jit(solution)/shard_map/ppermute | solution.py:573
  94.2 38.9 %collective-permute-start.8 = (f32[72,2048]{1,0:T(8,128)S(1)}, f32[72,2048]{1,0:T(8,128)S(1)}, u32[]{:S(2)}, u32[]{:S(2)}) collective-permute-start(f32[72,2048]{1,0:T(8,128)S(1)} %get-tuple-element.49), channel_id=1, source_target_pairs={{0,32},{16,48},{32,64},{48,80},{64,96},{80,112},{96,0},{112,16},{1... | collective-permute-start | bytes 1769480 | tf_op jit(solution)/shard_map/ppermute | solution.py:573
  94.9 38.2 %collective-permute-start.9 = (f32[72,2048]{1,0:T(8,128)S(1)}, f32[72,2048]{1,0:T(8,128)S(1)}, u32[]{:S(2)}, u32[]{:S(2)}) collective-permute-start(f32[72,2048]{1,0:T(8,128)S(1)} %get-tuple-element.50), channel_id=1, source_target_pairs={{0,96},{16,112},{32,0},{48,16},{64,32},{80,48},{96,64},{112,80},{1... | collective-permute-start | bytes 1769480 | tf_op jit(solution)/shard_map/ppermute | solution.py:573
  96.9 48.8 %collective-permute-start.10 = (f32[72,2048]{1,0:T(8,128)S(1)}, f32[72,2048]{1,0:T(8,128)S(1)}, u32[]{:S(2)}, u32[]{:S(2)}) collective-permute-start(f32[72,2048]{1,0:T(8,128)S(1)} %get-tuple-element.51), channel_id=1, source_target_pairs={{0,48},{16,32},{32,80},{48,64},{64,112},{80,96},{96,16},{112,0},{1... | collective-permute-start | bytes 1769480 | tf_op jit(solution)/shard_map/ppermute | solution.py:573
  120.1 25.6 %collective-permute-start.11 = (f32[72,2048]{1,0:T(8,128)S(1)}, f32[72,2048]{1,0:T(8,128)S(1)}, u32[]{:S(2)}, u32[]{:S(2)}) collective-permute-start(f32[72,2048]{1,0:T(8,128)S(1)} %get-tuple-element.52), channel_id=1, source_target_pairs={{0,112},{16,96},{32,16},{48,0},{64,48},{80,32},{96,80},{112,64},{1... | collective-permute-start | bytes 1769480 | tf_op jit(solution)/shard_map/ppermute | solution.py:573
  124.4 21.3 %collective-permute-start.13 = (f32[72,2048]{1,0:T(8,128)S(1)}, f32[72,2048]{1,0:T(8,128)S(1)}, u32[]{:S(2)}, u32[]{:S(2)}) collective-permute-start(f32[72,2048]{1,0:T(8,128)S(1)} %slice.9), channel_id=1, source_target_pairs={{0,16},{16,0},{32,48},{48,32},{64,80},{80,64},{96,112},{112,96},{1... | collective-permute-start | bytes 1769480 | tf_op jit(solution)/shard_map/ppermute | solution.py:573

commit v5 on v3

--- a/solution.py
+++ b/solution.py
@@ -34,7 +34,8 @@
 learn_rate = 0.001
 decay_rate = 0.1
 
-MOVES = [(0, 0), (0, 1), (2, 0), (2, 1), (1, 0), (3, 0), (1, 1), (3, 1)]
+MOVES = [(0, 0), (0, 1), (1, 0), (3, 0), (1, 1), (3, 1), (2, 0), (2, 1)]
+SINGLE = 6
 HBM = pl.BlockSpec(memory_space=pltpu.HBM)
 ANY = pl.BlockSpec(memory_space=pl.ANY)
 VMEM = pl.BlockSpec(memory_space=pltpu.VMEM)
@@ -58,6 +59,9 @@
         ),
         name=name,
     )(*args)
+
+
+GRID_ORDER = [(x - a) % 4 * 4 + x for a in range(4) for x in range(4)]
 
 
 def turned(row):
@@ -148,6 +152,10 @@
     return plan[:2], plan[2:]
 
 
+def chunk_of(shard):
+    return (shard - (shard >> 2) & 3) * 4 + (shard & 3)
+
+
 def unit_plan_kernel(place, units, send, take):
     m = place[0]
     lane = lax.broadcasted_iota(jnp.int32, (1, UNIT), 1)
@@ -162,7 +170,7 @@
     to_row = jnp.sum(to_row, axis=0, keepdims=True)
     to_column = jnp.sum(to_column, axis=1, keepdims=True)
     rank = jnp.sum(((to_row == to_column) & earlier).astype(jnp.int32), axis=0, keepdims=True)
-    send[...] = to_row * PAIR + rank
+    send[...] = chunk_of(to_row) * PAIR + rank
 
     row = units[pl.ds(m, 1), :]
     column = turned(row)
@@ -171,7 +179,7 @@
         from_row = from_row + (row >= t * UNITS).astype(jnp.int32)
         from_column = from_column + (column >= t * UNITS).astype(jnp.int32)
     lower = (from_row == from_column) & (column < row)
-    take[...] = from_row * PAIR + jnp.sum(lower.astype(jnp.int32), axis=0, keepdims=True)
+    take[...] = chunk_of(from_row) * PAIR + jnp.sum(lower.astype(jnp.int32), axis=0, keepdims=True)
 
 
 def unit_plan(new_units):
@@ -189,7 +197,7 @@
     )
 
 
-TERMS = 3
+TERMS = 2
 
 
 def terms(values):
@@ -235,6 +243,8 @@
 
 
 def pack_rows(tile, pack, pack_rest, outs):
+    double = outs[SINGLE]
+    outs = [*outs[:SINGLE], double.at[pl.ds(0, MESSAGE)], double.at[pl.ds(MESSAGE, MESSAGE)]]
     width = CHUNK * UNIT
     for i in range(0, TILES // 2, CHUNK):
         left = terms(joined([tile(n) for n in range(i, i + CHUNK)], 1))
@@ -250,6 +260,7 @@
 
 
 def take_rows(parts, take, take_rest, put):
+    parts = [*parts[:SINGLE], parts[SINGLE].at[pl.ds(0, MESSAGE)], parts[SINGLE + 1]]
     width = CHUNK * UNIT
     for i in range(0, TILES // 2, CHUNK):
         columns = slice(i * UNIT, (i + CHUNK) * UNIT)
@@ -311,7 +322,8 @@
                 parts[i] = None
 
 
-MESSAGES = [f32(MESSAGE, WIDE)] * DP
+MESSAGES = [f32(MESSAGE, WIDE)] * SINGLE + [f32(2 * MESSAGE, WIDE)]
+N_OUT = len(MESSAGES)
 SLOT_ARRAY = pltpu.HBM((SLOTS, BLOCK, UNIT), jnp.float32)
 SLOT_SPEC = HBM
 ARRAY = pltpu.VMEM((ROWS, COLS), jnp.float32)
@@ -351,7 +363,7 @@
 
 
 def row_pack_kernel(pack, pack_rest, whole, half, *rest):
-    outs, (whole_here, half_here, loads) = rest[:DP], rest[DP:]
+    outs, (whole_here, half_here, loads) = rest[:N_OUT], rest[N_OUT:]
     loads = Loads(loads)
     loads.start((whole, whole_here), (half, half_here))
 
@@ -374,7 +386,7 @@
         row_pack_kernel,
         "row_pack",
         [VMEM, VMEM, HBM, HBM],
-        [VMEM] * DP,
+        [VMEM] * N_OUT,
         MESSAGES,
         [ARRAY, ARRAY, dma(2 * PARTS)],
         9,
@@ -385,7 +397,7 @@
 
 
 def unit_row_pack_kernel(take, pack, pack_rest, recv, *rest):
-    outs, (here, sems) = rest[:DP], rest[DP:]
+    outs, (here, sems) = rest[:N_OUT], rest[N_OUT:]
     copies, arriving = Copies(sems), {}
     for i in range(0, TILES // 2, CHUNK):
         for n in [*range(i, i + CHUNK), *range(TILES // 2 + i, TILES // 2 + i + CHUNK)]:
@@ -413,7 +425,7 @@
         unit_row_pack_kernel,
         "unit_row_pack",
         [SMEM, VMEM, VMEM, ANY],
-        [VMEM] * DP,
+        [VMEM] * N_OUT,
         MESSAGES,
         [pltpu.VMEM((UNITS, BLOCK, UNIT), jnp.float32), dma(UNITS)],
         10,
@@ -552,17 +564,21 @@
     )
 
 
+def move(part, dz, dc):
+    pairs = [(z * 2 + c, (z + dz) % 4 * 2 + (c + dc) % 2) for z in range(4) for c in range(2)]
+    return lax.ppermute(part, "dp", pairs)
+
+
 def swap_rows(parts):
-    arrived = []
-    for part, (dz, dc) in zip(parts, MOVES):
-        pairs = [(z * 2 + c, (z + dz) % 4 * 2 + (c + dc) % 2) for z in range(4) for c in range(2)]
-        arrived.append(lax.ppermute(part, "dp", pairs) if dz or dc else part)
-    return arrived
+    arrived = [move(part, *step) if any(step) else part for part, step in zip(parts, MOVES)]
+    return arrived + [move(arrived[SINGLE][MESSAGE:], 0, 1)]
 
 
 def swap_units(packed):
     packed = packed.reshape(MP, PAIR, BLOCK, UNIT)
-    arrived = lax.all_to_all(packed, "mp", split_axis=0, concat_axis=0, tiled=True)
+    arrived = lax.all_to_all(
+        packed, "mp", split_axis=0, concat_axis=0, tiled=True, axis_index_groups=[GRID_ORDER]
+    )
     return arrived.reshape(SLOTS, BLOCK, UNIT)
 
 

time: 167 us -> 160 us (0.958)
  the two profiles are of different devices: /device:TPU:0 before, /device:TPU:12 now
where the time goes in v5:
time: 160 us
  waiting for transfers between devices  92 us (58%)
  starting transfers between devices  35.4 us (22%)
  Pallas kernels  29.5 us (18%)
  between operations  1.66 us (1%)
    ppermute x14, waiting for transfers between devices, move(): return lax.ppermute(part, 'dp', pairs)  87.9 us
    pallas_call x8, Pallas kernels, call(): pl.pallas_call(kernel, out_shape=out_shape, in_specs=ins, out_specs=outs,...  29.5 us
    ppermute x14, starting transfers between devices, move(): return lax.ppermute(part, 'dp', pairs)  20.8 us
    all_to_all x2, starting transfers between devices, swap_units(): lax.all_to_all(packed, 'mp', split_axis=0, concat_axis=0, tiled=True, axi...  14.7 us
    all_to_all x2, waiting for transfers between devices, swap_units(): lax.all_to_all(packed, 'mp', split_axis=0, concat_axis=0, tiled=True, axi...  4.09 us
  transfers between devices with their start and end apart: 16, of which 9 were waited for; matrix products, arithmetic and copies ran while one was open for 0% of the time, Pallas kernels for 11%

profile of v5, /device:TPU:12, one launch (start us, length us, event | category | flops | bytes accessed | tf_op | source)
XLA Modules:
  0.0 159.5 jit_solution(11681974092023935164)
XLA Ops:
  0.6 0.7 copy-done.1
  1.3 0.2 unit_plan.1
  1.5 4.2 %unit_pack.1 = f32[32,288,128]{2,1,0:T(8,128)} custom-call(s32[1,128]{1,0:T(1,128)S(1)} %get-tuple-element.32.send, f32[192,2688]{1,0:T(8,128)} %whole.2, f32[192,2688]{1,0:T(8,128)} %half.3), custom_call_target="tpu_custom_call" | custom-call | bytes 9437184 | tf_op jit(solution)/shard_map/unit_pack/pallas_call | solution.py:50
  5.7 0.0 copy-start.2
  5.7 0.0 copy-start.3
  5.7 7.3 %all-to-all-start = ((f32[16,2,288,128]{3,2,1,0:T(8,128)}), f32[16,2,288,128]{3,2,1,0:T(8,128)}, u32[]{:S(2)}, u32[]{:S(2)}) async-start(f32[16,2,288,128]{3,2,1,0:T(8,128)} %bitcast.7), calls=%async_computation | async-start | bytes 9437184 | tf_op jit(solution)/shard_map/all_to_all | solution.py:579
  13.1 1.3 row_plan.1
  14.4 4.5 %row_pack.1 = (f32[72,2048]{1,0:T(8,128)S(1)}, f32[72,2048]{1,0:T(8,128)S(1)}, f32[72,2048]{1,0:T(8,128)S(1)}, f32[72,2048]{1,0:T(8,128)S(1)}, f32[72,2048]{1,0:...) custom-call(bf16[256,192]{1,0:T(8,128)(2,1)S(1)} %get-tuple-element.35.pack, ...), custom_call_target="tpu_custom_call" | custom-call | bytes 9437184 | tf_op jit(solution)/shard_map/row_pack/pallas_call | solution.py:50
  18.9 4.0 %collective-permute-start.5 = (f32[144,2048]{1,0:T(8,128)S(1)}, f32[144,2048]{1,0:T(8,128)S(1)}, u32[]{:S(2)}, u32[]{:S(2)}) collective-permute-start(f32[144,2048]{1,0:T(8,128)S(1)} %get-tuple-element.43), channel_id=1, source_target_pairs={{0,64},{16,80},{32,96},{48,112},{64,0},{80,16},{96,32},{112,48},{1... | collective-permute-start | bytes 3538952 | tf_op jit(solution)/shard_map/ppermute | solution.py:569
  22.8 1.0 collective-permute-start.1
  23.9 2.2 %collective-permute-start.2 = (f32[72,2048]{1,0:T(8,128)S(1)}, f32[72,2048]{1,0:T(8,128)S(1)}, u32[]{:S(2)}, u32[]{:S(2)}) collective-permute-start(f32[72,2048]{1,0:T(8,128)S(1)} %get-tuple-element.40), channel_id=1, source_target_pairs={{0,96},{16,112},{32,0},{48,16},{64,32},{80,48},{96,64},{112,80},{1... | collective-permute-start | bytes 1769480 | tf_op jit(solution)/shard_map/ppermute | solution.py:569
  26.1 0.0 collective-permute-start.3
  26.1 23.7 %collective-permute-done.5.rest_6_ = f32[144,2048]{1,0:T(8,128)S(1)} collective-permute-done((f32[144,2048]{1,0:T(8,128)S(1)}, f32[144,2048]{1,0:T(8,128)S(1)}, u32[]{:S(2)}, u32[]{:S(2)}) %collective-permute-start.5) | collective-permute-done | bytes 1179680 | tf_op jit(solution)/shard_map/ppermute | solution.py:569
  49.8 0.0 collective-permute-done.rest_1_
  49.8 3.9 %collective-permute-start.6 = (f32[72,2048]{1,0:T(8,128)S(1)}, f32[72,2048]{1,0:T(8,128)S(1)}, u32[]{:S(2)}, u32[]{:S(2)}) collective-permute-start(f32[72,2048]{1,0:T(8,128)S(1)} %slice.8), channel_id=1, source_target_pairs={{0,16},{16,0},{32,48},{48,32},{64,80},{80,64},{96,112},{112,96},{1... | collective-permute-start | bytes 1769480 | tf_op jit(solution)/shard_map/ppermute | solution.py:569
  53.7 8.2 %collective-permute-done.1.rest_2_ = f32[72,2048]{1,0:T(8,128)S(1)} collective-permute-done((f32[72,2048]{1,0:T(8,128)S(1)}, f32[72,2048]{1,0:T(8,128)S(1)}, u32[]{:S(2)}, u32[]{:S(2)}) %collective-permute-start.1) | collective-permute-done | bytes 589856 | tf_op jit(solution)/shard_map/ppermute | solution.py:569
  61.9 1.5 collective-permute-done.2.rest_3_
  63.4 10.1 %collective-permute-done.3.rest_4_ = f32[72,2048]{1,0:T(8,128)S(1)} collective-permute-done((f32[72,2048]{1,0:T(8,128)S(1)}, f32[72,2048]{1,0:T(8,128)S(1)}, u32[]{:S(2)}, u32[]{:S(2)}) %collective-permute-start.3) | collective-permute-done | bytes 589856 | tf_op jit(solution)/shard_map/ppermute | solution.py:569
  73.5 3.8 %row_unit_pack.1 = f32[32,288,128]{2,1,0:T(8,128)} custom-call(s32[1,128]{1,0:T(1,128)S(1)} %get-tuple-element.32.send, bf16[192,256]{1,0:T(8,128)(2,1)S(1)} %get-tuple-element.33.take, bf16[384,64]{1,0:T(8,128)(2,1)S(1)} %get-tuple-element.34.take_rest, f32[72,2048]{1,0:T(8,128)S(1)} %get-tuple-element.37.rest_0_, ...), custom_call_target="tpu_custom_call" | custom-call | bytes 10485760 | tf_op jit(solution)/shard_map/row_unit_pack/pallas_call | solution.py:50
  77.3 7.3 %all-to-all-start.1 = ((f32[16,2,288,128]{3,2,1,0:T(8,128)}), f32[16,2,288,128]{3,2,1,0:T(8,128)}, u32[]{:S(2)}, u32[]{:S(2)}) async-start(f32[16,2,288,128]{3,2,1,0:T(8,128)} %bitcast.6), calls=%async_computation.1 | async-start | bytes 9437184 | tf_op jit(solution)/shard_map/all_to_all | solution.py:579
  84.7 4.8 %unit_row_pack.1 = (f32[72,2048]{1,0:T(8,128)S(1)}, f32[72,2048]{1,0:T(8,128)S(1)}, f32[72,2048]{1,0:T(8,128)S(1)}, f32[72,2048]{1,0:T(8,128)S(1)}, f32[72,2048]...) custom-call(s32[1,21]{1,0:T(1,128)S(1)} %get-tuple-element.31.take, ...), custom_call_target="tpu_custom_call" | custom-call | bytes 10485760 | tf_op jit(solution)/shard_map/unit_row_pack/pallas_call | solution.py:50
  89.4 3.3 %collective-permute-start.12 = (f32[144,2048]{1,0:T(8,128)S(1)}, f32[144,2048]{1,0:T(8,128)S(1)}, u32[]{:S(2)}, u32[]{:S(2)}) collective-permute-start(f32[144,2048]{1,0:T(8,128)S(1)} %get-tuple-element.52), channel_id=1, source_target_pairs={{0,64},{16,80},{32,96},{48,112},{64,0},{80,16},{96,32},{112,48},{1... | collective-permute-start | bytes 3538952 | tf_op jit(solution)/shard_map/ppermute | solution.py:569
  92.8 3.0 %collective-permute-start.11 = (f32[72,2048]{1,0:T(8,128)S(1)}, f32[72,2048]{1,0:T(8,128)S(1)}, u32[]{:S(2)}, u32[]{:S(2)}) collective-permute-start(f32[72,2048]{1,0:T(8,128)S(1)} %get-tuple-element.51), channel_id=1, source_target_pairs={{0,112},{16,96},{32,16},{48,0},{64,48},{80,32},{96,80},{112,64},{1... | collective-permute-start | bytes 1769480 | tf_op jit(solution)/shard_map/ppermute | solution.py:569
  95.7 24.2 %collective-permute-done.12.rest_6_ = f32[144,2048]{1,0:T(8,128)S(1)} collective-permute-done((f32[144,2048]{1,0:T(8,128)S(1)}, f32[144,2048]{1,0:T(8,128)S(1)}, u32[]{:S(2)}, u32[]{:S(2)}) %collective-permute-start.12) | collective-permute-done | bytes 1179680 | tf_op jit(solution)/shard_map/ppermute | solution.py:569
  119.9 3.4 %collective-permute-start.9 = (f32[72,2048]{1,0:T(8,128)S(1)}, f32[72,2048]{1,0:T(8,128)S(1)}, u32[]{:S(2)}, u32[]{:S(2)}) collective-permute-start(f32[72,2048]{1,0:T(8,128)S(1)} %get-tuple-element.49), channel_id=1, source_target_pairs={{0,96},{16,112},{32,0},{48,16},{64,32},{80,48},{96,64},{112,80},{1... | collective-permute-start | bytes 1769480 | tf_op jit(solution)/shard_map/ppermute | solution.py:569
  123.4 8.5 %collective-permute-done.10.rest_4_ = f32[72,2048]{1,0:T(8,128)S(1)} collective-permute-done((f32[72,2048]{1,0:T(8,128)S(1)}, f32[72,2048]{1,0:T(8,128)S(1)}, u32[]{:S(2)}, u32[]{:S(2)}) %collective-permute-start.10) | collective-permute-done | bytes 589856 | tf_op jit(solution)/shard_map/ppermute | solution.py:569
  132.6 0.1 pad_maximum_fusion.fixes
  132.6 11.6 %collective-permute-done.8.rest_2_ = f32[72,2048]{1,0:T(8,128)S(1)} collective-permute-done((f32[72,2048]{1,0:T(8,128)S(1)}, f32[72,2048]{1,0:T(8,128)S(1)}, u32[]{:S(2)}, u32[]{:S(2)}) %collective-permute-start.8) | collective-permute-done | bytes 589856 | tf_op jit(solution)/shard_map/ppermute | solution.py:569
  144.2 0.2 collective-permute-done.9.rest_3_
  144.5 3.5 %first_moment.1 = (f32[192,2688]{1,0:T(8,128)}, f32[11,192,128]{2,1,0:T(8,128)}) custom-call(f32[192,2688]{1,0:T(8,128)S(1)} %copy-done, bf16[192,256]{1,0:T(8,128)(2,1)S(1)} %get-tuple-element.33.take, bf16[384,64]{1,0:T(8,128)(2,1)S(1)} %get-tuple-element.34.take_rest, f32[72,2048]{1,0:T(8,128)S(1)} %get-tuple-element.46.rest_0_, ...), custom_call_target="tpu_custom_call" | custom-call | bytes 11534336 | tf_op jit(solution)/shard_map/first_moment/pallas_call | solution.py:50
  147.9 4.1 %all-to-all-done.1 = f32[16,2,288,128]{3,2,1,0:T(8,128)} async-done(((f32[16,2,288,128]{3,2,1,0:T(8,128)}), f32[16,2,288,128]{3,2,1,0:T(8,128)}, u32[]{:S(2)}, u32[]{:S(2)}) %all-to-all-start.1) | async-done | bytes 4718624 | tf_op jit(solution)/shard_map/all_to_all | solution.py:579
  152.0 7.3 %weight_update.1 = (f32[192,2688]{1,0:T(8,128)}, f32[192,2688]{1,0:T(8,128)}, f32[192,2688]{1,0:T(8,128)}) custom-call(s32[1,21]{1,0:T(1,128)S(1)} %get-tuple-element.31.take, f32[2]{0:T(128)S(1)} %pad_maximum_fusion.fixes, f32[32,288,128]{2,1,0:T(8,128)} %bitcast.5.recv, f32[192,2688]{1,0:T(8,128)} %get-tuple-element.28.first, ...), custom_call_target="tpu_custom_call" | custom-call | bytes 16777216 | tf_op jit(solution)/shard_map/weight_update/pallas_call | solution.py:50
  (19 shorter events, 0.1 us)
Async XLA Ops:
  0.6 0.7 copy-start.1
  5.7 7.4 %copy-start.2 = (s32[8,192]{1,0:T(8,128)S(1)}, s32[8,192]{1,0:T(8,128)}, u32[]{:S(2)}) copy-start(s32[8,192]{1,0:T(8,128)} %old.1) | copy-start | bytes 18436
  5.7 7.4 %copy-start.3 = (s32[8,192]{1,0:T(8,128)S(1)}, s32[8,192]{1,0:T(8,128)}, u32[]{:S(2)}) copy-start(s32[8,192]{1,0:T(8,128)} %new.1) | copy-start | bytes 18436
  5.7 71.6 %all-to-all-start = ((f32[16,2,288,128]{3,2,1,0:T(8,128)}), f32[16,2,288,128]{3,2,1,0:T(8,128)}, u32[]{:S(2)}, u32[]{:S(2)}) async-start(f32[16,2,288,128]{3,2,1,0:T(8,128)} %bitcast.7), calls=%async_computation | async-start | bytes 9437184 | tf_op jit(solution)/shard_map/all_to_all | solution.py:579
  18.9 30.9 %collective-permute-start.5 = (f32[144,2048]{1,0:T(8,128)S(1)}, f32[144,2048]{1,0:T(8,128)S(1)}, u32[]{:S(2)}, u32[]{:S(2)}) collective-permute-start(f32[144,2048]{1,0:T(8,128)S(1)} %get-tuple-element.43), channel_id=1, source_target_pairs={{0,64},{16,80},{32,96},{48,112},{64,0},{80,16},{96,32},{112,48},{1... | collective-permute-start | bytes 3538952 | tf_op jit(solution)/shard_map/ppermute | solution.py:569
  22.8 27.0 %collective-permute-start = (f32[72,2048]{1,0:T(8,128)S(1)}, f32[72,2048]{1,0:T(8,128)S(1)}, u32[]{:S(2)}, u32[]{:S(2)}) collective-permute-start(f32[72,2048]{1,0:T(8,128)S(1)} %get-tuple-element.38), channel_id=1, source_target_pairs={{0,16},{16,0},{32,48},{48,32},{64,80},{80,64},{96,112},{112,96},{1... | collective-permute-start | bytes 1769480 | tf_op jit(solution)/shard_map/ppermute | solution.py:569
  22.8 39.1 %collective-permute-start.1 = (f32[72,2048]{1,0:T(8,128)S(1)}, f32[72,2048]{1,0:T(8,128)S(1)}, u32[]{:S(2)}, u32[]{:S(2)}) collective-permute-start(f32[72,2048]{1,0:T(8,128)S(1)} %get-tuple-element.39), channel_id=1, source_target_pairs={{0,32},{16,48},{32,64},{48,80},{64,96},{80,112},{96,0},{112,16},{1... | collective-permute-start | bytes 1769480 | tf_op jit(solution)/shard_map/ppermute | solution.py:569
  23.9 39.6 %collective-permute-start.2 = (f32[72,2048]{1,0:T(8,128)S(1)}, f32[72,2048]{1,0:T(8,128)S(1)}, u32[]{:S(2)}, u32[]{:S(2)}) collective-permute-start(f32[72,2048]{1,0:T(8,128)S(1)} %get-tuple-element.40), channel_id=1, source_target_pairs={{0,96},{16,112},{32,0},{48,16},{64,32},{80,48},{96,64},{112,80},{1... | collective-permute-start | bytes 1769480 | tf_op jit(solution)/shard_map/ppermute | solution.py:569
  26.1 47.4 %collective-permute-start.3 = (f32[72,2048]{1,0:T(8,128)S(1)}, f32[72,2048]{1,0:T(8,128)S(1)}, u32[]{:S(2)}, u32[]{:S(2)}) collective-permute-start(f32[72,2048]{1,0:T(8,128)S(1)} %get-tuple-element.41), channel_id=1, source_target_pairs={{0,48},{16,32},{32,80},{48,64},{64,112},{80,96},{96,16},{112,0},{1... | collective-permute-start | bytes 1769480 | tf_op jit(solution)/shard_map/ppermute | solution.py:569
  49.8 23.7 %collective-permute-start.4 = (f32[72,2048]{1,0:T(8,128)S(1)}, f32[72,2048]{1,0:T(8,128)S(1)}, u32[]{:S(2)}, u32[]{:S(2)}) collective-permute-start(f32[72,2048]{1,0:T(8,128)S(1)} %get-tuple-element.42), channel_id=1, source_target_pairs={{0,112},{16,96},{32,16},{48,0},{64,48},{80,32},{96,80},{112,64},{1... | collective-permute-start | bytes 1769480 | tf_op jit(solution)/shard_map/ppermute | solution.py:569
  49.8 23.7 %collective-permute-start.6 = (f32[72,2048]{1,0:T(8,128)S(1)}, f32[72,2048]{1,0:T(8,128)S(1)}, u32[]{:S(2)}, u32[]{:S(2)}) collective-permute-start(f32[72,2048]{1,0:T(8,128)S(1)} %slice.8), channel_id=1, source_target_pairs={{0,16},{16,0},{32,48},{48,32},{64,80},{80,64},{96,112},{112,96},{1... | collective-permute-start | bytes 1769480 | tf_op jit(solution)/shard_map/ppermute | solution.py:569
  77.3 74.7 %all-to-all-start.1 = ((f32[16,2,288,128]{3,2,1,0:T(8,128)}), f32[16,2,288,128]{3,2,1,0:T(8,128)}, u32[]{:S(2)}, u32[]{:S(2)}) async-start(f32[16,2,288,128]{3,2,1,0:T(8,128)} %bitcast.6), calls=%async_computation.1 | async-start | bytes 9437184 | tf_op jit(solution)/shard_map/all_to_all | solution.py:579
  84.7 59.8 %copy-start = (f32[192,2688]{1,0:T(8,128)S(1)}, f32[192,2688]{1,0:T(8,128)}, u32[]{:S(2)}) copy-start(f32[192,2688]{1,0:T(8,128)} %gradient.3) | copy-start | bytes 6193156
  89.4 30.5 %collective-permute-start.12 = (f32[144,2048]{1,0:T(8,128)S(1)}, f32[144,2048]{1,0:T(8,128)S(1)}, u32[]{:S(2)}, u32[]{:S(2)}) collective-permute-start(f32[144,2048]{1,0:T(8,128)S(1)} %get-tuple-element.52), channel_id=1, source_target_pairs={{0,64},{16,80},{32,96},{48,112},{64,0},{80,16},{96,32},{112,48},{1... | collective-permute-start | bytes 3538952 | tf_op jit(solution)/shard_map/ppermute | solution.py:569
  92.8 39.1 %collective-permute-start.10 = (f32[72,2048]{1,0:T(8,128)S(1)}, f32[72,2048]{1,0:T(8,128)S(1)}, u32[]{:S(2)}, u32[]{:S(2)}) collective-permute-start(f32[72,2048]{1,0:T(8,128)S(1)} %get-tuple-element.50), channel_id=1, source_target_pairs={{0,48},{16,32},{32,80},{48,64},{64,112},{80,96},{96,16},{112,0},{1... | collective-permute-start | bytes 1769480 | tf_op jit(solution)/shard_map/ppermute | solution.py:569
  92.8 39.9 %collective-permute-start.11 = (f32[72,2048]{1,0:T(8,128)S(1)}, f32[72,2048]{1,0:T(8,128)S(1)}, u32[]{:S(2)}, u32[]{:S(2)}) collective-permute-start(f32[72,2048]{1,0:T(8,128)S(1)} %get-tuple-element.51), channel_id=1, source_target_pairs={{0,112},{16,96},{32,16},{48,0},{64,48},{80,32},{96,80},{112,64},{1... | collective-permute-start | bytes 1769480 | tf_op jit(solution)/shard_map/ppermute | solution.py:569
  95.7 36.9 %collective-permute-start.7 = (f32[72,2048]{1,0:T(8,128)S(1)}, f32[72,2048]{1,0:T(8,128)S(1)}, u32[]{:S(2)}, u32[]{:S(2)}) collective-permute-start(f32[72,2048]{1,0:T(8,128)S(1)} %get-tuple-element.47), channel_id=1, source_target_pairs={{0,16},{16,0},{32,48},{48,32},{64,80},{80,64},{96,112},{112,96},{1... | collective-permute-start | bytes 1769480 | tf_op jit(solution)/shard_map/ppermute | solution.py:569
  95.7 48.5 %collective-permute-start.8 = (f32[72,2048]{1,0:T(8,128)S(1)}, f32[72,2048]{1,0:T(8,128)S(1)}, u32[]{:S(2)}, u32[]{:S(2)}) collective-permute-start(f32[72,2048]{1,0:T(8,128)S(1)} %get-tuple-element.48), channel_id=1, source_target_pairs={{0,32},{16,48},{32,64},{48,80},{64,96},{80,112},{96,0},{112,16},{1... | collective-permute-start | bytes 1769480 | tf_op jit(solution)/shard_map/ppermute | solution.py:569
  119.9 24.6 %collective-permute-start.9 = (f32[72,2048]{1,0:T(8,128)S(1)}, f32[72,2048]{1,0:T(8,128)S(1)}, u32[]{:S(2)}, u32[]{:S(2)}) collective-permute-start(f32[72,2048]{1,0:T(8,128)S(1)} %get-tuple-element.49), channel_id=1, source_target_pairs={{0,96},{16,112},{32,0},{48,16},{64,32},{80,48},{96,64},{112,80},{1... | collective-permute-start | bytes 1769480 | tf_op jit(solution)/shard_map/ppermute | solution.py:569
  131.8 12.6 %collective-permute-start.13 = (f32[72,2048]{1,0:T(8,128)S(1)}, f32[72,2048]{1,0:T(8,128)S(1)}, u32[]{:S(2)}, u32[]{:S(2)}) collective-permute-start(f32[72,2048]{1,0:T(8,128)S(1)} %slice.9), channel_id=1, source_target_pairs={{0,16},{16,0},{32,48},{48,32},{64,80},{80,64},{96,112},{112,96},{1... | collective-permute-start | bytes 1769480 | tf_op jit(solution)/shard_map/ppermute | solution.py:569

commit v6 on v5

--- a/solution.py
+++ b/solution.py
@@ -526,13 +526,13 @@
         whole.wait(0, u)
         g = gradient_here[:, columns]
         second = beta_two * second + (1.0 - beta_two) * g * g
-        root = jnp.sqrt(second / fixes[1]) + epsilon
+        root = jnp.sqrt(second * fixes[1]) + epsilon
         whole.wait(1, u)
-        update = first_here[:, columns] / fixes[0] / root + decay_rate * weight
+        update = first_here[:, columns] * fixes[0] / root + decay_rate * weight
         for held, out, value in zip(helds, outs, (weight - learn_rate * update, second, update)):
             held[:, columns] = value
-            if u % SPAN == SPAN - 1:
-                span = span_of(u // SPAN)
+            if u % 3 == 2:
+                span = slice((u - 2) * UNIT, (u + 1) * UNIT)
                 stores.start(held.at[:, span], out.at[:, span])
     stores.wait()
 
@@ -552,7 +552,7 @@
             ARRAY,
             dma(2 * PARTS),
             dma(UNITS + 1),
-            dma(3 * PARTS),
+            dma(UNITS),
         ],
         16,
         take,
@@ -589,8 +589,8 @@
     count = step[0].astype(jnp.float32)
     fixes = jnp.stack(
         [
-            1.0 - jnp.power(jnp.float32(beta_one), count),
-            1.0 - jnp.power(jnp.float32(beta_two), count),
+            1.0 / (1.0 - jnp.power(jnp.float32(beta_one), count)),
+            1.0 / (1.0 - jnp.power(jnp.float32(beta_two), count)),
         ]
     )
 

time: 160 us -> 160 us (level)
  no operation moved by 1% of the time
where the time goes in v6:
time: 160 us; the launch traced here: 159 us
  waiting for transfers between devices  92.1 us (58%)
  starting transfers between devices  35.6 us (22%)
  Pallas kernels  29.3 us (18%)
  between operations  1.74 us (1%)
    ppermute x14, waiting for transfers between devices, move(): return lax.ppermute(part, 'dp', pairs)  87.7 us
    pallas_call x8, Pallas kernels, call(): pl.pallas_call(kernel, out_shape=out_shape, in_specs=ins, out_specs=outs,...  29.3 us
    ppermute x14, starting transfers between devices, move(): return lax.ppermute(part, 'dp', pairs)  20.9 us
    all_to_all x2, starting transfers between devices, swap_units(): lax.all_to_all(packed, 'mp', split_axis=0, concat_axis=0, tiled=True, axi...  14.6 us
    all_to_all x2, waiting for transfers between devices, swap_units(): lax.all_to_all(packed, 'mp', split_axis=0, concat_axis=0, tiled=True, axi...  4.33 us
  transfers between devices with their start and end apart: 16, of which 9 were waited for; matrix products, arithmetic and copies ran while one was open for 0% of the time, Pallas kernels for 11%

profile of v6, /device:TPU:12, one launch (start us, length us, event | category | flops | bytes accessed | tf_op | source)
XLA Modules:
  0.0 159.5 jit_solution(4633695032235521260)
XLA Ops:
  0.6 0.7 copy-done.1
  1.3 0.2 unit_plan.1
  1.5 4.2 %unit_pack.1 = f32[32,288,128]{2,1,0:T(8,128)} custom-call(s32[1,128]{1,0:T(1,128)S(1)} %get-tuple-element.32.send, f32[192,2688]{1,0:T(8,128)} %whole.2, f32[192,2688]{1,0:T(8,128)} %half.3), custom_call_target="tpu_custom_call" | custom-call | bytes 9437184 | tf_op jit(solution)/shard_map/unit_pack/pallas_call | solution.py:50
  5.7 0.0 copy-start.2
  5.8 0.0 copy-start.3
  5.8 7.4 %all-to-all-start = ((f32[16,2,288,128]{3,2,1,0:T(8,128)}), f32[16,2,288,128]{3,2,1,0:T(8,128)}, u32[]{:S(2)}, u32[]{:S(2)}) async-start(f32[16,2,288,128]{3,2,1,0:T(8,128)} %bitcast.7), calls=%async_computation | async-start | bytes 9437184 | tf_op jit(solution)/shard_map/all_to_all | solution.py:579
  13.2 1.3 row_plan.1
  14.4 4.5 %row_pack.1 = (f32[72,2048]{1,0:T(8,128)S(1)}, f32[72,2048]{1,0:T(8,128)S(1)}, f32[72,2048]{1,0:T(8,128)S(1)}, f32[72,2048]{1,0:T(8,128)S(1)}, f32[72,2048]{1,0:...) custom-call(bf16[256,192]{1,0:T(8,128)(2,1)S(1)} %get-tuple-element.35.pack, ...), custom_call_target="tpu_custom_call" | custom-call | bytes 9437184 | tf_op jit(solution)/shard_map/row_pack/pallas_call | solution.py:50
  19.0 4.0 %collective-permute-start.5 = (f32[144,2048]{1,0:T(8,128)S(1)}, f32[144,2048]{1,0:T(8,128)S(1)}, u32[]{:S(2)}, u32[]{:S(2)}) collective-permute-start(f32[144,2048]{1,0:T(8,128)S(1)} %get-tuple-element.43), channel_id=1, source_target_pairs={{0,64},{16,80},{32,96},{48,112},{64,0},{80,16},{96,32},{112,48},{1... | collective-permute-start | bytes 3538952 | tf_op jit(solution)/shard_map/ppermute | solution.py:569
  22.9 1.0 collective-permute-start.1
  23.9 2.2 %collective-permute-start.2 = (f32[72,2048]{1,0:T(8,128)S(1)}, f32[72,2048]{1,0:T(8,128)S(1)}, u32[]{:S(2)}, u32[]{:S(2)}) collective-permute-start(f32[72,2048]{1,0:T(8,128)S(1)} %get-tuple-element.40), channel_id=1, source_target_pairs={{0,96},{16,112},{32,0},{48,16},{64,32},{80,48},{96,64},{112,80},{1... | collective-permute-start | bytes 1769480 | tf_op jit(solution)/shard_map/ppermute | solution.py:569
  26.2 0.0 collective-permute-start.3
  26.2 23.7 %collective-permute-done.5.rest_6_ = f32[144,2048]{1,0:T(8,128)S(1)} collective-permute-done((f32[144,2048]{1,0:T(8,128)S(1)}, f32[144,2048]{1,0:T(8,128)S(1)}, u32[]{:S(2)}, u32[]{:S(2)}) %collective-permute-start.5) | collective-permute-done | bytes 1179680 | tf_op jit(solution)/shard_map/ppermute | solution.py:569
  49.9 3.9 %collective-permute-start.6 = (f32[72,2048]{1,0:T(8,128)S(1)}, f32[72,2048]{1,0:T(8,128)S(1)}, u32[]{:S(2)}, u32[]{:S(2)}) collective-permute-start(f32[72,2048]{1,0:T(8,128)S(1)} %slice.8), channel_id=1, source_target_pairs={{0,16},{16,0},{32,48},{48,32},{64,80},{80,64},{96,112},{112,96},{1... | collective-permute-start | bytes 1769480 | tf_op jit(solution)/shard_map/ppermute | solution.py:569
  53.8 8.2 %collective-permute-done.1.rest_2_ = f32[72,2048]{1,0:T(8,128)S(1)} collective-permute-done((f32[72,2048]{1,0:T(8,128)S(1)}, f32[72,2048]{1,0:T(8,128)S(1)}, u32[]{:S(2)}, u32[]{:S(2)}) %collective-permute-start.1) | collective-permute-done | bytes 589856 | tf_op jit(solution)/shard_map/ppermute | solution.py:569
  62.0 1.5 collective-permute-done.2.rest_3_
  63.5 10.1 %collective-permute-done.3.rest_4_ = f32[72,2048]{1,0:T(8,128)S(1)} collective-permute-done((f32[72,2048]{1,0:T(8,128)S(1)}, f32[72,2048]{1,0:T(8,128)S(1)}, u32[]{:S(2)}, u32[]{:S(2)}) %collective-permute-start.3) | collective-permute-done | bytes 589856 | tf_op jit(solution)/shard_map/ppermute | solution.py:569
  73.6 3.8 %row_unit_pack.1 = f32[32,288,128]{2,1,0:T(8,128)} custom-call(s32[1,128]{1,0:T(1,128)S(1)} %get-tuple-element.32.send, bf16[192,256]{1,0:T(8,128)(2,1)S(1)} %get-tuple-element.33.take, bf16[384,64]{1,0:T(8,128)(2,1)S(1)} %get-tuple-element.34.take_rest, f32[72,2048]{1,0:T(8,128)S(1)} %get-tuple-element.37.rest_0_, ...), custom_call_target="tpu_custom_call" | custom-call | bytes 10485760 | tf_op jit(solution)/shard_map/row_unit_pack/pallas_call | solution.py:50
  77.4 7.2 %all-to-all-start.1 = ((f32[16,2,288,128]{3,2,1,0:T(8,128)}), f32[16,2,288,128]{3,2,1,0:T(8,128)}, u32[]{:S(2)}, u32[]{:S(2)}) async-start(f32[16,2,288,128]{3,2,1,0:T(8,128)} %bitcast.6), calls=%async_computation.1 | async-start | bytes 9437184 | tf_op jit(solution)/shard_map/all_to_all | solution.py:579
  84.6 4.8 %unit_row_pack.1 = (f32[72,2048]{1,0:T(8,128)S(1)}, f32[72,2048]{1,0:T(8,128)S(1)}, f32[72,2048]{1,0:T(8,128)S(1)}, f32[72,2048]{1,0:T(8,128)S(1)}, f32[72,2048]...) custom-call(s32[1,21]{1,0:T(1,128)S(1)} %get-tuple-element.31.take, ...), custom_call_target="tpu_custom_call" | custom-call | bytes 10485760 | tf_op jit(solution)/shard_map/unit_row_pack/pallas_call | solution.py:50
  89.4 3.4 %collective-permute-start.12 = (f32[144,2048]{1,0:T(8,128)S(1)}, f32[144,2048]{1,0:T(8,128)S(1)}, u32[]{:S(2)}, u32[]{:S(2)}) collective-permute-start(f32[144,2048]{1,0:T(8,128)S(1)} %get-tuple-element.52), channel_id=1, source_target_pairs={{0,64},{16,80},{32,96},{48,112},{64,0},{80,16},{96,32},{112,48},{1... | collective-permute-start | bytes 3538952 | tf_op jit(solution)/shard_map/ppermute | solution.py:569
  92.8 3.0 %collective-permute-start.11 = (f32[72,2048]{1,0:T(8,128)S(1)}, f32[72,2048]{1,0:T(8,128)S(1)}, u32[]{:S(2)}, u32[]{:S(2)}) collective-permute-start(f32[72,2048]{1,0:T(8,128)S(1)} %get-tuple-element.51), channel_id=1, source_target_pairs={{0,112},{16,96},{32,16},{48,0},{64,48},{80,32},{96,80},{112,64},{1... | collective-permute-start | bytes 1769480 | tf_op jit(solution)/shard_map/ppermute | solution.py:569
  95.7 24.1 %collective-permute-done.12.rest_6_ = f32[144,2048]{1,0:T(8,128)S(1)} collective-permute-done((f32[144,2048]{1,0:T(8,128)S(1)}, f32[144,2048]{1,0:T(8,128)S(1)}, u32[]{:S(2)}, u32[]{:S(2)}) %collective-permute-start.12) | collective-permute-done | bytes 1179680 | tf_op jit(solution)/shard_map/ppermute | solution.py:569
  119.9 3.5 %collective-permute-start.9 = (f32[72,2048]{1,0:T(8,128)S(1)}, f32[72,2048]{1,0:T(8,128)S(1)}, u32[]{:S(2)}, u32[]{:S(2)}) collective-permute-start(f32[72,2048]{1,0:T(8,128)S(1)} %get-tuple-element.49), channel_id=1, source_target_pairs={{0,96},{16,112},{32,0},{48,16},{64,32},{80,48},{96,64},{112,80},{1... | collective-permute-start | bytes 1769480 | tf_op jit(solution)/shard_map/ppermute | solution.py:569
  123.4 8.5 %collective-permute-done.10.rest_4_ = f32[72,2048]{1,0:T(8,128)S(1)} collective-permute-done((f32[72,2048]{1,0:T(8,128)S(1)}, f32[72,2048]{1,0:T(8,128)S(1)}, u32[]{:S(2)}, u32[]{:S(2)}) %collective-permute-start.10) | collective-permute-done | bytes 589856 | tf_op jit(solution)/shard_map/ppermute | solution.py:569
  131.8 0.1 collective-permute-start.13
  132.7 0.1 pad_maximum_fusion.fixes
  132.8 11.5 %collective-permute-done.8.rest_2_ = f32[72,2048]{1,0:T(8,128)S(1)} collective-permute-done((f32[72,2048]{1,0:T(8,128)S(1)}, f32[72,2048]{1,0:T(8,128)S(1)}, u32[]{:S(2)}, u32[]{:S(2)}) %collective-permute-start.8) | collective-permute-done | bytes 589856 | tf_op jit(solution)/shard_map/ppermute | solution.py:569
  144.3 0.2 collective-permute-done.9.rest_3_
  144.5 3.5 %first_moment.1 = (f32[192,2688]{1,0:T(8,128)}, f32[11,192,128]{2,1,0:T(8,128)}) custom-call(f32[192,2688]{1,0:T(8,128)S(1)} %copy-done, bf16[192,256]{1,0:T(8,128)(2,1)S(1)} %get-tuple-element.33.take, bf16[384,64]{1,0:T(8,128)(2,1)S(1)} %get-tuple-element.34.take_rest, f32[72,2048]{1,0:T(8,128)S(1)} %get-tuple-element.46.rest_0_, ...), custom_call_target="tpu_custom_call" | custom-call | bytes 11534336 | tf_op jit(solution)/shard_map/first_moment/pallas_call | solution.py:50
  147.9 4.3 %all-to-all-done.1 = f32[16,2,288,128]{3,2,1,0:T(8,128)} async-done(((f32[16,2,288,128]{3,2,1,0:T(8,128)}), f32[16,2,288,128]{3,2,1,0:T(8,128)}, u32[]{:S(2)}, u32[]{:S(2)}) %all-to-all-start.1) | async-done | bytes 4718624 | tf_op jit(solution)/shard_map/all_to_all | solution.py:579
  152.3 7.1 %weight_update.1 = (f32[192,2688]{1,0:T(8,128)}, f32[192,2688]{1,0:T(8,128)}, f32[192,2688]{1,0:T(8,128)}) custom-call(s32[1,21]{1,0:T(1,128)S(1)} %get-tuple-element.31.take, f32[2]{0:T(128)S(1)} %pad_maximum_fusion.fixes, f32[32,288,128]{2,1,0:T(8,128)} %bitcast.5.recv, f32[192,2688]{1,0:T(8,128)} %get-tuple-element.28.first, ...), custom_call_target="tpu_custom_call" | custom-call | bytes 16777216 | tf_op jit(solution)/shard_map/weight_update/pallas_call | solution.py:50
  (19 shorter events, 0.1 us)
Async XLA Ops:
  0.6 0.7 copy-start.1
  5.7 7.4 %copy-start.2 = (s32[8,192]{1,0:T(8,128)S(1)}, s32[8,192]{1,0:T(8,128)}, u32[]{:S(2)}) copy-start(s32[8,192]{1,0:T(8,128)} %old.1) | copy-start | bytes 18436
  5.8 7.4 %copy-start.3 = (s32[8,192]{1,0:T(8,128)S(1)}, s32[8,192]{1,0:T(8,128)}, u32[]{:S(2)}) copy-start(s32[8,192]{1,0:T(8,128)} %new.1) | copy-start | bytes 18436
  5.8 71.6 %all-to-all-start = ((f32[16,2,288,128]{3,2,1,0:T(8,128)}), f32[16,2,288,128]{3,2,1,0:T(8,128)}, u32[]{:S(2)}, u32[]{:S(2)}) async-start(f32[16,2,288,128]{3,2,1,0:T(8,128)} %bitcast.7), calls=%async_computation | async-start | bytes 9437184 | tf_op jit(solution)/shard_map/all_to_all | solution.py:579
  19.0 30.9 %collective-permute-start.5 = (f32[144,2048]{1,0:T(8,128)S(1)}, f32[144,2048]{1,0:T(8,128)S(1)}, u32[]{:S(2)}, u32[]{:S(2)}) collective-permute-start(f32[144,2048]{1,0:T(8,128)S(1)} %get-tuple-element.43), channel_id=1, source_target_pairs={{0,64},{16,80},{32,96},{48,112},{64,0},{80,16},{96,32},{112,48},{1... | collective-permute-start | bytes 3538952 | tf_op jit(solution)/shard_map/ppermute | solution.py:569
  22.9 27.0 %collective-permute-start = (f32[72,2048]{1,0:T(8,128)S(1)}, f32[72,2048]{1,0:T(8,128)S(1)}, u32[]{:S(2)}, u32[]{:S(2)}) collective-permute-start(f32[72,2048]{1,0:T(8,128)S(1)} %get-tuple-element.38), channel_id=1, source_target_pairs={{0,16},{16,0},{32,48},{48,32},{64,80},{80,64},{96,112},{112,96},{1... | collective-permute-start | bytes 1769480 | tf_op jit(solution)/shard_map/ppermute | solution.py:569
  22.9 39.1 %collective-permute-start.1 = (f32[72,2048]{1,0:T(8,128)S(1)}, f32[72,2048]{1,0:T(8,128)S(1)}, u32[]{:S(2)}, u32[]{:S(2)}) collective-permute-start(f32[72,2048]{1,0:T(8,128)S(1)} %get-tuple-element.39), channel_id=1, source_target_pairs={{0,32},{16,48},{32,64},{48,80},{64,96},{80,112},{96,0},{112,16},{1... | collective-permute-start | bytes 1769480 | tf_op jit(solution)/shard_map/ppermute | solution.py:569
  23.9 39.6 %collective-permute-start.2 = (f32[72,2048]{1,0:T(8,128)S(1)}, f32[72,2048]{1,0:T(8,128)S(1)}, u32[]{:S(2)}, u32[]{:S(2)}) collective-permute-start(f32[72,2048]{1,0:T(8,128)S(1)} %get-tuple-element.40), channel_id=1, source_target_pairs={{0,96},{16,112},{32,0},{48,16},{64,32},{80,48},{96,64},{112,80},{1... | collective-permute-start | bytes 1769480 | tf_op jit(solution)/shard_map/ppermute | solution.py:569
  26.2 47.4 %collective-permute-start.3 = (f32[72,2048]{1,0:T(8,128)S(1)}, f32[72,2048]{1,0:T(8,128)S(1)}, u32[]{:S(2)}, u32[]{:S(2)}) collective-permute-start(f32[72,2048]{1,0:T(8,128)S(1)} %get-tuple-element.41), channel_id=1, source_target_pairs={{0,48},{16,32},{32,80},{48,64},{64,112},{80,96},{96,16},{112,0},{1... | collective-permute-start | bytes 1769480 | tf_op jit(solution)/shard_map/ppermute | solution.py:569
  49.8 23.7 %collective-permute-start.4 = (f32[72,2048]{1,0:T(8,128)S(1)}, f32[72,2048]{1,0:T(8,128)S(1)}, u32[]{:S(2)}, u32[]{:S(2)}) collective-permute-start(f32[72,2048]{1,0:T(8,128)S(1)} %get-tuple-element.42), channel_id=1, source_target_pairs={{0,112},{16,96},{32,16},{48,0},{64,48},{80,32},{96,80},{112,64},{1... | collective-permute-start | bytes 1769480 | tf_op jit(solution)/shard_map/ppermute | solution.py:569
  49.9 23.7 %collective-permute-start.6 = (f32[72,2048]{1,0:T(8,128)S(1)}, f32[72,2048]{1,0:T(8,128)S(1)}, u32[]{:S(2)}, u32[]{:S(2)}) collective-permute-start(f32[72,2048]{1,0:T(8,128)S(1)} %slice.8), channel_id=1, source_target_pairs={{0,16},{16,0},{32,48},{48,32},{64,80},{80,64},{96,112},{112,96},{1... | collective-permute-start | bytes 1769480 | tf_op jit(solution)/shard_map/ppermute | solution.py:569
  77.4 74.9 %all-to-all-start.1 = ((f32[16,2,288,128]{3,2,1,0:T(8,128)}), f32[16,2,288,128]{3,2,1,0:T(8,128)}, u32[]{:S(2)}, u32[]{:S(2)}) async-start(f32[16,2,288,128]{3,2,1,0:T(8,128)} %bitcast.6), calls=%async_computation.1 | async-start | bytes 9437184 | tf_op jit(solution)/shard_map/all_to_all | solution.py:579
  84.6 59.8 %copy-start = (f32[192,2688]{1,0:T(8,128)S(1)}, f32[192,2688]{1,0:T(8,128)}, u32[]{:S(2)}) copy-start(f32[192,2688]{1,0:T(8,128)} %gradient.3) | copy-start | bytes 6193156
  89.4 30.4 %collective-permute-start.12 = (f32[144,2048]{1,0:T(8,128)S(1)}, f32[144,2048]{1,0:T(8,128)S(1)}, u32[]{:S(2)}, u32[]{:S(2)}) collective-permute-start(f32[144,2048]{1,0:T(8,128)S(1)} %get-tuple-element.52), channel_id=1, source_target_pairs={{0,64},{16,80},{32,96},{48,112},{64,0},{80,16},{96,32},{112,48},{1... | collective-permute-start | bytes 3538952 | tf_op jit(solution)/shard_map/ppermute | solution.py:569
  92.8 39.1 %collective-permute-start.10 = (f32[72,2048]{1,0:T(8,128)S(1)}, f32[72,2048]{1,0:T(8,128)S(1)}, u32[]{:S(2)}, u32[]{:S(2)}) collective-permute-start(f32[72,2048]{1,0:T(8,128)S(1)} %get-tuple-element.50), channel_id=1, source_target_pairs={{0,48},{16,32},{32,80},{48,64},{64,112},{80,96},{96,16},{112,0},{1... | collective-permute-start | bytes 1769480 | tf_op jit(solution)/shard_map/ppermute | solution.py:569
  92.8 40.0 %collective-permute-start.11 = (f32[72,2048]{1,0:T(8,128)S(1)}, f32[72,2048]{1,0:T(8,128)S(1)}, u32[]{:S(2)}, u32[]{:S(2)}) collective-permute-start(f32[72,2048]{1,0:T(8,128)S(1)} %get-tuple-element.51), channel_id=1, source_target_pairs={{0,112},{16,96},{32,16},{48,0},{64,48},{80,32},{96,80},{112,64},{1... | collective-permute-start | bytes 1769480 | tf_op jit(solution)/shard_map/ppermute | solution.py:569
  95.7 37.0 %collective-permute-start.7 = (f32[72,2048]{1,0:T(8,128)S(1)}, f32[72,2048]{1,0:T(8,128)S(1)}, u32[]{:S(2)}, u32[]{:S(2)}) collective-permute-start(f32[72,2048]{1,0:T(8,128)S(1)} %get-tuple-element.47), channel_id=1, source_target_pairs={{0,16},{16,0},{32,48},{48,32},{64,80},{80,64},{96,112},{112,96},{1... | collective-permute-start | bytes 1769480 | tf_op jit(solution)/shard_map/ppermute | solution.py:569
  95.7 48.6 %collective-permute-start.8 = (f32[72,2048]{1,0:T(8,128)S(1)}, f32[72,2048]{1,0:T(8,128)S(1)}, u32[]{:S(2)}, u32[]{:S(2)}) collective-permute-start(f32[72,2048]{1,0:T(8,128)S(1)} %get-tuple-element.48), channel_id=1, source_target_pairs={{0,32},{16,48},{32,64},{48,80},{64,96},{80,112},{96,0},{112,16},{1... | collective-permute-start | bytes 1769480 | tf_op jit(solution)/shard_map/ppermute | solution.py:569
  119.9 24.6 %collective-permute-start.9 = (f32[72,2048]{1,0:T(8,128)S(1)}, f32[72,2048]{1,0:T(8,128)S(1)}, u32[]{:S(2)}, u32[]{:S(2)}) collective-permute-start(f32[72,2048]{1,0:T(8,128)S(1)} %get-tuple-element.49), channel_id=1, source_target_pairs={{0,96},{16,112},{32,0},{48,16},{64,32},{80,48},{96,64},{112,80},{1... | collective-permute-start | bytes 1769480 | tf_op jit(solution)/shard_map/ppermute | solution.py:569
  131.8 12.6 %collective-permute-start.13 = (f32[72,2048]{1,0:T(8,128)S(1)}, f32[72,2048]{1,0:T(8,128)S(1)}, u32[]{:S(2)}, u32[]{:S(2)}) collective-permute-start(f32[72,2048]{1,0:T(8,128)S(1)} %slice.9), channel_id=1, source_target_pairs={{0,16},{16,0},{32,48},{48,32},{64,80},{80,64},{96,112},{112,96},{1... | collective-permute-start | bytes 1769480 | tf_op jit(solution)/shard_map/ppermute | solution.py:569

commit v7 on v6

--- a/solution.py
+++ b/solution.py
@@ -34,7 +34,7 @@
 learn_rate = 0.001
 decay_rate = 0.1
 
-MOVES = [(0, 0), (0, 1), (1, 0), (3, 0), (1, 1), (3, 1), (2, 0), (2, 1)]
+MOVES = [(0, 0), (1, 0), (3, 0), (1, 1), (3, 1), (0, 1), (2, 0), (2, 1)]
 SINGLE = 6
 HBM = pl.BlockSpec(memory_space=pltpu.HBM)
 ANY = pl.BlockSpec(memory_space=pl.ANY)

time: 160 us -> 160 us (level)
  transfers between devices with their start and end apart: 16 -> 16, of which waited for: 9 -> 8; matrix products, arithmetic and copies ran while one was open for 0% -> 0% of each run, Pallas kernels for 11% -> 11%
where the time goes in v7:
time: 160 us; the launch traced here: 159 us
  waiting for transfers between devices  92.7 us (58%)
  starting transfers between devices  34.9 us (22%)
  Pallas kernels  29.3 us (18%)
  between operations  1.74 us (1%)
    ppermute x14, waiting for transfers between devices, move(): return lax.ppermute(part, 'dp', pairs)  88.3 us
    pallas_call x8, Pallas kernels, call(): pl.pallas_call(kernel, out_shape=out_shape, in_specs=ins, out_specs=outs,...  29.3 us
    ppermute x14, starting transfers between devices, move(): return lax.ppermute(part, 'dp', pairs)  20.3 us
    all_to_all x2, starting transfers between devices, swap_units(): lax.all_to_all(packed, 'mp', split_axis=0, concat_axis=0, tiled=True, axi...  14.6 us
    all_to_all x2, waiting for transfers between devices, swap_units(): lax.all_to_all(packed, 'mp', split_axis=0, concat_axis=0, tiled=True, axi...  4.38 us
  transfers between devices with their start and end apart: 16, of which 8 were waited for; matrix products, arithmetic and copies ran while one was open for 0% of the time, Pallas kernels for 11%

profile of v7, /device:TPU:12, one launch (start us, length us, event | category | flops | bytes accessed | tf_op | source)
XLA Modules:
  0.0 159.5 jit_solution(2021481846385000744)
XLA Ops:
  0.6 0.7 copy-done.1
  1.3 0.2 unit_plan.1
  1.5 4.2 %unit_pack.1 = f32[32,288,128]{2,1,0:T(8,128)} custom-call(s32[1,128]{1,0:T(1,128)S(1)} %get-tuple-element.32.send, f32[192,2688]{1,0:T(8,128)} %whole.2, f32[192,2688]{1,0:T(8,128)} %half.3), custom_call_target="tpu_custom_call" | custom-call | bytes 9437184 | tf_op jit(solution)/shard_map/unit_pack/pallas_call | solution.py:50
  5.7 0.0 copy-start.2
  5.7 0.0 copy-start.3
  5.8 7.3 %all-to-all-start = ((f32[16,2,288,128]{3,2,1,0:T(8,128)}), f32[16,2,288,128]{3,2,1,0:T(8,128)}, u32[]{:S(2)}, u32[]{:S(2)}) async-start(f32[16,2,288,128]{3,2,1,0:T(8,128)} %bitcast.7), calls=%async_computation | async-start | bytes 9437184 | tf_op jit(solution)/shard_map/all_to_all | solution.py:579
  13.1 1.3 row_plan.1
  14.4 4.5 %row_pack.1 = (f32[72,2048]{1,0:T(8,128)S(1)}, f32[72,2048]{1,0:T(8,128)S(1)}, f32[72,2048]{1,0:T(8,128)S(1)}, f32[72,2048]{1,0:T(8,128)S(1)}, f32[72,2048]{1,0:...) custom-call(bf16[256,192]{1,0:T(8,128)(2,1)S(1)} %get-tuple-element.35.pack, ...), custom_call_target="tpu_custom_call" | custom-call | bytes 9437184 | tf_op jit(solution)/shard_map/row_pack/pallas_call | solution.py:50
  18.9 4.0 %collective-permute-start.5 = (f32[144,2048]{1,0:T(8,128)S(1)}, f32[144,2048]{1,0:T(8,128)S(1)}, u32[]{:S(2)}, u32[]{:S(2)}) collective-permute-start(f32[144,2048]{1,0:T(8,128)S(1)} %get-tuple-element.43), channel_id=1, source_target_pairs={{0,64},{16,80},{32,96},{48,112},{64,0},{80,16},{96,32},{112,48},{1... | collective-permute-start | bytes 3538952 | tf_op jit(solution)/shard_map/ppermute | solution.py:569
  22.9 1.0 collective-permute-start
  23.9 2.2 %collective-permute-start.1 = (f32[72,2048]{1,0:T(8,128)S(1)}, f32[72,2048]{1,0:T(8,128)S(1)}, u32[]{:S(2)}, u32[]{:S(2)}) collective-permute-start(f32[72,2048]{1,0:T(8,128)S(1)} %get-tuple-element.39), channel_id=1, source_target_pairs={{0,96},{16,112},{32,0},{48,16},{64,32},{80,48},{96,64},{112,80},{1... | collective-permute-start | bytes 1769480 | tf_op jit(solution)/shard_map/ppermute | solution.py:569
  26.1 3.0 %collective-permute-start.3 = (f32[72,2048]{1,0:T(8,128)S(1)}, f32[72,2048]{1,0:T(8,128)S(1)}, u32[]{:S(2)}, u32[]{:S(2)}) collective-permute-start(f32[72,2048]{1,0:T(8,128)S(1)} %get-tuple-element.41), channel_id=1, source_target_pairs={{0,112},{16,96},{32,16},{48,0},{64,48},{80,32},{96,80},{112,64},{1... | collective-permute-start | bytes 1769480 | tf_op jit(solution)/shard_map/ppermute | solution.py:569
  29.1 20.7 %collective-permute-done.5.rest_6_ = f32[144,2048]{1,0:T(8,128)S(1)} collective-permute-done((f32[144,2048]{1,0:T(8,128)S(1)}, f32[144,2048]{1,0:T(8,128)S(1)}, u32[]{:S(2)}, u32[]{:S(2)}) %collective-permute-start.5) | collective-permute-done | bytes 1179680 | tf_op jit(solution)/shard_map/ppermute | solution.py:569
  49.8 12.1 %collective-permute-done.rest_1_ = f32[72,2048]{1,0:T(8,128)S(1)} collective-permute-done((f32[72,2048]{1,0:T(8,128)S(1)}, f32[72,2048]{1,0:T(8,128)S(1)}, u32[]{:S(2)}, u32[]{:S(2)}) %collective-permute-start) | collective-permute-done | bytes 589856 | tf_op jit(solution)/shard_map/ppermute | solution.py:569
  61.9 1.5 collective-permute-done.1.rest_2_
  63.5 10.0 %collective-permute-done.2.rest_3_ = f32[72,2048]{1,0:T(8,128)S(1)} collective-permute-done((f32[72,2048]{1,0:T(8,128)S(1)}, f32[72,2048]{1,0:T(8,128)S(1)}, u32[]{:S(2)}, u32[]{:S(2)}) %collective-permute-start.2) | collective-permute-done | bytes 589856 | tf_op jit(solution)/shard_map/ppermute | solution.py:569
  73.5 3.8 %row_unit_pack.1 = f32[32,288,128]{2,1,0:T(8,128)} custom-call(s32[1,128]{1,0:T(1,128)S(1)} %get-tuple-element.32.send, bf16[192,256]{1,0:T(8,128)(2,1)S(1)} %get-tuple-element.33.take, bf16[384,64]{1,0:T(8,128)(2,1)S(1)} %get-tuple-element.34.take_rest, f32[72,2048]{1,0:T(8,128)S(1)} %get-tuple-element.37.rest_0_, ...), custom_call_target="tpu_custom_call" | custom-call | bytes 10485760 | tf_op jit(solution)/shard_map/row_unit_pack/pallas_call | solution.py:50
  77.3 7.2 %all-to-all-start.1 = ((f32[16,2,288,128]{3,2,1,0:T(8,128)}), f32[16,2,288,128]{3,2,1,0:T(8,128)}, u32[]{:S(2)}, u32[]{:S(2)}) async-start(f32[16,2,288,128]{3,2,1,0:T(8,128)} %bitcast.6), calls=%async_computation.1 | async-start | bytes 9437184 | tf_op jit(solution)/shard_map/all_to_all | solution.py:579
  84.6 4.8 %unit_row_pack.1 = (f32[72,2048]{1,0:T(8,128)S(1)}, f32[72,2048]{1,0:T(8,128)S(1)}, f32[72,2048]{1,0:T(8,128)S(1)}, f32[72,2048]{1,0:T(8,128)S(1)}, f32[72,2048]...) custom-call(s32[1,21]{1,0:T(1,128)S(1)} %get-tuple-element.31.take, ...), custom_call_target="tpu_custom_call" | custom-call | bytes 10485760 | tf_op jit(solution)/shard_map/unit_row_pack/pallas_call | solution.py:50
  89.3 2.8 %collective-permute-start.12 = (f32[144,2048]{1,0:T(8,128)S(1)}, f32[144,2048]{1,0:T(8,128)S(1)}, u32[]{:S(2)}, u32[]{:S(2)}) collective-permute-start(f32[144,2048]{1,0:T(8,128)S(1)} %get-tuple-element.52), channel_id=1, source_target_pairs={{0,64},{16,80},{32,96},{48,112},{64,0},{80,16},{96,32},{112,48},{1... | collective-permute-start | bytes 3538952 | tf_op jit(solution)/shard_map/ppermute | solution.py:569
  92.2 0.5 collective-permute-start.10
  92.7 0.8 collective-permute-start.11
  93.5 0.8 collective-permute-start.7
  94.3 2.4 %collective-permute-start.8 = (f32[72,2048]{1,0:T(8,128)S(1)}, f32[72,2048]{1,0:T(8,128)S(1)}, u32[]{:S(2)}, u32[]{:S(2)}) collective-permute-start(f32[72,2048]{1,0:T(8,128)S(1)} %get-tuple-element.48), channel_id=1, source_target_pairs={{0,96},{16,112},{32,0},{48,16},{64,32},{80,48},{96,64},{112,80},{1... | collective-permute-start | bytes 1769480 | tf_op jit(solution)/shard_map/ppermute | solution.py:569
  96.7 23.0 %collective-permute-done.12.rest_6_ = f32[144,2048]{1,0:T(8,128)S(1)} collective-permute-done((f32[144,2048]{1,0:T(8,128)S(1)}, f32[144,2048]{1,0:T(8,128)S(1)}, u32[]{:S(2)}, u32[]{:S(2)}) %collective-permute-start.12) | collective-permute-done | bytes 1179680 | tf_op jit(solution)/shard_map/ppermute | solution.py:569
  119.8 10.9 %collective-permute-done.10.rest_4_ = f32[72,2048]{1,0:T(8,128)S(1)} collective-permute-done((f32[72,2048]{1,0:T(8,128)S(1)}, f32[72,2048]{1,0:T(8,128)S(1)}, u32[]{:S(2)}, u32[]{:S(2)}) %collective-permute-start.10) | collective-permute-done | bytes 589856 | tf_op jit(solution)/shard_map/ppermute | solution.py:569
  130.7 2.8 %collective-permute-start.13 = (f32[72,2048]{1,0:T(8,128)S(1)}, f32[72,2048]{1,0:T(8,128)S(1)}, u32[]{:S(2)}, u32[]{:S(2)}) collective-permute-start(f32[72,2048]{1,0:T(8,128)S(1)} %slice.9), channel_id=1, source_target_pairs={{0,16},{16,0},{32,48},{48,32},{64,80},{80,64},{96,112},{112,96},{1... | collective-permute-start | bytes 1769480 | tf_op jit(solution)/shard_map/ppermute | solution.py:569
  134.3 0.1 pad_maximum_fusion.fixes
  134.3 10.1 %collective-permute-done.8.rest_2_ = f32[72,2048]{1,0:T(8,128)S(1)} collective-permute-done((f32[72,2048]{1,0:T(8,128)S(1)}, f32[72,2048]{1,0:T(8,128)S(1)}, u32[]{:S(2)}, u32[]{:S(2)}) %collective-permute-start.8) | collective-permute-done | bytes 589856 | tf_op jit(solution)/shard_map/ppermute | solution.py:569
  144.4 3.5 %first_moment.1 = (f32[192,2688]{1,0:T(8,128)}, f32[11,192,128]{2,1,0:T(8,128)}) custom-call(f32[192,2688]{1,0:T(8,128)S(1)} %copy-done, bf16[192,256]{1,0:T(8,128)(2,1)S(1)} %get-tuple-element.33.take, bf16[384,64]{1,0:T(8,128)(2,1)S(1)} %get-tuple-element.34.take_rest, f32[72,2048]{1,0:T(8,128)S(1)} %get-tuple-element.46.rest_0_, ...), custom_call_target="tpu_custom_call" | custom-call | bytes 11534336 | tf_op jit(solution)/shard_map/first_moment/pallas_call | solution.py:50
  147.9 4.4 %all-to-all-done.1 = f32[16,2,288,128]{3,2,1,0:T(8,128)} async-done(((f32[16,2,288,128]{3,2,1,0:T(8,128)}), f32[16,2,288,128]{3,2,1,0:T(8,128)}, u32[]{:S(2)}, u32[]{:S(2)}) %all-to-all-start.1) | async-done | bytes 4718624 | tf_op jit(solution)/shard_map/all_to_all | solution.py:579
  152.3 7.1 %weight_update.1 = (f32[192,2688]{1,0:T(8,128)}, f32[192,2688]{1,0:T(8,128)}, f32[192,2688]{1,0:T(8,128)}) custom-call(s32[1,21]{1,0:T(1,128)S(1)} %get-tuple-element.31.take, f32[2]{0:T(128)S(1)} %pad_maximum_fusion.fixes, f32[32,288,128]{2,1,0:T(8,128)} %bitcast.5.recv, f32[192,2688]{1,0:T(8,128)} %get-tuple-element.28.first, ...), custom_call_target="tpu_custom_call" | custom-call | bytes 16777216 | tf_op jit(solution)/shard_map/weight_update/pallas_call | solution.py:50
  (19 shorter events, 0.1 us)
Async XLA Ops:
  0.6 0.7 copy-start.1
  5.7 7.4 %copy-start.2 = (s32[8,192]{1,0:T(8,128)S(1)}, s32[8,192]{1,0:T(8,128)}, u32[]{:S(2)}) copy-start(s32[8,192]{1,0:T(8,128)} %old.1) | copy-start | bytes 18436
  5.7 7.4 %copy-start.3 = (s32[8,192]{1,0:T(8,128)S(1)}, s32[8,192]{1,0:T(8,128)}, u32[]{:S(2)}) copy-start(s32[8,192]{1,0:T(8,128)} %new.1) | copy-start | bytes 18436
  5.8 71.6 %all-to-all-start = ((f32[16,2,288,128]{3,2,1,0:T(8,128)}), f32[16,2,288,128]{3,2,1,0:T(8,128)}, u32[]{:S(2)}, u32[]{:S(2)}) async-start(f32[16,2,288,128]{3,2,1,0:T(8,128)} %bitcast.7), calls=%async_computation | async-start | bytes 9437184 | tf_op jit(solution)/shard_map/all_to_all | solution.py:579
  18.9 30.9 %collective-permute-start.5 = (f32[144,2048]{1,0:T(8,128)S(1)}, f32[144,2048]{1,0:T(8,128)S(1)}, u32[]{:S(2)}, u32[]{:S(2)}) collective-permute-start(f32[144,2048]{1,0:T(8,128)S(1)} %get-tuple-element.43), channel_id=1, source_target_pairs={{0,64},{16,80},{32,96},{48,112},{64,0},{80,16},{96,32},{112,48},{1... | collective-permute-start | bytes 3538952 | tf_op jit(solution)/shard_map/ppermute | solution.py:569
  22.9 39.1 %collective-permute-start = (f32[72,2048]{1,0:T(8,128)S(1)}, f32[72,2048]{1,0:T(8,128)S(1)}, u32[]{:S(2)}, u32[]{:S(2)}) collective-permute-start(f32[72,2048]{1,0:T(8,128)S(1)} %get-tuple-element.38), channel_id=1, source_target_pairs={{0,32},{16,48},{32,64},{48,80},{64,96},{80,112},{96,0},{112,16},{1... | collective-permute-start | bytes 1769480 | tf_op jit(solution)/shard_map/ppermute | solution.py:569
  23.9 39.6 %collective-permute-start.1 = (f32[72,2048]{1,0:T(8,128)S(1)}, f32[72,2048]{1,0:T(8,128)S(1)}, u32[]{:S(2)}, u32[]{:S(2)}) collective-permute-start(f32[72,2048]{1,0:T(8,128)S(1)} %get-tuple-element.39), channel_id=1, source_target_pairs={{0,96},{16,112},{32,0},{48,16},{64,32},{80,48},{96,64},{112,80},{1... | collective-permute-start | bytes 1769480 | tf_op jit(solution)/shard_map/ppermute | solution.py:569
  26.1 47.4 %collective-permute-start.2 = (f32[72,2048]{1,0:T(8,128)S(1)}, f32[72,2048]{1,0:T(8,128)S(1)}, u32[]{:S(2)}, u32[]{:S(2)}) collective-permute-start(f32[72,2048]{1,0:T(8,128)S(1)} %get-tuple-element.40), channel_id=1, source_target_pairs={{0,48},{16,32},{32,80},{48,64},{64,112},{80,96},{96,16},{112,0},{1... | collective-permute-start | bytes 1769480 | tf_op jit(solution)/shard_map/ppermute | solution.py:569
  26.1 47.4 %collective-permute-start.3 = (f32[72,2048]{1,0:T(8,128)S(1)}, f32[72,2048]{1,0:T(8,128)S(1)}, u32[]{:S(2)}, u32[]{:S(2)}) collective-permute-start(f32[72,2048]{1,0:T(8,128)S(1)} %get-tuple-element.41), channel_id=1, source_target_pairs={{0,112},{16,96},{32,16},{48,0},{64,48},{80,32},{96,80},{112,64},{1... | collective-permute-start | bytes 1769480 | tf_op jit(solution)/shard_map/ppermute | solution.py:569
  49.8 23.7 %collective-permute-start.4 = (f32[72,2048]{1,0:T(8,128)S(1)}, f32[72,2048]{1,0:T(8,128)S(1)}, u32[]{:S(2)}, u32[]{:S(2)}) collective-permute-start(f32[72,2048]{1,0:T(8,128)S(1)} %get-tuple-element.42), channel_id=1, source_target_pairs={{0,16},{16,0},{32,48},{48,32},{64,80},{80,64},{96,112},{112,96},{1... | collective-permute-start | bytes 1769480 | tf_op jit(solution)/shard_map/ppermute | solution.py:569
  61.9 11.5 %collective-permute-start.6 = (f32[72,2048]{1,0:T(8,128)S(1)}, f32[72,2048]{1,0:T(8,128)S(1)}, u32[]{:S(2)}, u32[]{:S(2)}) collective-permute-start(f32[72,2048]{1,0:T(8,128)S(1)} %slice.8), channel_id=1, source_target_pairs={{0,16},{16,0},{32,48},{48,32},{64,80},{80,64},{96,112},{112,96},{1... | collective-permute-start | bytes 1769480 | tf_op jit(solution)/shard_map/ppermute | solution.py:569
  77.3 74.9 %all-to-all-start.1 = ((f32[16,2,288,128]{3,2,1,0:T(8,128)}), f32[16,2,288,128]{3,2,1,0:T(8,128)}, u32[]{:S(2)}, u32[]{:S(2)}) async-start(f32[16,2,288,128]{3,2,1,0:T(8,128)} %bitcast.6), calls=%async_computation.1 | async-start | bytes 9437184 | tf_op jit(solution)/shard_map/all_to_all | solution.py:579
  84.6 59.9 %copy-start = (f32[192,2688]{1,0:T(8,128)S(1)}, f32[192,2688]{1,0:T(8,128)}, u32[]{:S(2)}) copy-start(f32[192,2688]{1,0:T(8,128)} %gradient.3) | copy-start | bytes 6193156
  89.3 30.4 %collective-permute-start.12 = (f32[144,2048]{1,0:T(8,128)S(1)}, f32[144,2048]{1,0:T(8,128)S(1)}, u32[]{:S(2)}, u32[]{:S(2)}) collective-permute-start(f32[144,2048]{1,0:T(8,128)S(1)} %get-tuple-element.52), channel_id=1, source_target_pairs={{0,64},{16,80},{32,96},{48,112},{64,0},{80,16},{96,32},{112,48},{1... | collective-permute-start | bytes 3538952 | tf_op jit(solution)/shard_map/ppermute | solution.py:569
  92.2 38.5 %collective-permute-start.10 = (f32[72,2048]{1,0:T(8,128)S(1)}, f32[72,2048]{1,0:T(8,128)S(1)}, u32[]{:S(2)}, u32[]{:S(2)}) collective-permute-start(f32[72,2048]{1,0:T(8,128)S(1)} %get-tuple-element.50), channel_id=1, source_target_pairs={{0,112},{16,96},{32,16},{48,0},{64,48},{80,32},{96,80},{112,64},{1... | collective-permute-start | bytes 1769480 | tf_op jit(solution)/shard_map/ppermute | solution.py:569
  92.7 41.7 %collective-permute-start.11 = (f32[72,2048]{1,0:T(8,128)S(1)}, f32[72,2048]{1,0:T(8,128)S(1)}, u32[]{:S(2)}, u32[]{:S(2)}) collective-permute-start(f32[72,2048]{1,0:T(8,128)S(1)} %get-tuple-element.51), channel_id=1, source_target_pairs={{0,16},{16,0},{32,48},{48,32},{64,80},{80,64},{96,112},{112,96},{1... | collective-permute-start | bytes 1769480 | tf_op jit(solution)/shard_map/ppermute | solution.py:569
  93.5 40.8 %collective-permute-start.7 = (f32[72,2048]{1,0:T(8,128)S(1)}, f32[72,2048]{1,0:T(8,128)S(1)}, u32[]{:S(2)}, u32[]{:S(2)}) collective-permute-start(f32[72,2048]{1,0:T(8,128)S(1)} %get-tuple-element.47), channel_id=1, source_target_pairs={{0,32},{16,48},{32,64},{48,80},{64,96},{80,112},{96,0},{112,16},{1... | collective-permute-start | bytes 1769480 | tf_op jit(solution)/shard_map/ppermute | solution.py:569
  94.3 50.1 %collective-permute-start.8 = (f32[72,2048]{1,0:T(8,128)S(1)}, f32[72,2048]{1,0:T(8,128)S(1)}, u32[]{:S(2)}, u32[]{:S(2)}) collective-permute-start(f32[72,2048]{1,0:T(8,128)S(1)} %get-tuple-element.48), channel_id=1, source_target_pairs={{0,96},{16,112},{32,0},{48,16},{64,32},{80,48},{96,64},{112,80},{1... | collective-permute-start | bytes 1769480 | tf_op jit(solution)/shard_map/ppermute | solution.py:569
  119.8 24.6 %collective-permute-start.9 = (f32[72,2048]{1,0:T(8,128)S(1)}, f32[72,2048]{1,0:T(8,128)S(1)}, u32[]{:S(2)}, u32[]{:S(2)}) collective-permute-start(f32[72,2048]{1,0:T(8,128)S(1)} %get-tuple-element.49), channel_id=1, source_target_pairs={{0,48},{16,32},{32,80},{48,64},{64,112},{80,96},{96,16},{112,0},{1... | collective-permute-start | bytes 1769480 | tf_op jit(solution)/shard_map/ppermute | solution.py:569
  130.7 13.7 %collective-permute-start.13 = (f32[72,2048]{1,0:T(8,128)S(1)}, f32[72,2048]{1,0:T(8,128)S(1)}, u32[]{:S(2)}, u32[]{:S(2)}) collective-permute-start(f32[72,2048]{1,0:T(8,128)S(1)} %slice.9), channel_id=1, source_target_pairs={{0,16},{16,0},{32,48},{48,32},{64,80},{80,64},{96,112},{112,96},{1... | collective-permute-start | bytes 1769480 | tf_op jit(solution)/shard_map/ppermute | solution.py:569
